TPU v7x, 512 devices: a whole 4x8x8 slice. The times are simulated.
512 devices in a mesh: seq: 64 (over y, z_lo, core), head: 8 (over x, z_hi).
Axes of the slice: x: 4, y: 8, z: 8 (z_hi: 2, z_lo: 4; z = z_hi * 4 + z_lo), core: 2. Of those that a mesh axis runs over, the one named last changes fastest.
Arguments:
- query_pre: bfloat16 [16384, 5120], P('seq', 'head'), may hold values from -250 to 250
- key_pre: bfloat16 [16384, 5120], P('seq', 'head'), may hold values from -250 to 250
- value: bfloat16 [16384, 5120], P('seq', 'head'), may hold values from -6 to 6
- d_out: bfloat16 [16384, 5120], P('seq', 'head'), may hold values from -96 to 96
- gain_q: bfloat16 [5120], P('head'), may hold values from 0.25 to 1.75
- gain_k: bfloat16 [5120], P('head'), may hold values from 0.25 to 1.75
- head_class: int32 [40], P('head'), may hold values from 0 to 1, as said below
- head_band: int32 [40], P('head'), may hold values from 0 to 1, as said below
Outputs:
- d_query: bfloat16 [16384, 5120], P('seq', 'head')
- d_key: bfloat16 [16384, 5120], P('seq', 'head')
- d_value: bfloat16 [16384, 5120], P('seq', 'head')
Inputs may be any that keep to these rules, and one draw needn't show every extreme that they name: `head_class`: each group of 5 consecutive heads holds exactly 3 spatial heads (0) and 2 temporal heads (1). `head_band`: temporal heads hold 0; each group of 5 consecutive heads has a spatial head with 0 and one with 1.
All inputs are finite; a program needn't handle non-finite values.
Results may differ from a plain program's by a relative error of at most 0.0095.
The roundings to bfloat16 on the way count: a program that leaves them out, or rounds other values in their place, can miss the bound.
Values may be sent and summed in bfloat16 or wider, within the bound.
No kernel may reach another device: no remote copies, remote signals or barrier semaphores. Data moves between devices by JAX's collectives and lax.ppermute only.
A program may use at most 64 MiB of HBM per device.

v0:
```python
import math

import jax
import jax.numpy as jnp
from jax import lax
from jax.sharding import PartitionSpec as P

HD = 128
SPAT_DEV = 3
FR_DEV = 1
TILE = 4


EPSILON = 1e-06


def extended(block, sides, width):
    for axis, dim in sides:
        count = lax.axis_size(axis)
        forward = [(i, i + 1) for i in range(count - 1)]
        backward = [(target, source) for source, target in forward]
        low = lax.ppermute(
            lax.slice_in_dim(block, block.shape[dim] - width, None, axis=dim), axis, forward
        )
        high = lax.ppermute(lax.slice_in_dim(block, 0, width, axis=dim), axis, backward)
        block = jnp.concatenate([low, block, high], axis=dim)
    return block


def passed_along(block, axis, distance):
    devices = range(lax.axis_size(axis))
    route = [(i - distance, i) for i in devices if i - distance in devices]
    return lax.ppermute(block, axis, route)


def attend_rows(q_rows, g_rows, k_win, v_win, allowed):
    scaling = 1.0 / math.sqrt(HD)
    scores = jnp.einsum("qd,kd->qk", q_rows, k_win, preferred_element_type=jnp.float32) * scaling
    scores = jnp.where(allowed, scores, -1e30)
    largest = jnp.max(scores, axis=-1, keepdims=True)
    powers = jnp.where(allowed, jnp.exp(scores - largest), 0.0)
    totals = jnp.sum(powers, axis=-1, keepdims=True)
    attention = powers / totals
    d_attention = jnp.einsum("qd,kd->qk", g_rows, v_win, preferred_element_type=jnp.float32)
    deltas = jnp.sum(attention * d_attention, axis=-1, keepdims=True)
    d_scores = (attention * (d_attention - deltas)).astype(jnp.bfloat16)
    return (attention.astype(jnp.bfloat16), d_scores, largest + jnp.log(totals), deltas)


def temporal_grads(stacked):
    q_rows = stacked[:, :, :, 0]
    k_rows = stacked[:, :, :, 1]
    v_rows = stacked[:, :, :, 2]
    g_rows = stacked[:, :, :, 3]
    frames_all, positions, item_count, head_size = q_rows.shape
    tile_count = positions // TILE
    scaling = 1.0 / math.sqrt(HD)

    def to_tiles(values):
        return (
            values.reshape(frames_all, tile_count, TILE, item_count, head_size)
            .transpose(3, 1, 0, 2, 4)
            .reshape(item_count, tile_count, frames_all * TILE, head_size)
        )

    def from_tiles(values):
        return (
            values.reshape(item_count, tile_count, frames_all, TILE, head_size)
            .transpose(2, 1, 3, 0, 4)
            .reshape(frames_all, positions, item_count, head_size)
            .astype(jnp.bfloat16)
        )

    q_tiles = to_tiles(q_rows)
    k_tiles = to_tiles(k_rows)
    v_tiles = to_tiles(v_rows)
    g_tiles = to_tiles(g_rows)
    scores = (
        jnp.einsum("hnqd,hnkd->hnqk", q_tiles, k_tiles, preferred_element_type=jnp.float32)
        * scaling
    )
    largest = jnp.max(scores, axis=-1, keepdims=True)
    powers = jnp.exp(scores - largest)
    attention = powers / jnp.sum(powers, axis=-1, keepdims=True)
    d_attention = jnp.einsum(
        "hnqd,hnkd->hnqk", g_tiles, v_tiles, preferred_element_type=jnp.float32
    )
    deltas = jnp.sum(attention * d_attention, axis=-1, keepdims=True)
    d_scores = (attention * (d_attention - deltas)).astype(jnp.bfloat16)
    attention_b = attention.astype(jnp.bfloat16)
    d_q = (
        jnp.einsum("hnqk,hnkd->hnqd", d_scores, k_tiles, preferred_element_type=jnp.float32)
        * scaling
    )
    d_k = (
        jnp.einsum("hnqk,hnqd->hnkd", d_scores, q_tiles, preferred_element_type=jnp.float32)
        * scaling
    )
    d_v = jnp.einsum("hnqk,hnqd->hnkd", attention_b, g_tiles, preferred_element_type=jnp.float32)
    return jnp.stack((from_tiles(d_q), from_tiles(d_k), from_tiles(d_v)), axis=3)


def per_device(query_pre, key_pre, value, d_out, gain_q, gain_k, head_class, head_band):
    row_count, width = query_pre.shape
    head_count = width // HD
    frame_count = FR_DEV
    frame_tokens = row_count // frame_count
    all_frames = frame_count * lax.axis_size("seq")
    full_width = width * lax.axis_size("head")
    scaling = 1.0 / math.sqrt(HD)
    spatial = SPAT_DEV
    q_wide = query_pre.astype(jnp.float32)
    k_wide = key_pre.astype(jnp.float32)
    squares = lax.psum((jnp.sum(q_wide * q_wide, axis=1), jnp.sum(k_wide * k_wide, axis=1)), "head")
    q_inverse = lax.rsqrt(squares[0] / full_width + EPSILON)[:, None]
    k_inverse = lax.rsqrt(squares[1] / full_width + EPSILON)[:, None]
    q_gain = gain_q.astype(jnp.float32)
    k_gain = gain_k.astype(jnp.float32)
    q_norm = (q_wide * q_inverse * q_gain).astype(jnp.bfloat16)
    k_norm = (k_wide * k_inverse * k_gain).astype(jnp.bfloat16)
    ordering = jnp.argsort(head_class, stable=True)
    placing = jnp.arange(head_count)[:, None] == ordering[None, :]
    placing_b = placing.astype(jnp.bfloat16)
    slot_bands = jnp.sum(head_band[:, None] * placing.astype(jnp.int32), axis=0)

    def to_slots(values):
        picked = jnp.einsum(
            "thd,hs->tsd",
            values.reshape(row_count, head_count, HD),
            placing_b,
            preferred_element_type=jnp.float32,
        )
        return picked.astype(jnp.bfloat16).reshape(frame_count, frame_tokens, head_count, HD)

    q_slots = to_slots(q_norm)
    k_slots = to_slots(k_norm)
    v_slots = to_slots(value)
    g_slots = to_slots(d_out)
    padded = extended(
        jnp.stack((k_slots[:, :, :spatial], v_slots[:, :, :spatial]), axis=2), (("seq", 0),), 1
    )
    first_frame = lax.axis_index("seq") * frame_count
    offsets = jnp.arange(3 * frame_tokens, dtype=jnp.int32) // frame_tokens - 1
    grad_parts = jnp.zeros((frame_count + 2, frame_tokens, 2, spatial, HD), jnp.float32)
    d_q_heads = []
    for slot_idx in range(spatial):
        k_win = padded[0:3, :, 0, slot_idx].reshape(3 * frame_tokens, HD)
        v_win = padded[0:3, :, 1, slot_idx].reshape(3 * frame_tokens, HD)
        k_win, v_win = (k_win, v_win)
        q_rows = q_slots[0, :, slot_idx]
        g_rows = g_slots[0, :, slot_idx]
        target = first_frame + 0 + offsets
        allowed = (
            (jnp.abs(offsets) <= slot_bands[slot_idx]) & (target >= 0) & (target < all_frames)
        )[None, :]
        attention_b, d_scores, log_totals, deltas = attend_rows(
            q_rows, g_rows, k_win, v_win, allowed
        )
        d_q_heads.append(jnp.dot(d_scores, k_win, preferred_element_type=jnp.float32) * scaling)
        d_k_win = (
            jnp.einsum("qk,qd->kd", d_scores, q_rows, preferred_element_type=jnp.float32) * scaling
        )
        d_v_win = jnp.einsum("qk,qd->kd", attention_b, g_rows, preferred_element_type=jnp.float32)
        grad_parts = grad_parts.at[0:3, :, 0, slot_idx].add(d_k_win.reshape(3, frame_tokens, HD))
        grad_parts = grad_parts.at[0:3, :, 1, slot_idx].add(d_v_win.reshape(3, frame_tokens, HD))
    d_q_frames = [jnp.stack(d_q_heads, axis=1)]
    own_grads = grad_parts[1 : frame_count + 1]
    for shift_by, source, target_frame in ((-1, 0, frame_count - 1), (1, frame_count + 1, 0)):
        arrived = passed_along(grad_parts[source].astype(jnp.bfloat16), "seq", shift_by).astype(
            jnp.float32
        )
        own_grads = own_grads.at[target_frame, :, :, :spatial].add(arrived)
    d_q_spatial = jnp.stack(d_q_frames).astype(jnp.bfloat16)
    d_k_spatial = own_grads[:, :, 0].astype(jnp.bfloat16)
    d_v_spatial = own_grads[:, :, 1].astype(jnp.bfloat16)
    temporal_in = jnp.stack(
        (
            q_slots[:, :, spatial:],
            k_slots[:, :, spatial:],
            v_slots[:, :, spatial:],
            g_slots[:, :, spatial:],
        ),
        axis=3,
    )
    temporal_out = temporal_grads(
        lax.all_to_all(temporal_in, "seq", split_axis=1, concat_axis=0, tiled=True)
    )
    returned = lax.all_to_all(temporal_out, "seq", split_axis=0, concat_axis=1, tiled=True)
    d_q_temporal = returned[:, :, :, 0]
    d_k_temporal = returned[:, :, :, 1]
    d_v_temporal = returned[:, :, :, 2]

    def from_slots(spatial_part, temporal_part):
        joined = jnp.concatenate((spatial_part, temporal_part), axis=2).reshape(
            row_count, head_count, HD
        )
        return jnp.einsum(
            "tsd,hs->thd", joined, placing_b, preferred_element_type=jnp.float32
        ).reshape(row_count, width)

    d_q_norm = from_slots(d_q_spatial, d_q_temporal)
    d_k_norm = from_slots(d_k_spatial, d_k_temporal)
    d_value = from_slots(d_v_spatial, d_v_temporal).astype(jnp.bfloat16)
    inner_sums = lax.psum(
        (jnp.sum(q_gain * d_q_norm * q_wide, axis=1), jnp.sum(k_gain * d_k_norm * k_wide, axis=1)),
        "head",
    )
    q_cubed = q_inverse * q_inverse * q_inverse
    k_cubed = k_inverse * k_inverse * k_inverse
    d_query = (
        q_inverse * q_gain * d_q_norm - q_wide * q_cubed * inner_sums[0][:, None] / full_width
    ).astype(jnp.bfloat16)
    d_key = (
        k_inverse * k_gain * d_k_norm - k_wide * k_cubed * inner_sums[1][:, None] / full_width
    ).astype(jnp.bfloat16)
    return (d_query, d_key, d_value)


def solution(mesh):
    in_specs = (
        P("seq", "head"),
        P("seq", "head"),
        P("seq", "head"),
        P("seq", "head"),
        P("head"),
        P("head"),
        P("head"),
        P("head"),
    )
    out_specs = (P("seq", "head"), P("seq", "head"), P("seq", "head"))
    return jax.shard_map(
        per_device, mesh=mesh, in_specs=in_specs, out_specs=out_specs, check_vma=False
    )
```

profile of v0, /device:TPU:8, one launch (start us, length us, event | category | flops | bytes accessed | tf_op | source)
XLA Modules:
  0.0 175.2 jit_solution(15644336102248416996)
XLA Ops:
  3.9 35.1 %all-reduce.2 = (f32[256]{0:T(256)S(1)}, f32[256]{0:T(256)S(1)}) all-reduce(f32[256]{0:T(256)S(1)} %fusion.35, f32[256]{0:T(256)S(1)} %fusion.27), channel_id=1, replica_groups=mesh['seq'=64,'head'=8] {'head'}, use_global_device_ids=true, to_apply=%region_5.6 | all-reduce | flops 512 | bytes 4096 | tf_op jit(solution)/shard_map/psum | solution.py:114
  43.7 1.9 %collective-permute-start.1 = (bf16[1,256,2,3,128]{4,3,1,2,0:T(4,128)(2,1)}, bf16[1,256,2,3,128]{4,3,1,2,0:T(4,128)(2,1)}, u32[]{:S(2)}, u32[]{:S(2)}) collective-permute-start(bf16[1,256,2,3,128]{4,3,1,2,0:T(4,128)(2,1)} %pad_maximum_fusion.1), channel_id=1, source_target_pairs={{8,0},{16,8},{24,16},{32,24},{40,32},{48,40},{56,48},{64,56},{72,6... | collective-permute-start | bytes 1179656 | tf_op jit(solution)/shard_map/ppermute | solution.py:25
  45.6 2.4 %collective-permute-start = (bf16[1,256,2,3,128]{4,3,1,2,0:T(4,128)(2,1)}, bf16[1,256,2,3,128]{4,3,1,2,0:T(4,128)(2,1)}, u32[]{:S(2)}, u32[]{:S(2)}) collective-permute-start(bf16[1,256,2,3,128]{4,3,1,2,0:T(4,128)(2,1)} %pad_maximum_fusion.1), channel_id=1, source_target_pairs={{0,8},{8,16},{16,24},{24,32},{32,40},{40,48},{48,56},{56,64},{64,7... | collective-permute-start | bytes 1179656 | tf_op jit(solution)/shard_map/ppermute | solution.py:22
  52.5 11.0 %all-to-all-start = ((bf16[1,256,2,4,128]{4,2,3,0,1:T(2,128)(2,1)}), bf16[1,256,2,4,128]{4,2,3,0,1:T(2,128)(2,1)}, u32[]{:S(2)}, u32[]{:S(2)}) async-start(bf16[1,256,2,4,128]{4,2,3,0,1:T(2,128)(2,1)} %copy.81), calls=%async_computation | async-start | bytes 1048576 | tf_op jit(solution)/shard_map/all_to_all | solution.py:186
  65.7 1.3 fusion.107
  68.8 2.6 %pad_maximum_fusion = bf16[3,256,2,3,128]{4,3,1,2,0:T(4,128)(2,1)S(1)} fusion(bf16[1,256,2,3,128]{4,3,1,2,0:T(4,128)(2,1)} %collective-permute-done.1, bf16[1,256,1,3,128]{4,3,1,2,0:T(4,128)(2,1)S(1)} %slice_bitcast_fusion.3, bf16[1,256,1,3,128]{4,3,1,2,0:T(4,128)(2,1)S(1)} %slice_bitcast_fusion.4, bf16[1,256,2,3,128]{4,3,1,2,0:T(4,128)(2,1)} %collective-permute-done), kind=kLoop, calls=%fused_computation.1 | loop fusion | flops 1769472 | bytes 2359296 | tf_op jit(solution)/shard_map/concatenate | solution.py:26
  71.4 2.3 %fusion.121 = (bf16[3,256,1,1,128]{4,3,1,2,0:T(2,128)(2,1)S(1)}, bf16[3,256,1,1,128]{4,3,1,2,0:T(2,128)(2,1)S(1)}, bf16[3,256,1,1,128]{4,3,1,2,0:T(2,128)(2,1)S(...) fusion(bf16[3,256,2,3,128]{4,3,1,2,0:T(4,128)(2,1)S(1)} %pad_ma, ...), kind=kLoop, calls=%fused_computation.202 | loop fusion | bytes 2359296 | tf_op jit(solution)/shard_map/slice | solution.py:147
  86.9 1.9 %copy.96 = bf16[768,256]{1,0:T(8,128)(2,1)} copy(bf16[768,256]{0,1:T(8,128)(2,1)} %get-tuple-element.121) | data formatting | bytes 786432 | tf_op jit(solution)/shard_map/convert_element_type | solution.py:47
  88.8 1.6 copy.92
  90.4 1.9 %copy.97 = bf16[768,256]{1,0:T(8,128)(2,1)} copy(bf16[768,256]{0,1:T(8,128)(2,1)} %get-tuple-element.119) | data formatting | bytes 786432 | tf_op jit(solution)/shard_map/convert_element_type | solution.py:47
  92.3 1.3 fusion.13
  93.7 3.0 %fusion.57 = f32[3,256,2,3,128]{4,1,0,3,2:T(8,128)S(1)} fusion(f32[3,256,2,3,128]{4,1,0,3,2:T(8,128)S(1)} %fusion.13, s32[]{:T(128)} %bitcast.74, s32[]{:T(128)} %bitcast.75, f32[3,256,1,1,128]{4,1,0,3,2:T(8,128)} %bitcast.274, pred[]{:T(512)} %and_reduce_fusion), kind=kLoop, calls=%fused_computation.109 | loop fusion | flops 196608 | bytes 1179657 | tf_op jit(solution)/shard_map/scatter-add | solution.py:164
  98.2 4.9 %collective-permute-start.2 = (bf16[256,2,3,128]{3,0,2,1:T(8,128)(2,1)}, bf16[256,2,3,128]{3,0,2,1:T(8,128)(2,1)}, u32[]{:S(2)}, u32[]{:S(2)}) collective-permute-start(bf16[256,2,3,128]{3,0,2,1:T(8,128)(2,1)} %get-tuple-element.117), channel_id=1, source_target_pairs={{8,0},{16,8},{24,16},{32,24},{40,32},{48,40},{56,48},{64,56},{72,6... | collective-permute-start | bytes 1179656 | tf_op jit(solution)/shard_map/ppermute | solution.py:33
  103.1 1.9 %collective-permute-start.3 = (bf16[256,2,3,128]{3,0,2,1:T(8,128)(2,1)}, bf16[256,2,3,128]{3,0,2,1:T(8,128)(2,1)}, u32[]{:S(2)}, u32[]{:S(2)}) collective-permute-start(bf16[256,2,3,128]{3,0,2,1:T(8,128)(2,1)} %get-tuple-element.118), channel_id=1, source_target_pairs={{0,8},{8,16},{16,24},{24,32},{32,40},{40,48},{48,56},{56,64},{64,7... | collective-permute-start | bytes 1179656 | tf_op jit(solution)/shard_map/ppermute | solution.py:33
  105.1 1.5 fusion.124
  108.7 2.6 %fusion.128 = (f32[2,256]{1,0:T(2,128)}, f32[2,256,256]{1,2,0:T(8,128)}) fusion(bf16[2,256,128]{2,1,0:T(8,128)(2,1)} %bitcast.289, bf16[2,256,128]{2,1,0:T(8,128)(2,1)S(1)} %bitcast.286), kind=kOutput, calls=%fused_computation.209 | convolution fusion | flops 33947904 | bytes 788480 | tf_op jit(solution)/shard_map/sub | solution.py:83
  111.3 2.1 %convolution_convert_fusion.5 = bf16[2,256,128]{2,1,0:T(8,128)(2,1)} fusion(bf16[2,256,128]{2,1,0:T(8,128)(2,1)} %bitcast.302, f32[2,256]{1,0:T(2,128)} %get-tuple-element.151, bf16[2,256,128]{2,1,0:T(8,128)(2,1)} %bitcast.290, bf16[2,256,128]{2,1,0:T(8,128)(2,1)S(1)} %bitcast.287), kind=kOutput, calls=%fused_computation.38 | convolution fusion | flops 67699456 | bytes 526336 | tf_op jit(solution)/shard_map/hnqk,hnqd->hnkd/dot_general | solution.py:99
  113.4 1.5 multiply_reduce_fusion.3
  117.4 12.0 %all-to-all-start.1 = ((bf16[64,4,2,3,128]{4,1,2,3,0:T(4,128)(2,1)}), bf16[64,4,2,3,128]{4,1,2,3,0:T(4,128)(2,1)}, u32[]{:S(2)}, u32[]{:S(2)}) async-start(bf16[64,4,2,3,128]{4,1,2,3,0:T(4,128)(2,1)} %pad_maximum_fusion.3), calls=%async_computation.1 | async-start | bytes 786432 | tf_op jit(solution)/shard_map/all_to_all | solution.py:188
  130.6 1.3 fusion.23
  132.1 1.3 fusion.26
  133.4 10.6 %all-to-all-done.1 = bf16[64,4,2,3,128]{4,1,2,3,0:T(4,128)(2,1)} async-done(((bf16[64,4,2,3,128]{4,1,2,3,0:T(4,128)(2,1)}), bf16[64,4,2,3,128]{4,1,2,3,0:T(4,128)(2,1)}, u32[]{:S(2)}, u32[]{:S(2)}) %all-to-all-start.1) | async-done | bytes 393248 | tf_op jit(solution)/shard_map/all_to_all | solution.py:188
  143.9 1.4 copy.90
  149.2 23.9 %all-reduce.1 = (f32[256]{0:T(256)S(1)}, f32[256]{0:T(256)S(1)}) all-reduce(f32[256]{0:T(256)S(1)} %fusion.34, f32[256]{0:T(256)S(1)} %fusion.42), channel_id=1, replica_groups=mesh['seq'=64,'head'=8] {'head'}, use_global_device_ids=true, to_apply=%region_19.20 | all-reduce | flops 512 | bytes 4096 | tf_op jit(solution)/shard_map/psum | solution.py:204
  (158 shorter events, 42.4 us)
Async XLA Ops:
  0.6 39.5 %copy-start.24 = (s32[5]{0:T(128)S(1)}, s32[5]{0:T(128)}, u32[]{:S(2)}) copy-start(s32[5]{0:T(128)} %param.30) | copy-start | bytes 64
  2.5 39.1 %copy-start.12 = (bf16[256,640]{1,0:T(8,128)(2,1)S(1)}, bf16[256,640]{1,0:T(8,128)(2,1)}, u32[]{:S(2)}) copy-start(bf16[256,640]{1,0:T(8,128)(2,1)} %param.26) | copy-start | bytes 983044
  39.6 8.6 %copy-start.18 = (f32[256]{0:T(256)}, f32[256]{0:T(256)S(1)}, u32[]{:S(2)}) copy-start(f32[256]{0:T(256)S(1)} %get-tuple-element.167) | copy-start | bytes 3076
  41.4 6.8 %copy-start.22 = (bf16[640]{0:T(1024)(128)(2,1)S(1)}, bf16[640]{0:T(1024)(128)(2,1)}, u32[]{:S(2)}) copy-start(bf16[640]{0:T(1024)(128)(2,1)} %param.28) | copy-start | bytes 3844
  42.4 6.8 %copy-start.13 = (bf16[256,640]{1,0:T(8,128)(2,1)S(1)}, bf16[256,640]{1,0:T(8,128)(2,1)}, u32[]{:S(2)}) copy-start(bf16[256,640]{1,0:T(8,128)(2,1)} %param.27) | copy-start | bytes 983044
  43.7 25.1 %collective-permute-start.1 = (bf16[1,256,2,3,128]{4,3,1,2,0:T(4,128)(2,1)}, bf16[1,256,2,3,128]{4,3,1,2,0:T(4,128)(2,1)}, u32[]{:S(2)}, u32[]{:S(2)}) collective-permute-start(bf16[1,256,2,3,128]{4,3,1,2,0:T(4,128)(2,1)} %pad_maximum_fusion.1), channel_id=1, source_target_pairs={{8,0},{16,8},{24,16},{32,24},{40,32},{48,40},{56,48},{64,56},{72,6... | collective-permute-start | bytes 1179656 | tf_op jit(solution)/shard_map/ppermute | solution.py:25
  45.6 23.2 %collective-permute-start = (bf16[1,256,2,3,128]{4,3,1,2,0:T(4,128)(2,1)}, bf16[1,256,2,3,128]{4,3,1,2,0:T(4,128)(2,1)}, u32[]{:S(2)}, u32[]{:S(2)}) collective-permute-start(bf16[1,256,2,3,128]{4,3,1,2,0:T(4,128)(2,1)} %pad_maximum_fusion.1), channel_id=1, source_target_pairs={{0,8},{8,16},{16,24},{24,32},{32,40},{40,48},{48,56},{56,64},{64,7... | collective-permute-start | bytes 1179656 | tf_op jit(solution)/shard_map/ppermute | solution.py:22
  50.1 15.0 %copy-start.25 = (s32[5]{0:T(128)S(1)}, s32[5]{0:T(128)}, u32[]{:S(2)}) copy-start(s32[5]{0:T(128)} %param.31) | copy-start | bytes 64
  50.1 17.6 %copy-start.23 = (s32[5]{0:T(128)S(1)}, s32[5]{0:T(128)}, u32[]{:S(2)}) copy-start(s32[5]{0:T(128)} %constant.270.clone.1) | copy-start | bytes 64
  52.5 52.6 %all-to-all-start = ((bf16[1,256,2,4,128]{4,2,3,0,1:T(2,128)(2,1)}), bf16[1,256,2,4,128]{4,2,3,0,1:T(2,128)(2,1)}, u32[]{:S(2)}, u32[]{:S(2)}) async-start(bf16[1,256,2,4,128]{4,2,3,0,1:T(2,128)(2,1)} %copy.81), calls=%async_computation | async-start | bytes 1048576 | tf_op jit(solution)/shard_map/all_to_all | solution.py:186
  68.8 5.9 %copy-start.14 = (bf16[1,256,1,128]{3,2,1,0:T(2,128)(2,1)}, bf16[1,256,1,128]{3,2,1,0:T(2,128)(2,1)S(1)}, u32[]{:S(2)}) copy-start(bf16[1,256,1,128]{3,2,1,0:T(2,128)(2,1)S(1)} %get-tuple-element.130) | copy-start | bytes 196612
  68.8 12.2 %copy-start.15 = (bf16[1,256,1,128]{3,2,1,0:T(2,128)(2,1)}, bf16[1,256,1,128]{3,2,1,0:T(2,128)(2,1)S(1)}, u32[]{:S(2)}) copy-start(bf16[1,256,1,128]{3,2,1,0:T(2,128)(2,1)S(1)} %get-tuple-element.128) | copy-start | bytes 196612
  73.8 6.5 %copy-start.3 = (bf16[3,256,1,1,128]{4,1,3,2,0:T(8,128)(2,1)}, bf16[3,256,1,1,128]{4,1,3,2,0:T(8,128)(2,1)S(1)}, u32[]{:S(2)}) copy-start(bf16[3,256,1,1,128]{4,1,3,2,0:T(8,128)(2,1)S(1)} %copy.119) | copy-start | bytes 589828
  73.9 3.3 %copy-start.4 = (bf16[3,256,1,1,128]{4,1,3,2,0:T(8,128)(2,1)}, bf16[3,256,1,1,128]{4,1,3,2,0:T(8,128)(2,1)S(1)}, u32[]{:S(2)}) copy-start(bf16[3,256,1,1,128]{4,1,3,2,0:T(8,128)(2,1)S(1)} %copy.127) | copy-start | bytes 589828
  82.9 3.1 %copy-start.2 = (bf16[256,768]{1,0:T(8,128)(2,1)S(1)}, bf16[256,768]{1,0:T(8,128)(2,1)}, u32[]{:S(2)}) copy-start(bf16[256,768]{1,0:T(8,128)(2,1)} %copy-done.1) | copy-start | bytes 1179652
  82.9 3.1 %copy-start.6 = (bf16[3,256,1,1,128]{4,1,3,2,0:T(8,128)(2,1)S(1)}, bf16[3,256,1,1,128]{4,1,3,2,0:T(8,128)(2,1)}, u32[]{:S(2)}) copy-start(bf16[3,256,1,1,128]{4,1,3,2,0:T(8,128)(2,1)} %copy-done.5) | copy-start | bytes 589828
  92.3 4.4 %copy-start.7 = (bf16[768,256]{1,0:T(8,128)(2,1)S(1)}, bf16[768,256]{1,0:T(8,128)(2,1)}, u32[]{:S(2)}) copy-start(bf16[768,256]{1,0:T(8,128)(2,1)} %copy.97) | copy-start | bytes 1179652
  98.2 33.8 %collective-permute-start.2 = (bf16[256,2,3,128]{3,0,2,1:T(8,128)(2,1)}, bf16[256,2,3,128]{3,0,2,1:T(8,128)(2,1)}, u32[]{:S(2)}, u32[]{:S(2)}) collective-permute-start(bf16[256,2,3,128]{3,0,2,1:T(8,128)(2,1)} %get-tuple-element.117), channel_id=1, source_target_pairs={{8,0},{16,8},{24,16},{32,24},{40,32},{48,40},{56,48},{64,56},{72,6... | collective-permute-start | bytes 1179656 | tf_op jit(solution)/shard_map/ppermute | solution.py:33
  103.1 28.9 %collective-permute-start.3 = (bf16[256,2,3,128]{3,0,2,1:T(8,128)(2,1)}, bf16[256,2,3,128]{3,0,2,1:T(8,128)(2,1)}, u32[]{:S(2)}, u32[]{:S(2)}) collective-permute-start(bf16[256,2,3,128]{3,0,2,1:T(8,128)(2,1)} %get-tuple-element.118), channel_id=1, source_target_pairs={{0,8},{8,16},{16,24},{24,32},{32,40},{40,48},{48,56},{56,64},{64,7... | collective-permute-start | bytes 1179656 | tf_op jit(solution)/shard_map/ppermute | solution.py:33
  117.4 26.6 %all-to-all-start.1 = ((bf16[64,4,2,3,128]{4,1,2,3,0:T(4,128)(2,1)}), bf16[64,4,2,3,128]{4,1,2,3,0:T(4,128)(2,1)}, u32[]{:S(2)}, u32[]{:S(2)}) async-start(bf16[64,4,2,3,128]{4,1,2,3,0:T(4,128)(2,1)} %pad_maximum_fusion.3), calls=%async_computation.1 | async-start | bytes 786432 | tf_op jit(solution)/shard_map/all_to_all | solution.py:188
  132.0 13.7 %copy-start.16 = (bf16[1,256,1,128]{3,2,1,0:T(2,128)(2,1)S(1)}, bf16[1,256,1,128]{3,2,1,0:T(2,128)(2,1)}, u32[]{:S(2)}) copy-start(bf16[1,256,1,128]{3,2,1,0:T(2,128)(2,1)} %copy.92) | copy-start | bytes 196612
  148.4 24.7 %copy-start.19 = (f32[256]{0:T(256)S(1)}, f32[256]{0:T(256)}, u32[]{:S(2)}) copy-start(f32[256]{0:T(256)} %copy-done.18) | copy-start | bytes 3076
  148.4 24.7 %copy-start.21 = (f32[256]{0:T(256)S(1)}, f32[256]{0:T(256)}, u32[]{:S(2)}) copy-start(f32[256]{0:T(256)} %get-tuple-element.168) | copy-start | bytes 3076
  148.7 25.4 %copy-start.20 = (f32[256]{0:T(256)S(1)}, f32[256]{0:T(256)}, u32[]{:S(2)}) copy-start(f32[256]{0:T(256)} %get-tuple-element.140) | copy-start | bytes 3076
  (8 other events, 14.1 us)
where the time goes:
time: 176 us; the launch traced here: 175 us
  blocking collectives  59 us (34%)
  starting transfers between devices  34.1 us (19%)
  local copies, waits for them, and re-layouts  28 us (16%)
  other arithmetic  21.9 us (12%)
  matrix products  20.2 us (11%)
  waiting for transfers between devices  10.6 us (6%)
    psum x1, blocking collectives, per_device(): lax.psum((jnp.sum(q_wide * q_wide, axis=1), jnp.sum(k_wide * k_wide, axis...  35.1 us
    psum x1, blocking collectives, per_device(): lax.psum((jnp.sum(q_gain * d_q_norm * q_wide, axis=1), jnp.sum(k_gain * d...  23.9 us
    all_to_all x1, starting transfers between devices, per_device(): lax.all_to_all(temporal_out, 'seq', split_axis=0, concat_axis=1, tiled=True)  12 us
    all_to_all x1, starting transfers between devices, per_device(): lax.all_to_all(temporal_in, 'seq', split_axis=1, concat_axis=0, tiled=True)  11 us
    all_to_all x1, waiting for transfers between devices, per_device(): lax.all_to_all(temporal_out, 'seq', split_axis=0, concat_axis=1, tiled=True)  10.6 us
    unnamed x69, local copies, waits for them, and re-layouts  8.14 us
    ppermute x2, starting transfers between devices, passed_along(): return lax.ppermute(block, axis, route)  6.83 us
    convert_element_type x3, local copies, waits for them, and re-layouts, attend_rows(): attention.astype(jnp.bfloat16)  4.74 us
  transfers between devices with their start and end apart: 6, of which 1 were waited for; matrix products, arithmetic and copies ran while one was open for 31% of the time, Pallas kernels for 0%

commit v1 on v0

v1 whole, which is shorter than its diff:
```python
import functools
import math

import jax
import jax.numpy as jnp
from jax import lax
from jax.experimental import pallas as pl
from jax.experimental.pallas import tpu as pltpu
from jax.sharding import PartitionSpec as P

HD = 128
TOK = 256
HEADS_DEV = 5
FRAMES = 64
WIDTH = HEADS_DEV * HD
FULL = 5120
EPSILON = 1e-06
SCALE = 1.0 / math.sqrt(HD)
NEG = -1e30

BF = jnp.bfloat16
F32 = jnp.float32
VM = pl.BlockSpec(memory_space=pltpu.VMEM)
SM = pl.BlockSpec(memory_space=pltpu.SMEM)


def shape(dims, dtype):
    return jax.ShapeDtypeStruct(dims, dtype)


def call(body, outs, specs, name, micros, mib=24):
    return pl.pallas_call(
        body,
        out_shape=outs,
        in_specs=specs,
        out_specs=jax.tree.map(lambda _: VM, outs),
        name=name,
        compiler_params=pltpu.CompilerParams(vmem_limit_bytes=mib << 20),
        cost_estimate=pl.CostEstimate(
            flops=int(micros * 1e9), bytes_accessed=int(micros * 1e6), transcendentals=0
        ),
    )


def head_slots(cls_ref, band_ref):
    kinds = [cls_ref[i] for i in range(HEADS_DEV)]
    bands = [band_ref[i] for i in range(HEADS_DEV)]
    zero = jnp.int32(0)
    first = zero
    for i in reversed(range(HEADS_DEV)):
        first = jnp.where((kinds[i] == 0) & (bands[i] == 0), i, first)
    second, third, band_2, band_3, temp_0, temp_1 = zero, zero, zero, zero, zero, zero
    for i in reversed(range(HEADS_DEV)):
        other = (kinds[i] == 0) & (first != i)
        second = jnp.where(other, i, second)
        band_2 = jnp.where(other, bands[i], band_2)
        temp_0 = jnp.where(kinds[i] != 0, i, temp_0)
    for i in range(HEADS_DEV):
        other = (kinds[i] == 0) & (first != i)
        third = jnp.where(other, i, third)
        band_3 = jnp.where(other, bands[i], band_3)
        temp_1 = jnp.where(kinds[i] != 0, i, temp_1)
    return (first, second, third, temp_0, temp_1), (band_2, band_3)


def columns(slot):
    return pl.ds(pl.multiple_of(slot * HD, HD), HD)


def dot_nt(a, b, precision=None):
    return lax.dot_general(
        a, b, (((1,), (1,)), ((), ())), preferred_element_type=F32, precision=precision
    )


def dot_tn(a, b):
    return lax.dot_general(a, b, (((0,), (0,)), ((), ())), preferred_element_type=F32)


def dot_nn(a, b):
    return lax.dot_general(a, b, (((1,), (0,)), ((), ())), preferred_element_type=F32)


def rows_of(q_row, k_row):
    at = lax.broadcasted_iota(jnp.int32, (8, HD), 0)
    return jnp.where(
        at == 0,
        q_row[:, :HD],
        jnp.where(at == 1, q_row[:, HD:], jnp.where(at == 2, k_row[:, :HD], k_row[:, HD:])),
    )


def spread(rows, at):
    low = jnp.broadcast_to(rows[at : at + 1], (HD, HD)).T
    high = jnp.broadcast_to(rows[at + 1 : at + 2], (HD, HD)).T
    return jnp.concatenate([low, high], axis=0)


def lane_sums(values):
    return dot_nt(jnp.ones((8, HD), F32), values, lax.Precision.HIGHEST)


def inverses(sums_ref):
    return lax.rsqrt(jnp.sum(sums_ref[...], axis=0) / FULL + EPSILON)


def squares_body(q_ref, k_ref, out_ref):
    sums = []
    for ref in (q_ref, k_ref):
        total = jnp.zeros((TOK, HD), F32)
        for head in range(HEADS_DEV):
            wide = ref[:, head * HD : (head + 1) * HD].astype(F32)
            total += wide * wide
        sums.append(lane_sums(total))
    out_ref[...] = jnp.broadcast_to(rows_of(*sums)[None], (8, 8, HD))


def norm_body(
    cls_ref, band_ref, sums_ref, gain_ref, q_ref, k_ref, v_ref, g_ref, send_ref, halo_ref, qs_ref, ks_ref
):
    slots, _ = head_slots(cls_ref, band_ref)
    inv = inverses(sums_ref)
    q_inv, k_inv = spread(inv, 0), spread(inv, 2)

    def normed(ref, inverse, which, slot):
        gain = gain_ref[which, pl.ds(slot, 1), :]
        return (ref[:, columns(slot)].astype(F32) * inverse * gain).astype(BF)

    for s in range(2):
        slot = slots[3 + s]
        parts = (
            normed(q_ref, q_inv, 0, slot),
            normed(k_ref, k_inv, 1, slot),
            v_ref[:, columns(slot)],
            g_ref[:, columns(slot)],
        )
        for a, part in enumerate(parts):
            send_ref[s * 32 : (s + 1) * 32, a] = part.reshape(32, 8, HD)
    for s in range(3):
        slot = slots[s]
        qs_ref[s] = normed(q_ref, q_inv, 0, slot)
        k_norm = normed(k_ref, k_inv, 1, slot)
        if s == 0:
            ks_ref[...] = k_norm
        else:
            halo_ref[2 * s - 2] = k_norm
            halo_ref[2 * s - 1] = v_ref[:, columns(slot)]


def attend(q, g, keys, values, allowed):
    scores = []
    for key, ok in zip(keys, allowed):
        score = dot_nt(key, q) * SCALE
        scores.append(score if ok is None else jnp.where(ok, score, NEG))
    largest = functools.reduce(
        jnp.maximum, [jnp.max(score, axis=0, keepdims=True) for score in scores]
    )
    powers = [jnp.exp(score - largest) for score in scores]
    totals = sum(jnp.sum(power, axis=0, keepdims=True) for power in powers)
    inverse = 1.0 / totals
    probs = [power * inverse for power in powers]
    d_probs = [dot_nt(value, g) for value in values]
    deltas = sum(jnp.sum(p * d, axis=0, keepdims=True) for p, d in zip(probs, d_probs))
    d_scores = [(p * (d - deltas)).astype(BF) for p, d in zip(probs, d_probs)]
    d_q = sum(dot_tn(d, key) for d, key in zip(d_scores, keys)) * SCALE
    d_keys = [dot_nn(d, q) * SCALE for d in d_scores]
    d_values = [dot_nn(p.astype(BF), g) for p in probs]
    return d_q, d_keys, d_values


def spatial_body(
    cls_ref,
    band_ref,
    frame_ref,
    qs_ref,
    ks_ref,
    halo_ref,
    low_ref,
    high_ref,
    v_ref,
    g_ref,
    dq_ref,
    fin_ref,
    own_ref,
    to_low_ref,
    to_high_ref,
):
    slots, bands = head_slots(cls_ref, band_ref)
    frame = frame_ref[0]
    d_q, d_k, d_v = attend(
        qs_ref[0], g_ref[:, columns(slots[0])], [ks_ref[...]], [v_ref[:, columns(slots[0])]], [None]
    )
    dq_ref[0] = d_q.astype(BF)
    fin_ref[0] = d_k[0].astype(BF)
    fin_ref[1] = d_v[0].astype(BF)
    for s in (1, 2):
        at = 2 * s - 2
        wide = bands[s - 1] > 0
        g = g_ref[:, columns(slots[s])]
        keys = [low_ref[at], halo_ref[at], high_ref[at]]
        values = [low_ref[at + 1], halo_ref[at + 1], high_ref[at + 1]]
        allowed = [wide & (frame > 0), None, wide & (frame < FRAMES - 1)]
        d_q, d_k, d_v = attend(qs_ref[s], g, keys, values, allowed)
        dq_ref[s] = d_q.astype(BF)
        to_low_ref[at] = d_k[0].astype(BF)
        to_low_ref[at + 1] = d_v[0].astype(BF)
        own_ref[at] = d_k[1]
        own_ref[at + 1] = d_v[1]
        to_high_ref[at] = d_k[2].astype(BF)
        to_high_ref[at + 1] = d_v[2].astype(BF)


def temporal_body(in_ref, out_ref):
    rows = FRAMES * 8
    q, k, v, g = (in_ref[:, a].reshape(rows, HD) for a in range(4))
    d_k = jnp.zeros((rows, HD), F32)
    d_v = jnp.zeros((rows, HD), F32)
    step = 256
    for part in range(rows // step):
        q_part, g_part = q[part * step : (part + 1) * step], g[part * step : (part + 1) * step]
        key_tile = lax.broadcasted_iota(jnp.int32, (rows, step), 0) & 4
        query_tile = lax.broadcasted_iota(jnp.int32, (rows, step), 1) & 4
        d_q, d_keys, d_values = attend(q_part, g_part, [k], [v], [key_tile == query_tile])
        frames = step // 8
        out_ref[part * frames : (part + 1) * frames, 0] = d_q.astype(BF).reshape(frames, 8, HD)
        d_k += d_keys[0]
        d_v += d_values[0]
    out_ref[:, 1] = d_k.astype(BF).reshape(FRAMES, 8, HD)
    out_ref[:, 2] = d_v.astype(BF).reshape(FRAMES, 8, HD)


def product(gain_ref, which, slot, grad, ref):
    gain = gain_ref[which, pl.ds(slot, 1), :]
    return gain * grad.astype(F32) * ref[:, columns(slot)].astype(F32)


def spatial_sums_body(
    cls_ref, band_ref, gain_ref, q_ref, k_ref, dq_ref, fin_ref, own_ref, low_ref, high_ref, grad_ref, part_ref
):
    slots, _ = head_slots(cls_ref, band_ref)
    q_total = product(gain_ref, 0, slots[0], dq_ref[0], q_ref)
    k_total = product(gain_ref, 1, slots[0], fin_ref[0], k_ref)
    for s in (1, 2):
        for b in range(2):
            at = 2 * s - 2 + b
            grad_ref[at] = (
                own_ref[at] + low_ref[at].astype(F32) + high_ref[at].astype(F32)
            ).astype(BF)
        q_total += product(gain_ref, 0, slots[s], dq_ref[s], q_ref)
        k_total += product(gain_ref, 1, slots[s], grad_ref[2 * s - 2], k_ref)
    part_ref[0] = q_total
    part_ref[1] = k_total


def inner_body(cls_ref, band_ref, gain_ref, q_ref, k_ref, back_ref, part_ref, out_ref):
    slots, _ = head_slots(cls_ref, band_ref)
    sums = []
    for which, ref in enumerate((q_ref, k_ref)):
        total = part_ref[which]
        for s in range(2):
            grad = back_ref[s * 32 : (s + 1) * 32, which].reshape(TOK, HD)
            total += product(gain_ref, which, slots[3 + s], grad, ref)
        sums.append(lane_sums(total))
    out_ref[...] = jnp.broadcast_to(rows_of(*sums)[None], (8, 8, HD))


def final_body(
    cls_ref,
    band_ref,
    gain_ref,
    sums_ref,
    inner_ref,
    q_ref,
    k_ref,
    back_ref,
    dq_ref,
    fin_ref,
    grad_ref,
    out_q_ref,
    out_k_ref,
    out_v_ref,
):
    slots, _ = head_slots(cls_ref, band_ref)
    inv = inverses(sums_ref)
    pull = inv * inv * inv * jnp.sum(inner_ref[...], axis=0) / FULL
    for which, (ref, out) in enumerate(((q_ref, out_q_ref), (k_ref, out_k_ref))):
        inverse, pulled = spread(inv, 2 * which), spread(pull, 2 * which)
        for s in range(HEADS_DEV):
            if s >= 3:
                grad = back_ref[(s - 3) * 32 : (s - 2) * 32, which].reshape(TOK, HD)
            elif which == 0:
                grad = dq_ref[s]
            else:
                grad = fin_ref[0] if s == 0 else grad_ref[2 * s - 2]
            gain = gain_ref[which, pl.ds(slots[s], 1), :]
            at = columns(slots[s])
            out[:, at] = (
                inverse * gain * grad.astype(F32) - ref[:, at].astype(F32) * pulled
            ).astype(BF)
    out_v_ref[:, columns(slots[0])] = fin_ref[1]
    for s in (1, 2):
        out_v_ref[:, columns(slots[s])] = grad_ref[2 * s - 1]
    for s in range(2):
        out_v_ref[:, columns(slots[3 + s])] = back_ref[s * 32 : (s + 1) * 32, 2].reshape(TOK, HD)


def per_device(query_pre, key_pre, value, d_out, gain_q, gain_k, head_class, head_band):
    gains = jnp.stack([gain_q, gain_k]).astype(F32).reshape(2, HEADS_DEV, HD)
    frame = lax.axis_index("seq").astype(jnp.int32).reshape(1)
    up = [(i, i + 1) for i in range(FRAMES - 1)]
    down = [(i + 1, i) for i in range(FRAMES - 1)]
    block = (4, TOK, HD)

    sums = call(squares_body, shape((8, 8, HD), F32), [VM] * 2, "squares", 2)(query_pre, key_pre)
    sums = lax.all_to_all(sums, "head", 0, 0, tiled=True)
    send, halo, qs, ks = call(
        norm_body,
        (
            shape((FRAMES, 4, 8, HD), BF),
            shape(block, BF),
            shape((3, TOK, HD), BF),
            shape((TOK, HD), BF),
        ),
        [SM, SM] + [VM] * 6,
        "norm",
        3,
    )(head_class, head_band, sums, gains, query_pre, key_pre, value, d_out)
    held = lax.all_to_all(send, "seq", 0, 0, tiled=True)
    low = lax.ppermute(halo, "seq", up)
    high = lax.ppermute(halo, "seq", down)
    dq, fin, own, to_low, to_high = call(
        spatial_body,
        (
            shape((3, TOK, HD), BF),
            shape((2, TOK, HD), BF),
            shape(block, F32),
            shape(block, BF),
            shape(block, BF),
        ),
        [SM] * 3 + [VM] * 7,
        "spatial",
        6,
    )(head_class, head_band, frame, qs, ks, halo, low, high, value, d_out)
    from_low = lax.ppermute(to_high, "seq", up)
    from_high = lax.ppermute(to_low, "seq", down)
    grads = call(temporal_body, shape((FRAMES, 3, 8, HD), BF), [VM], "temporal", 3)(held)
    back = lax.all_to_all(grads, "seq", 0, 0, tiled=True)
    grad, part = call(
        spatial_sums_body,
        (shape(block, BF), shape((2, TOK, HD), F32)),
        [SM, SM] + [VM] * 8,
        "spatial_sums",
        3,
    )(head_class, head_band, gains, query_pre, key_pre, dq, fin, own, from_low, from_high)
    inner = call(
        inner_body, shape((8, 8, HD), F32), [SM, SM] + [VM] * 5, "inner", 2
    )(head_class, head_band, gains, query_pre, key_pre, back, part)
    inner = lax.all_to_all(inner, "head", 0, 0, tiled=True)
    return call(
        final_body,
        (shape((TOK, WIDTH), BF),) * 3,
        [SM, SM] + [VM] * 9,
        "final",
        3,
    )(head_class, head_band, gains, sums, inner, query_pre, key_pre, back, dq, fin, grad)


def solution(mesh):
    whole = P("seq", "head")
    return jax.shard_map(
        per_device,
        mesh=mesh,
        in_specs=(whole,) * 4 + (P("head"),) * 4,
        out_specs=(whole,) * 3,
        check_vma=False,
    )
```

time: 176 us -> 99.1 us (0.56)
  the two profiles are of different devices: /device:TPU:8 before, /device:TPU:9 now
where the time goes in v1:
time: 99.1 us; the launch traced here: 98.5 us
  starting transfers between devices  41.3 us (42%)
  waiting for transfers between devices  30.8 us (31%)
  Pallas kernels  11.6 us (12%)
  blocking collectives  11.4 us (12%)
  local copies, waits for them, and re-layouts  2.68 us (3%)
    all_to_all x1, waiting for transfers between devices, per_device(): held = lax.all_to_all(send, 'seq', 0, 0, tiled=True)  13 us
    all_to_all x1, starting transfers between devices, per_device(): sums = lax.all_to_all(sums, 'head', 0, 0, tiled=True)  12.6 us
    all_to_all x1, starting transfers between devices, per_device(): held = lax.all_to_all(send, 'seq', 0, 0, tiled=True)  12.6 us
    all_to_all x1, blocking collectives, per_device(): inner = lax.all_to_all(inner, 'head', 0, 0, tiled=True)  11.4 us
    all_to_all x1, waiting for transfers between devices, per_device(): sums = lax.all_to_all(sums, 'head', 0, 0, tiled=True)  8.33 us
    ppermute x1, waiting for transfers between devices, per_device(): from_high = lax.ppermute(to_low, 'seq', down)  6.2 us
    all_to_all x1, starting transfers between devices, per_device(): back = lax.all_to_all(grads, 'seq', 0, 0, tiled=True)  5.27 us
    ppermute x1, starting transfers between devices, per_device(): from_low = lax.ppermute(to_high, 'seq', up)  3.35 us
  transfers between devices with their start and end apart: 7, of which 4 were waited for; matrix products, arithmetic and copies ran while one was open for 0% of the time, Pallas kernels for 6%

profile of v1, /device:TPU:9, one launch (start us, length us, event | category | flops | bytes accessed | tf_op | source)
XLA Modules:
  0.0 98.5 jit_solution(5839800784799485410)
XLA Ops:
  0.7 1.0 %copy-done.2 = bf16[256,640]{1,0:T(8,128)(2,1)S(1)} copy-done((bf16[256,640]{1,0:T(8,128)(2,1)S(1)}, bf16[256,640]{1,0:T(8,128)(2,1)}, u32[]{:S(2)}) %copy-start.2) | copy-done | bytes 327704
  1.7 1.0 copy-done.4
  2.6 1.0 %squares.1 = f32[8,8,128]{2,1,0:T(8,128)} custom-call(bf16[256,640]{1,0:T(8,128)(2,1)S(1)} %copy-done.2, bf16[256,640]{1,0:T(8,128)(2,1)S(1)} %copy-done.4), custom_call_target="tpu_custom_call" | custom-call | flops 2000000000 | bytes 2000000 | tf_op jit(solution)/shard_map/squares/pallas_call | solution.py:314
  3.7 12.6 %all-to-all-start = ((f32[8,8,128]{2,1,0:T(8,128)}), f32[8,8,128]{2,1,0:T(8,128)S(1)}, u32[]{:S(2)}, u32[]{:S(2)}) async-start(f32[8,8,128]{2,1,0:T(8,128)} %squares.1), calls=%async_computation | async-start | bytes 65536 | tf_op jit(solution)/shard_map/all_to_all | solution.py:315
  16.3 0.7 copy-done.8
  17.0 8.3 %all-to-all-done.sums_ref = f32[8,8,128]{2,1,0:T(8,128)S(1)} async-done(((f32[8,8,128]{2,1,0:T(8,128)}), f32[8,8,128]{2,1,0:T(8,128)S(1)}, u32[]{:S(2)}, u32[]{:S(2)}) %all-to-all-start) | async-done | bytes 32800 | tf_op jit(solution)/shard_map/all_to_all | solution.py:315
  25.3 1.6 %norm.1 = (bf16[64,4,8,128]{3,2,1,0:T(8,128)(2,1)}, bf16[4,256,128]{2,1,0:T(8,128)(2,1)S(1)}, bf16[3,256,128]{2,1,0:T(8,128)(2,1)S(1)}, bf16[256,128]{1,0:T(8,128)(2,1)S(1)}) custom-call(s32[5]{0:T(128)S(1)} %copy-done.6, s32[5]{0:T(128)S(1)} %copy-done.7, f32[8,8,128]{2,1,0:T(8,128)S(1)} %all-to-all-done.sums_ref, ...), custom_call_target="tpu_custom_call" | custom-call | flops 3000000000 | bytes 3000000 | tf_op jit(solution)/shard_map/norm/pallas_call | solution.py:316
  27.0 12.6 %all-to-all-start.1 = ((bf16[64,4,8,128]{3,2,1,0:T(8,128)(2,1)}), bf16[64,4,8,128]{3,2,1,0:T(8,128)(2,1)S(1)}, u32[]{:S(2)}, u32[]{:S(2)}) async-start(bf16[64,4,8,128]{3,2,1,0:T(8,128)(2,1)} %get-tuple-element.14), calls=%async_computation.1 | async-start | bytes 1048576 | tf_op jit(solution)/shard_map/all_to_all | solution.py:328
  39.6 2.3 %collective-permute-start.1 = (bf16[4,256,128]{2,1,0:T(8,128)(2,1)S(1)}, bf16[4,256,128]{2,1,0:T(8,128)(2,1)S(1)}, u32[]{:S(2)}, u32[]{:S(2)}) collective-permute-start(bf16[4,256,128]{2,1,0:T(8,128)(2,1)S(1)} %get-tuple-element.17.halo_ref), channel_id=1, source_target_pairs={{8,0},{16,8},{24,16},{32,24},{40,32},{48,40},{56,48},{64,56},{72,6... | collective-permute-start | bytes 786440 | tf_op jit(solution)/shard_map/ppermute | solution.py:330
  41.9 3.3 %collective-permute-start = (bf16[4,256,128]{2,1,0:T(8,128)(2,1)S(1)}, bf16[4,256,128]{2,1,0:T(8,128)(2,1)S(1)}, u32[]{:S(2)}, u32[]{:S(2)}) collective-permute-start(bf16[4,256,128]{2,1,0:T(8,128)(2,1)S(1)} %get-tuple-element.17.halo_ref), channel_id=1, source_target_pairs={{0,8},{8,16},{16,24},{24,32},{32,40},{40,48},{48,56},{56,64},{64,7... | collective-permute-start | bytes 786440 | tf_op jit(solution)/shard_map/ppermute | solution.py:329
  45.2 13.0 %all-to-all-done.1.in_ref = bf16[64,4,8,128]{3,2,1,0:T(8,128)(2,1)S(1)} async-done(((bf16[64,4,8,128]{3,2,1,0:T(8,128)(2,1)}), bf16[64,4,8,128]{3,2,1,0:T(8,128)(2,1)S(1)}, u32[]{:S(2)}, u32[]{:S(2)}) %all-to-all-start.1) | async-done | bytes 524320 | tf_op jit(solution)/shard_map/all_to_all | solution.py:328
  58.1 2.5 %temporal.1 = bf16[64,3,8,128]{3,2,1,0:T(8,128)(2,1)} custom-call(bf16[64,4,8,128]{3,2,1,0:T(8,128)(2,1)S(1)} %all-to-all-done.1.in_ref), custom_call_target="tpu_custom_call" | custom-call | flops 3000000000 | bytes 3000000 | tf_op jit(solution)/shard_map/temporal/pallas_call | solution.py:346
  60.6 5.3 %all-to-all-start.2 = ((bf16[64,3,8,128]{3,2,1,0:T(8,128)(2,1)}), bf16[64,3,8,128]{3,2,1,0:T(8,128)(2,1)S(1)}, u32[]{:S(2)}, u32[]{:S(2)}) async-start(bf16[64,3,8,128]{3,2,1,0:T(8,128)(2,1)} %temporal.1), calls=%async_computation.2 | async-start | bytes 786432 | tf_op jit(solution)/shard_map/all_to_all | solution.py:347
  65.8 0.0 collective-permute-done.1.high_ref
  65.9 0.0 collective-permute-done.low_ref
  65.9 2.9 %spatial.1 = (bf16[3,256,128]{2,1,0:T(8,128)(2,1)S(1)}, bf16[2,256,128]{2,1,0:T(8,128)(2,1)S(1)}, f32[4,256,128]{2,1,0:T(8,128)S(1)}, bf16[4,256,128]{2,1,0:T(8,128)(2,1)S(1)}, bf16[4,256,128]{2,1,0:T(8,128)(2,1)S(1)}) custom-call(s32[5]{0:T(128)S(1)} %copy-done.6, s32[5]{0:T(128)S(1)} %copy-done.7, s32[1]{0:T(128)} %bitcast.2.frame_ref, ...), custom_call_target="tpu_custom_call" | custom-call | flops 6000000000 | bytes 6000000 | tf_op jit(solution)/shard_map/spatial/pallas_call | solution.py:331
  68.8 3.3 %collective-permute-start.2 = (bf16[4,256,128]{2,1,0:T(8,128)(2,1)S(1)}, bf16[4,256,128]{2,1,0:T(8,128)(2,1)S(1)}, u32[]{:S(2)}, u32[]{:S(2)}) collective-permute-start(bf16[4,256,128]{2,1,0:T(8,128)(2,1)S(1)} %get-tuple-element.21), channel_id=1, source_target_pairs={{0,8},{8,16},{16,24},{24,32},{32,40},{40,48},{48,56},{56,64},{64,7... | collective-permute-start | bytes 786440 | tf_op jit(solution)/shard_map/ppermute | solution.py:344
  72.1 1.9 %collective-permute-start.3 = (bf16[4,256,128]{2,1,0:T(8,128)(2,1)S(1)}, bf16[4,256,128]{2,1,0:T(8,128)(2,1)S(1)}, u32[]{:S(2)}, u32[]{:S(2)}) collective-permute-start(bf16[4,256,128]{2,1,0:T(8,128)(2,1)S(1)} %get-tuple-element.22), channel_id=1, source_target_pairs={{8,0},{16,8},{24,16},{32,24},{40,32},{48,40},{56,48},{64,56},{72,6... | collective-permute-start | bytes 786440 | tf_op jit(solution)/shard_map/ppermute | solution.py:345
  74.1 3.3 %collective-permute-done.2.low_ref = bf16[4,256,128]{2,1,0:T(8,128)(2,1)S(1)} collective-permute-done((bf16[4,256,128]{2,1,0:T(8,128)(2,1)S(1)}, bf16[4,256,128]{2,1,0:T(8,128)(2,1)S(1)}, u32[]{:S(2)}, u32[]{:S(2)}) %collective-permute-start.2) | collective-permute-done | bytes 262176 | tf_op jit(solution)/shard_map/ppermute | solution.py:344
  77.4 6.2 %collective-permute-done.3.high_ref = bf16[4,256,128]{2,1,0:T(8,128)(2,1)S(1)} collective-permute-done((bf16[4,256,128]{2,1,0:T(8,128)(2,1)S(1)}, bf16[4,256,128]{2,1,0:T(8,128)(2,1)S(1)}, u32[]{:S(2)}, u32[]{:S(2)}) %collective-permute-start.3) | collective-permute-done | bytes 262176 | tf_op jit(solution)/shard_map/ppermute | solution.py:345
  83.6 0.8 spatial_sums.1
  84.4 0.9 inner.1
  85.3 11.4 %all_to_all.20.inner_ref = f32[8,8,128]{2,1,0:T(8,128)S(1)} all-to-all(f32[8,8,128]{2,1,0:T(8,128)S(1)} %inner.1), channel_id=1, replica_groups=mesh['seq'=64,'head'=8] {'head'}, dimensions={0} | all-to-all | bytes 65536 | tf_op jit(solution)/shard_map/all_to_all | solution.py:358
  96.7 1.8 %final.1 = (bf16[256,640]{1,0:T(8,128)(2,1)}, bf16[256,640]{1,0:T(8,128)(2,1)}, bf16[256,640]{1,0:T(8,128)(2,1)}) custom-call(s32[5]{0:T(128)S(1)} %copy-done.6, s32[5]{0:T(128)S(1)} %copy-done.7, f32[2,5,128]{2,1,0:T(8,128)S(1)} %maximum_convert_fusion.gain_ref, f32[8,8,128]{2,1,0:T(8,128)S(1)} %all-to-all-done.sums_ref, ...), custom_call_target="tpu_custom_call" | custom-call | flops 3000000000 | bytes 3000000 | tf_op jit(solution)/shard_map/final/pallas_call | solution.py:359
  (19 shorter events, 0.0 us)
Async XLA Ops:
  0.6 24.7 %copy-start.1 = (bf16[256,640]{1,0:T(8,128)(2,1)S(1)}, bf16[256,640]{1,0:T(8,128)(2,1)}, u32[]{:S(2)}) copy-start(bf16[256,640]{1,0:T(8,128)(2,1)} %g_ref.3) | copy-start | bytes 983044
  0.6 1.0 %copy-start.2 = (bf16[256,640]{1,0:T(8,128)(2,1)S(1)}, bf16[256,640]{1,0:T(8,128)(2,1)}, u32[]{:S(2)}) copy-start(bf16[256,640]{1,0:T(8,128)(2,1)} %q_ref.9) | copy-start | bytes 983044
  1.7 1.0 copy-start.4
  2.6 22.7 %copy-start = (bf16[256,640]{1,0:T(8,128)(2,1)S(1)}, bf16[256,640]{1,0:T(8,128)(2,1)}, u32[]{:S(2)}) copy-start(bf16[256,640]{1,0:T(8,128)(2,1)} %v_ref.3) | copy-start | bytes 983044
  2.6 22.7 %copy-start.3 = (bf16[256,640]{1,0:T(8,128)(2,1)S(1)}, bf16[256,640]{1,0:T(8,128)(2,1)}, u32[]{:S(2)}) copy-start(bf16[256,640]{1,0:T(8,128)(2,1)} %q_ref.9) | copy-start | bytes 983044
  2.6 22.7 %copy-start.5 = (bf16[256,640]{1,0:T(8,128)(2,1)S(1)}, bf16[256,640]{1,0:T(8,128)(2,1)}, u32[]{:S(2)}) copy-start(bf16[256,640]{1,0:T(8,128)(2,1)} %k_ref.9) | copy-start | bytes 983044
  3.7 12.6 %copy-start.9 = (bf16[640]{0:T(1024)(128)(2,1)S(1)}, bf16[640]{0:T(1024)(128)(2,1)}, u32[]{:S(2)}) copy-start(bf16[640]{0:T(1024)(128)(2,1)} %param.12) | copy-start | bytes 3844
  3.7 21.6 %all-to-all-start = ((f32[8,8,128]{2,1,0:T(8,128)}), f32[8,8,128]{2,1,0:T(8,128)S(1)}, u32[]{:S(2)}, u32[]{:S(2)}) async-start(f32[8,8,128]{2,1,0:T(8,128)} %squares.1), calls=%async_computation | async-start | bytes 65536 | tf_op jit(solution)/shard_map/all_to_all | solution.py:315
  16.3 0.7 copy-start.8
  17.0 8.4 %copy-start.6 = (s32[5]{0:T(128)S(1)}, s32[5]{0:T(128)}, u32[]{:S(2)}) copy-start(s32[5]{0:T(128)} %cls_ref.9) | copy-start | bytes 64
  17.0 8.4 %copy-start.7 = (s32[5]{0:T(128)S(1)}, s32[5]{0:T(128)}, u32[]{:S(2)}) copy-start(s32[5]{0:T(128)} %band_ref.9) | copy-start | bytes 64
  27.0 31.1 %all-to-all-start.1 = ((bf16[64,4,8,128]{3,2,1,0:T(8,128)(2,1)}), bf16[64,4,8,128]{3,2,1,0:T(8,128)(2,1)S(1)}, u32[]{:S(2)}, u32[]{:S(2)}) async-start(bf16[64,4,8,128]{3,2,1,0:T(8,128)(2,1)} %get-tuple-element.14), calls=%async_computation.1 | async-start | bytes 1048576 | tf_op jit(solution)/shard_map/all_to_all | solution.py:328
  39.6 26.3 %collective-permute-start.1 = (bf16[4,256,128]{2,1,0:T(8,128)(2,1)S(1)}, bf16[4,256,128]{2,1,0:T(8,128)(2,1)S(1)}, u32[]{:S(2)}, u32[]{:S(2)}) collective-permute-start(bf16[4,256,128]{2,1,0:T(8,128)(2,1)S(1)} %get-tuple-element.17.halo_ref), channel_id=1, source_target_pairs={{8,0},{16,8},{24,16},{32,24},{40,32},{48,40},{56,48},{64,56},{72,6... | collective-permute-start | bytes 786440 | tf_op jit(solution)/shard_map/ppermute | solution.py:330
  41.9 24.0 %collective-permute-start = (bf16[4,256,128]{2,1,0:T(8,128)(2,1)S(1)}, bf16[4,256,128]{2,1,0:T(8,128)(2,1)S(1)}, u32[]{:S(2)}, u32[]{:S(2)}) collective-permute-start(bf16[4,256,128]{2,1,0:T(8,128)(2,1)S(1)} %get-tuple-element.17.halo_ref), channel_id=1, source_target_pairs={{0,8},{8,16},{16,24},{24,32},{32,40},{40,48},{48,56},{56,64},{64,7... | collective-permute-start | bytes 786440 | tf_op jit(solution)/shard_map/ppermute | solution.py:329
  60.6 23.8 %all-to-all-start.2 = ((bf16[64,3,8,128]{3,2,1,0:T(8,128)(2,1)}), bf16[64,3,8,128]{3,2,1,0:T(8,128)(2,1)S(1)}, u32[]{:S(2)}, u32[]{:S(2)}) async-start(bf16[64,3,8,128]{3,2,1,0:T(8,128)(2,1)} %temporal.1), calls=%async_computation.2 | async-start | bytes 786432 | tf_op jit(solution)/shard_map/all_to_all | solution.py:347
  68.8 8.6 %collective-permute-start.2 = (bf16[4,256,128]{2,1,0:T(8,128)(2,1)S(1)}, bf16[4,256,128]{2,1,0:T(8,128)(2,1)S(1)}, u32[]{:S(2)}, u32[]{:S(2)}) collective-permute-start(bf16[4,256,128]{2,1,0:T(8,128)(2,1)S(1)} %get-tuple-element.21), channel_id=1, source_target_pairs={{0,8},{8,16},{16,24},{24,32},{32,40},{40,48},{48,56},{56,64},{64,7... | collective-permute-start | bytes 786440 | tf_op jit(solution)/shard_map/ppermute | solution.py:344
  72.1 11.4 %collective-permute-start.3 = (bf16[4,256,128]{2,1,0:T(8,128)(2,1)S(1)}, bf16[4,256,128]{2,1,0:T(8,128)(2,1)S(1)}, u32[]{:S(2)}, u32[]{:S(2)}) collective-permute-start(bf16[4,256,128]{2,1,0:T(8,128)(2,1)S(1)} %get-tuple-element.22), channel_id=1, source_target_pairs={{8,0},{16,8},{24,16},{32,24},{40,32},{48,40},{56,48},{64,56},{72,6... | collective-permute-start | bytes 786440 | tf_op jit(solution)/shard_map/ppermute | solution.py:345

commit v2 on v1

--- a/solution.py
+++ b/solution.py
@@ -17,11 +17,13 @@
 EPSILON = 1e-06
 SCALE = 1.0 / math.sqrt(HD)
 NEG = -1e30
+LOG2E = math.log2(math.e)
 
 BF = jnp.bfloat16
 F32 = jnp.float32
 VM = pl.BlockSpec(memory_space=pltpu.VMEM)
 SM = pl.BlockSpec(memory_space=pltpu.SMEM)
+ANY = pl.BlockSpec(memory_space=pl.ANY)
 
 
 def shape(dims, dtype):
@@ -104,58 +106,67 @@
     return lax.rsqrt(jnp.sum(sums_ref[...], axis=0) / FULL + EPSILON)
 
 
-def squares_body(q_ref, k_ref, out_ref):
+def squares_body(cls_ref, band_ref, q_hbm, k_hbm, v_hbm, out_ref, halo_ref, q_ref, k_ref, v_ref, sems):
+    copies = [
+        pltpu.make_async_copy(source, target, sems.at[i])
+        for i, (source, target) in enumerate(((q_hbm, q_ref), (k_hbm, k_ref), (v_hbm, v_ref)))
+    ]
+    for copy in copies:
+        copy.start()
+    slots, _ = head_slots(cls_ref, band_ref)
     sums = []
-    for ref in (q_ref, k_ref):
+    for copy, ref in zip(copies, (q_ref, k_ref)):
+        copy.wait()
         total = jnp.zeros((TOK, HD), F32)
         for head in range(HEADS_DEV):
             wide = ref[:, head * HD : (head + 1) * HD].astype(F32)
             total += wide * wide
         sums.append(lane_sums(total))
     out_ref[...] = jnp.broadcast_to(rows_of(*sums)[None], (8, 8, HD))
+    copies[2].wait()
+    for s in (1, 2):
+        halo_ref[2 * s - 2] = k_ref[:, columns(slots[s])]
+        halo_ref[2 * s - 1] = v_ref[:, columns(slots[s])]
+
+
+def gains_body(q_ref, k_ref, after_ref, g_ref, out_ref):
+    out_ref[0] = q_ref[...].astype(F32)
+    out_ref[1] = k_ref[...].astype(F32)
+
+
+def normed(values, inverse, gain):
+    return (values.astype(F32) * inverse * gain).astype(BF)
 
 
 def norm_body(
-    cls_ref, band_ref, sums_ref, gain_ref, q_ref, k_ref, v_ref, g_ref, send_ref, halo_ref, qs_ref, ks_ref
+    cls_ref, band_ref, sums_ref, gain_ref, q_ref, k_ref, v_ref, g_ref, after_ref, send_ref, inv_ref
 ):
     slots, _ = head_slots(cls_ref, band_ref)
     inv = inverses(sums_ref)
+    inv_ref[...] = inv
     q_inv, k_inv = spread(inv, 0), spread(inv, 2)
-
-    def normed(ref, inverse, which, slot):
-        gain = gain_ref[which, pl.ds(slot, 1), :]
-        return (ref[:, columns(slot)].astype(F32) * inverse * gain).astype(BF)
-
     for s in range(2):
         slot = slots[3 + s]
+        at = columns(slot)
         parts = (
-            normed(q_ref, q_inv, 0, slot),
-            normed(k_ref, k_inv, 1, slot),
-            v_ref[:, columns(slot)],
-            g_ref[:, columns(slot)],
+            normed(q_ref[:, at], q_inv, gain_ref[0, pl.ds(slot, 1), :]),
+            normed(k_ref[:, at], k_inv, gain_ref[1, pl.ds(slot, 1), :]),
+            v_ref[:, at],
+            g_ref[:, at],
         )
         for a, part in enumerate(parts):
             send_ref[s * 32 : (s + 1) * 32, a] = part.reshape(32, 8, HD)
-    for s in range(3):
-        slot = slots[s]
-        qs_ref[s] = normed(q_ref, q_inv, 0, slot)
-        k_norm = normed(k_ref, k_inv, 1, slot)
-        if s == 0:
-            ks_ref[...] = k_norm
-        else:
-            halo_ref[2 * s - 2] = k_norm
-            halo_ref[2 * s - 1] = v_ref[:, columns(slot)]
 
 
 def attend(q, g, keys, values, allowed):
     scores = []
     for key, ok in zip(keys, allowed):
-        score = dot_nt(key, q) * SCALE
+        score = dot_nt(key, q)
         scores.append(score if ok is None else jnp.where(ok, score, NEG))
     largest = functools.reduce(
         jnp.maximum, [jnp.max(score, axis=0, keepdims=True) for score in scores]
     )
-    powers = [jnp.exp(score - largest) for score in scores]
+    powers = [jnp.exp2((score - largest) * (SCALE * LOG2E)) for score in scores]
     totals = sum(jnp.sum(power, axis=0, keepdims=True) for power in powers)
     inverse = 1.0 / totals
     probs = [power * inverse for power in powers]
@@ -172,45 +183,57 @@
     cls_ref,
     band_ref,
     frame_ref,
-    qs_ref,
-    ks_ref,
-    halo_ref,
-    low_ref,
-    high_ref,
+    gain_ref,
+    inv_ref,
+    inv_near_ref,
+    inv_far_ref,
+    q_ref,
+    k_ref,
     v_ref,
     g_ref,
+    near_ref,
+    far_ref,
     dq_ref,
     fin_ref,
     own_ref,
-    to_low_ref,
-    to_high_ref,
+    to_near_ref,
+    to_far_ref,
+    done_ref,
 ):
+    done_ref[...] = inv_ref[...]
     slots, bands = head_slots(cls_ref, band_ref)
     frame = frame_ref[0]
-    d_q, d_k, d_v = attend(
-        qs_ref[0], g_ref[:, columns(slots[0])], [ks_ref[...]], [v_ref[:, columns(slots[0])]], [None]
-    )
-    dq_ref[0] = d_q.astype(BF)
-    fin_ref[0] = d_k[0].astype(BF)
-    fin_ref[1] = d_v[0].astype(BF)
-    for s in (1, 2):
-        at = 2 * s - 2
-        wide = bands[s - 1] > 0
-        g = g_ref[:, columns(slots[s])]
-        keys = [low_ref[at], halo_ref[at], high_ref[at]]
-        values = [low_ref[at + 1], halo_ref[at + 1], high_ref[at + 1]]
-        allowed = [wide & (frame > 0), None, wide & (frame < FRAMES - 1)]
-        d_q, d_k, d_v = attend(qs_ref[s], g, keys, values, allowed)
+    inv = inv_ref[...]
+    q_inv, k_inv = spread(inv, 0), spread(inv, 2)
+    near_inv, far_inv = spread(inv_near_ref[...], 2), spread(inv_far_ref[...], 2)
+    for s in range(3):
+        slot = slots[s]
+        cols = columns(slot)
+        k_gain = gain_ref[1, pl.ds(slot, 1), :]
+        q = normed(q_ref[:, cols], q_inv, gain_ref[0, pl.ds(slot, 1), :])
+        k = normed(k_ref[:, cols], k_inv, k_gain)
+        v, g = v_ref[:, cols], g_ref[:, cols]
+        if s == 0:
+            d_q, d_k, d_v = attend(q, g, [k], [v], [None])
+            fin_ref[0] = d_k[0].astype(BF)
+            fin_ref[1] = d_v[0].astype(BF)
+        else:
+            at = 2 * s - 2
+            wide = bands[s - 1] > 0
+            keys = [normed(near_ref[at], near_inv, k_gain), k, normed(far_ref[at], far_inv, k_gain)]
+            values = [near_ref[at + 1], v, far_ref[at + 1]]
+            allowed = [wide, None, wide & (frame > 0) & (frame < FRAMES - 1)]
+            d_q, d_k, d_v = attend(q, g, keys, values, allowed)
+            to_near_ref[at] = d_k[0].astype(BF)
+            to_near_ref[at + 1] = d_v[0].astype(BF)
+            own_ref[at] = d_k[1]
+            own_ref[at + 1] = d_v[1]
+            to_far_ref[at] = d_k[2].astype(BF)
+            to_far_ref[at + 1] = d_v[2].astype(BF)
         dq_ref[s] = d_q.astype(BF)
-        to_low_ref[at] = d_k[0].astype(BF)
-        to_low_ref[at + 1] = d_v[0].astype(BF)
-        own_ref[at] = d_k[1]
-        own_ref[at + 1] = d_v[1]
-        to_high_ref[at] = d_k[2].astype(BF)
-        to_high_ref[at + 1] = d_v[2].astype(BF)
-
-
-def temporal_body(in_ref, out_ref):
+
+
+def temporal_body(in_ref, after_ref, out_ref):
     rows = FRAMES * 8
     q, k, v, g = (in_ref[:, a].reshape(rows, HD) for a in range(4))
     d_k = jnp.zeros((rows, HD), F32)
@@ -235,7 +258,7 @@
 
 
 def spatial_sums_body(
-    cls_ref, band_ref, gain_ref, q_ref, k_ref, dq_ref, fin_ref, own_ref, low_ref, high_ref, grad_ref, part_ref
+    cls_ref, band_ref, gain_ref, q_ref, k_ref, dq_ref, fin_ref, own_ref, near_ref, far_ref, grad_ref, part_ref
 ):
     slots, _ = head_slots(cls_ref, band_ref)
     q_total = product(gain_ref, 0, slots[0], dq_ref[0], q_ref)
@@ -244,7 +267,7 @@
         for b in range(2):
             at = 2 * s - 2 + b
             grad_ref[at] = (
-                own_ref[at] + low_ref[at].astype(F32) + high_ref[at].astype(F32)
+                own_ref[at] + near_ref[at].astype(F32) + far_ref[at].astype(F32)
             ).astype(BF)
         q_total += product(gain_ref, 0, slots[s], dq_ref[s], q_ref)
         k_total += product(gain_ref, 1, slots[s], grad_ref[2 * s - 2], k_ref)
@@ -264,11 +287,20 @@
     out_ref[...] = jnp.broadcast_to(rows_of(*sums)[None], (8, 8, HD))
 
 
+def value_body(cls_ref, band_ref, back_ref, fin_ref, grad_ref, out_ref):
+    slots, _ = head_slots(cls_ref, band_ref)
+    out_ref[:, columns(slots[0])] = fin_ref[1]
+    for s in (1, 2):
+        out_ref[:, columns(slots[s])] = grad_ref[2 * s - 1]
+    for s in range(2):
+        out_ref[:, columns(slots[3 + s])] = back_ref[s * 32 : (s + 1) * 32, 2].reshape(TOK, HD)
+
+
 def final_body(
     cls_ref,
     band_ref,
     gain_ref,
-    sums_ref,
+    inv_ref,
     inner_ref,
     q_ref,
     k_ref,
@@ -278,10 +310,9 @@
     grad_ref,
     out_q_ref,
     out_k_ref,
-    out_v_ref,
 ):
     slots, _ = head_slots(cls_ref, band_ref)
-    inv = inverses(sums_ref)
+    inv = inv_ref[...]
     pull = inv * inv * inv * jnp.sum(inner_ref[...], axis=0) / FULL
     for which, (ref, out) in enumerate(((q_ref, out_q_ref), (k_ref, out_k_ref))):
         inverse, pulled = spread(inv, 2 * which), spread(pull, 2 * which)
@@ -297,38 +328,40 @@
             out[:, at] = (
                 inverse * gain * grad.astype(F32) - ref[:, at].astype(F32) * pulled
             ).astype(BF)
-    out_v_ref[:, columns(slots[0])] = fin_ref[1]
-    for s in (1, 2):
-        out_v_ref[:, columns(slots[s])] = grad_ref[2 * s - 1]
-    for s in range(2):
-        out_v_ref[:, columns(slots[3 + s])] = back_ref[s * 32 : (s + 1) * 32, 2].reshape(TOK, HD)
 
 
 def per_device(query_pre, key_pre, value, d_out, gain_q, gain_k, head_class, head_band):
-    gains = jnp.stack([gain_q, gain_k]).astype(F32).reshape(2, HEADS_DEV, HD)
     frame = lax.axis_index("seq").astype(jnp.int32).reshape(1)
-    up = [(i, i + 1) for i in range(FRAMES - 1)]
-    down = [(i + 1, i) for i in range(FRAMES - 1)]
+    core = [(i, i ^ 1) for i in range(FRAMES)]
+    chip = [(i, ((i - 1) ^ 1) + 1) for i in range(1, FRAMES - 1)]
     block = (4, TOK, HD)
 
-    sums = call(squares_body, shape((8, 8, HD), F32), [VM] * 2, "squares", 2)(query_pre, key_pre)
+    sums, halo = pl.pallas_call(
+        squares_body,
+        out_shape=(shape((8, 8, HD), F32), shape(block, BF)),
+        in_specs=[SM, SM] + [ANY] * 3,
+        out_specs=(VM,) * 2,
+        scratch_shapes=[pltpu.VMEM((TOK, WIDTH), BF)] * 3 + [pltpu.SemaphoreType.DMA((3,))],
+        name="squares",
+        compiler_params=pltpu.CompilerParams(vmem_limit_bytes=56 << 20),
+    )(head_class, head_band, query_pre, key_pre, value)
+    gains = call(gains_body, shape((2, HEADS_DEV, HD), F32), [VM, VM, ANY, VM], "gains", 1)(
+        gain_q.reshape(HEADS_DEV, HD), gain_k.reshape(HEADS_DEV, HD), sums, d_out
+    )
+    near = lax.ppermute(halo, "seq", core)
+    far = lax.ppermute(halo, "seq", chip)
     sums = lax.all_to_all(sums, "head", 0, 0, tiled=True)
-    send, halo, qs, ks = call(
+    send, inv = call(
         norm_body,
-        (
-            shape((FRAMES, 4, 8, HD), BF),
-            shape(block, BF),
-            shape((3, TOK, HD), BF),
-            shape((TOK, HD), BF),
-        ),
-        [SM, SM] + [VM] * 6,
+        (shape((FRAMES, 4, 8, HD), BF), shape((8, HD), F32)),
+        [SM, SM] + [VM] * 6 + [ANY],
         "norm",
-        3,
-    )(head_class, head_band, sums, gains, query_pre, key_pre, value, d_out)
+        2,
+    )(head_class, head_band, sums, gains, query_pre, key_pre, value, d_out, far)
     held = lax.all_to_all(send, "seq", 0, 0, tiled=True)
-    low = lax.ppermute(halo, "seq", up)
-    high = lax.ppermute(halo, "seq", down)
-    dq, fin, own, to_low, to_high = call(
+    inv_near = lax.ppermute(inv, "seq", core)
+    inv_far = lax.ppermute(inv, "seq", chip)
+    dq, fin, own, to_near, to_far, done = call(
         spatial_body,
         (
             shape((3, TOK, HD), BF),
@@ -336,14 +369,29 @@
             shape(block, F32),
             shape(block, BF),
             shape(block, BF),
+            shape((8, HD), F32),
         ),
-        [SM] * 3 + [VM] * 7,
+        [SM] * 3 + [VM] * 10,
         "spatial",
-        6,
-    )(head_class, head_band, frame, qs, ks, halo, low, high, value, d_out)
-    from_low = lax.ppermute(to_high, "seq", up)
-    from_high = lax.ppermute(to_low, "seq", down)
-    grads = call(temporal_body, shape((FRAMES, 3, 8, HD), BF), [VM], "temporal", 3)(held)
+        4,
+    )(
+        head_class,
+        head_band,
+        frame,
+        gains,
+        inv,
+        inv_near,
+        inv_far,
+        query_pre,
+        key_pre,
+        value,
+        d_out,
+        near,
+        far,
+    )
+    from_near = lax.ppermute(to_near, "seq", core)
+    from_far = lax.ppermute(to_far, "seq", chip)
+    grads = call(temporal_body, shape((FRAMES, 3, 8, HD), BF), [VM, ANY], "temporal", 3)(held, done)
     back = lax.all_to_all(grads, "seq", 0, 0, tiled=True)
     grad, part = call(
         spatial_sums_body,
@@ -351,18 +399,18 @@
         [SM, SM] + [VM] * 8,
         "spatial_sums",
         3,
-    )(head_class, head_band, gains, query_pre, key_pre, dq, fin, own, from_low, from_high)
-    inner = call(
-        inner_body, shape((8, 8, HD), F32), [SM, SM] + [VM] * 5, "inner", 2
-    )(head_class, head_band, gains, query_pre, key_pre, back, part)
+    )(head_class, head_band, gains, query_pre, key_pre, dq, fin, own, from_near, from_far)
+    inner = call(inner_body, shape((8, 8, HD), F32), [SM, SM] + [VM] * 5, "inner", 2)(
+        head_class, head_band, gains, query_pre, key_pre, back, part
+    )
     inner = lax.all_to_all(inner, "head", 0, 0, tiled=True)
-    return call(
-        final_body,
-        (shape((TOK, WIDTH), BF),) * 3,
-        [SM, SM] + [VM] * 9,
-        "final",
-        3,
-    )(head_class, head_band, gains, sums, inner, query_pre, key_pre, back, dq, fin, grad)
+    d_value = call(value_body, shape((TOK, WIDTH), BF), [SM, SM] + [VM] * 3, "value", 2)(
+        head_class, head_band, back, fin, grad
+    )
+    d_query, d_key = call(
+        final_body, (shape((TOK, WIDTH), BF),) * 2, [SM, SM] + [VM] * 9, "final", 3
+    )(head_class, head_band, gains, inv, inner, query_pre, key_pre, back, dq, fin, grad)
+    return d_query, d_key, d_value
 
 
 def solution(mesh):

time: 99.1 us -> 105 us (1.060)
  the two profiles are of different devices: /device:TPU:9 before, /device:TPU:24 now
where the time goes in v2:
time: 105 us
  starting transfers between devices  52.2 us (50%)
  waiting for transfers between devices  33.9 us (32%)
  Pallas kernels  15.6 us (15%)
  local copies, waits for them, and re-layouts  2.02 us (2%)
    all_to_all x1, starting transfers between devices, per_device(): sums = lax.all_to_all(sums, 'head', 0, 0, tiled=True)  10.1 us
    all_to_all x1, waiting for transfers between devices, per_device(): sums = lax.all_to_all(sums, 'head', 0, 0, tiled=True)  9.45 us
    ppermute x1, waiting for transfers between devices, per_device(): from_far = lax.ppermute(to_far, 'seq', chip)  9.07 us
    all_to_all x1, waiting for transfers between devices, per_device(): inner = lax.all_to_all(inner, 'head', 0, 0, tiled=True)  8.8 us
    all_to_all x1, starting transfers between devices, per_device(): held = lax.all_to_all(send, 'seq', 0, 0, tiled=True)  8.18 us
    ppermute x1, starting transfers between devices, per_device(): far = lax.ppermute(halo, 'seq', chip)  7.22 us
    all_to_all x1, starting transfers between devices, per_device(): back = lax.all_to_all(grads, 'seq', 0, 0, tiled=True)  7.12 us
    ppermute x1, waiting for transfers between devices, per_device(): inv_far = lax.ppermute(inv, 'seq', chip)  6.6 us
  transfers between devices with their start and end apart: 10, of which 4 were waited for; matrix products, arithmetic and copies ran while one was open for 0% of the time, Pallas kernels for 5%

profile of v2, /device:TPU:24, one launch (start us, length us, event | category | flops | bytes accessed | tf_op | source)
XLA Modules:
  0.0 104.7 jit_solution(12928667145270970676)
XLA Ops:
  0.6 3.3 %squares.1 = (f32[8,8,128]{2,1,0:T(8,128)}, bf16[4,256,128]{2,1,0:T(8,128)(2,1)}) custom-call(s32[5]{0:T(128)} %cls_ref.13, s32[5]{0:T(128)} %band_ref.13, bf16[256,640]{1,0:T(8,128)(2,1)} %q_ref.9, bf16[256,640]{1,0:T(8,128)(2,1)} %k_ref.9, bf16[256,640]{1,0:T(8,128)(2,1)} %v_ref.3), custom_call_target="tpu_custom_call" | custom-call | tf_op jit(solution)/shard_map/squares/pallas_call | solution.py:339
  3.9 7.2 %collective-permute-start = (bf16[4,256,128]{2,1,0:T(8,128)(2,1)}, bf16[4,256,128]{2,1,0:T(8,128)(2,1)S(1)}, u32[]{:S(2)}, u32[]{:S(2)}) collective-permute-start(bf16[4,256,128]{2,1,0:T(8,128)(2,1)} %get-tuple-element.18), channel_id=1, source_target_pairs={{8,16},{16,8},{24,32},{32,24},{40,48},{48,40},{56,64},{64,56},{72,... | collective-permute-start | bytes 786440 | tf_op jit(solution)/shard_map/ppermute | solution.py:352
  11.2 10.1 %all-to-all-start = ((f32[8,8,128]{2,1,0:T(8,128)}), f32[8,8,128]{2,1,0:T(8,128)S(1)}, u32[]{:S(2)}, u32[]{:S(2)}) async-start(f32[8,8,128]{2,1,0:T(8,128)} %get-tuple-element.17.after_ref), calls=%async_computation | async-start | bytes 65536 | tf_op jit(solution)/shard_map/all_to_all | solution.py:353
  21.3 0.6 copy-done.7
  22.0 9.4 %all-to-all-done.sums_ref = f32[8,8,128]{2,1,0:T(8,128)S(1)} async-done(((f32[8,8,128]{2,1,0:T(8,128)}), f32[8,8,128]{2,1,0:T(8,128)S(1)}, u32[]{:S(2)}, u32[]{:S(2)}) %all-to-all-start) | async-done | bytes 32800 | tf_op jit(solution)/shard_map/all_to_all | solution.py:353
  31.5 1.5 %norm.1 = (bf16[64,4,8,128]{3,2,1,0:T(8,128)(2,1)}, f32[8,128]{1,0:T(8,128)S(1)}) custom-call(s32[5]{0:T(128)S(1)} %copy-done.4, s32[5]{0:T(128)S(1)} %copy-done.5, f32[8,8,128]{2,1,0:T(8,128)S(1)} %all-to-all-done.sums_ref, f32[2,5,128]{2,1,0:T(8,128)S(1)} %gains.1.gain_ref, bf16[256,640]{1,0:T(8,128)(2,1)S(1)} %copy-done.1, ...), custom_call_target="tpu_custom_call" | custom-call | flops 2000000000 | bytes 2000000 | tf_op jit(solution)/shard_map/norm/pallas_call | solution.py:354
  33.0 8.2 %all-to-all-start.1 = ((bf16[64,4,8,128]{3,2,1,0:T(8,128)(2,1)}), bf16[64,4,8,128]{3,2,1,0:T(8,128)(2,1)S(1)}, u32[]{:S(2)}, u32[]{:S(2)}) async-start(bf16[64,4,8,128]{3,2,1,0:T(8,128)(2,1)} %get-tuple-element.20), calls=%async_computation.1 | async-start | bytes 1048576 | tf_op jit(solution)/shard_map/all_to_all | solution.py:361
  41.2 2.1 %collective-permute-start.3 = (bf16[4,256,128]{2,1,0:T(8,128)(2,1)S(1)}, bf16[4,256,128]{2,1,0:T(8,128)(2,1)S(1)}, u32[]{:S(2)}, u32[]{:S(2)}) collective-permute-start(bf16[4,256,128]{2,1,0:T(8,128)(2,1)S(1)} %copy-done.13), channel_id=1, source_target_pairs={{0,8},{8,0},{16,24},{24,16},{32,40},{40,32},{48,56},{56,48},{64,72... | collective-permute-start | bytes 786440 | tf_op jit(solution)/shard_map/ppermute | solution.py:351
  43.3 5.1 %collective-permute-start.2 = (f32[8,128]{1,0:T(8,128)S(1)}, f32[8,128]{1,0:T(8,128)S(1)}, u32[]{:S(2)}, u32[]{:S(2)}) collective-permute-start(f32[8,128]{1,0:T(8,128)S(1)} %get-tuple-element.19.inv_ref), channel_id=1, source_target_pairs={{8,16},{16,8},{24,32},{32,24},{40,48},{48,40},{56,64},{64,56},{72,... | collective-permute-start | bytes 12296 | tf_op jit(solution)/shard_map/ppermute | solution.py:363
  48.4 1.9 %collective-permute-start.1 = (f32[8,128]{1,0:T(8,128)S(1)}, f32[8,128]{1,0:T(8,128)S(1)}, u32[]{:S(2)}, u32[]{:S(2)}) collective-permute-start(f32[8,128]{1,0:T(8,128)S(1)} %get-tuple-element.19.inv_ref), channel_id=1, source_target_pairs={{0,8},{8,0},{16,24},{24,16},{32,40},{40,32},{48,56},{56,48},{64,72... | collective-permute-start | bytes 12296 | tf_op jit(solution)/shard_map/ppermute | solution.py:362
  50.3 6.6 %collective-permute-done.2.inv_far_ref = f32[8,128]{1,0:T(8,128)S(1)} collective-permute-done((f32[8,128]{1,0:T(8,128)S(1)}, f32[8,128]{1,0:T(8,128)S(1)}, u32[]{:S(2)}, u32[]{:S(2)}) %collective-permute-start.2) | collective-permute-done | bytes 4128 | tf_op jit(solution)/shard_map/ppermute | solution.py:363
  56.9 3.0 %spatial.1 = (bf16[3,256,128]{2,1,0:T(8,128)(2,1)S(1)}, bf16[2,256,128]{2,1,0:T(8,128)(2,1)S(1)}, f32[4,256,128]{2,1,0:T(8,128)S(1)}, bf16[4,256,128]{2,1,0:T(8,...) custom-call(s32[5]{0:T(128)S(1)} %copy-done.4, s32[5]{0:T(128)S(1)} %copy-done.5, ...), custom_call_target="tpu_custom_call" | custom-call | flops 4000000000 | bytes 4000000 | tf_op jit(solution)/shard_map/spatial/pallas_call | solution.py:364
  60.6 0.7 copy-done.11
  61.2 2.5 %temporal.1 = bf16[64,3,8,128]{3,2,1,0:T(8,128)(2,1)} custom-call(bf16[64,4,8,128]{3,2,1,0:T(8,128)(2,1)S(1)} %all-to-all-done.1.in_ref, f32[8,128]{1,0:T(8,128)S(1)} %get-tuple-element.21.after_ref), custom_call_target="tpu_custom_call" | custom-call | flops 3000000000 | bytes 3000000 | tf_op jit(solution)/shard_map/temporal/pallas_call | solution.py:394
  63.7 7.1 %all-to-all-start.2 = ((bf16[64,3,8,128]{3,2,1,0:T(8,128)(2,1)}), bf16[64,3,8,128]{3,2,1,0:T(8,128)(2,1)S(1)}, u32[]{:S(2)}, u32[]{:S(2)}) async-start(bf16[64,3,8,128]{3,2,1,0:T(8,128)(2,1)} %temporal.1), calls=%async_computation.2 | async-start | bytes 786432 | tf_op jit(solution)/shard_map/all_to_all | solution.py:395
  70.8 2.1 %collective-permute-start.4 = (bf16[4,256,128]{2,1,0:T(8,128)(2,1)S(1)}, bf16[4,256,128]{2,1,0:T(8,128)(2,1)S(1)}, u32[]{:S(2)}, u32[]{:S(2)}) collective-permute-start(bf16[4,256,128]{2,1,0:T(8,128)(2,1)S(1)} %get-tuple-element.25), channel_id=1, source_target_pairs={{0,8},{8,0},{16,24},{24,16},{32,40},{40,32},{48,56},{56,48},{64,72... | collective-permute-start | bytes 786440 | tf_op jit(solution)/shard_map/ppermute | solution.py:392
  72.9 5.1 %collective-permute-start.5 = (bf16[4,256,128]{2,1,0:T(8,128)(2,1)S(1)}, bf16[4,256,128]{2,1,0:T(8,128)(2,1)S(1)}, u32[]{:S(2)}, u32[]{:S(2)}) collective-permute-start(bf16[4,256,128]{2,1,0:T(8,128)(2,1)S(1)} %get-tuple-element.26), channel_id=1, source_target_pairs={{8,16},{16,8},{24,32},{32,24},{40,48},{48,40},{56,64},{64,56},{72,... | collective-permute-start | bytes 786440 | tf_op jit(solution)/shard_map/ppermute | solution.py:393
  78.0 9.1 %collective-permute-done.5.far_ref = bf16[4,256,128]{2,1,0:T(8,128)(2,1)S(1)} collective-permute-done((bf16[4,256,128]{2,1,0:T(8,128)(2,1)S(1)}, bf16[4,256,128]{2,1,0:T(8,128)(2,1)S(1)}, u32[]{:S(2)}, u32[]{:S(2)}) %collective-permute-start.5) | collective-permute-done | bytes 262176 | tf_op jit(solution)/shard_map/ppermute | solution.py:393
  87.1 0.8 spatial_sums.1
  87.9 1.6 %inner.1 = f32[8,8,128]{2,1,0:T(8,128)} custom-call(s32[5]{0:T(128)S(1)} %copy-done.4, s32[5]{0:T(128)S(1)} %copy-done.5, f32[2,5,128]{2,1,0:T(8,128)S(1)} %gains.1.gain_ref, bf16[256,640]{1,0:T(8,128)(2,1)S(1)} %copy-done.1, bf16[256,640]{1,0:T(8,128)(2,1)S(1)} %copy-done.2, bf16[64,3,8,128]{3,2,1,0:T(8,128)(2,1)S(1)} %all-to-all-done.2.back_ref, ...), custom_call_target="tpu_custom_call" | custom-call | flops 2000000000 | bytes 2000000 | tf_op jit(solution)/shard_map/inner/pallas_call | solution.py:403
  89.5 3.3 %all-to-all-start.3 = ((f32[8,8,128]{2,1,0:T(8,128)}), f32[8,8,128]{2,1,0:T(8,128)S(1)}, u32[]{:S(2)}, u32[]{:S(2)}) async-start(f32[8,8,128]{2,1,0:T(8,128)} %inner.1), calls=%async_computation.3 | async-start | bytes 65536 | tf_op jit(solution)/shard_map/all_to_all | solution.py:406
  92.9 1.3 %value.1 = bf16[256,640]{1,0:T(8,128)(2,1)} custom-call(s32[5]{0:T(128)S(1)} %copy-done.4, s32[5]{0:T(128)S(1)} %copy-done.5, bf16[64,3,8,128]{3,2,1,0:T(8,128)(2,1)S(1)} %all-to-all-done.2.back_ref, bf16[2,256,128]{2,1,0:T(8,128)(2,1)S(1)} %copy-done.10, bf16[4,256,128]{2,1,0:T(8,128)(2,1)S(1)} %get-tuple-element.28.grad_ref), custom_call_target="tpu_custom_call" | custom-call | flops 2000000000 | bytes 2000000 | tf_op jit(solution)/shard_map/value/pallas_call | solution.py:407
  94.2 8.8 %all-to-all-done.3.inner_ref = f32[8,8,128]{2,1,0:T(8,128)S(1)} async-done(((f32[8,8,128]{2,1,0:T(8,128)}), f32[8,8,128]{2,1,0:T(8,128)S(1)}, u32[]{:S(2)}, u32[]{:S(2)}) %all-to-all-start.3) | async-done | bytes 32800 | tf_op jit(solution)/shard_map/all_to_all | solution.py:406
  103.0 1.7 %final.1 = (bf16[256,640]{1,0:T(8,128)(2,1)}, bf16[256,640]{1,0:T(8,128)(2,1)}) custom-call(s32[5]{0:T(128)S(1)} %copy-done.4, s32[5]{0:T(128)S(1)} %copy-done.5, f32[2,5,128]{2,1,0:T(8,128)S(1)} %gains.1.gain_ref, f32[8,128]{1,0:T(8,128)S(1)} %get-tuple-element.19.inv_ref, f32[8,8,128]{2,1,0:T(8,128)S(1)} %all-to-all-done.3.inner_ref, ...), custom_call_target="tpu_custom_call" | custom-call | flops 3000000000 | bytes 3000000 | tf_op jit(solution)/shard_map/final/pallas_call | solution.py:410
  (33 shorter events, 0.7 us)
Async XLA Ops:
  0.6 20.6 %copy-start.6 = (bf16[256,640]{1,0:T(8,128)(2,1)S(1)}, bf16[256,640]{1,0:T(8,128)(2,1)}, u32[]{:S(2)}) copy-start(bf16[256,640]{1,0:T(8,128)(2,1)} %g_ref.5) | copy-start | bytes 983044
  3.9 27.5 %collective-permute-start = (bf16[4,256,128]{2,1,0:T(8,128)(2,1)}, bf16[4,256,128]{2,1,0:T(8,128)(2,1)S(1)}, u32[]{:S(2)}, u32[]{:S(2)}) collective-permute-start(bf16[4,256,128]{2,1,0:T(8,128)(2,1)} %get-tuple-element.18), channel_id=1, source_target_pairs={{8,16},{16,8},{24,32},{32,24},{40,48},{48,40},{56,64},{64,56},{72,... | collective-permute-start | bytes 786440 | tf_op jit(solution)/shard_map/ppermute | solution.py:352
  11.2 10.1 %copy-start.3 = (f32[8,8,128]{2,1,0:T(8,128)S(1)}, f32[8,8,128]{2,1,0:T(8,128)}, u32[]{:S(2)}) copy-start(f32[8,8,128]{2,1,0:T(8,128)} %get-tuple-element.17.after_ref) | copy-start | bytes 98308
  11.2 10.1 %copy-start.8 = (bf16[640]{0:T(1024)(128)(2,1)S(1)}, bf16[640]{0:T(1024)(128)(2,1)}, u32[]{:S(2)}) copy-start(bf16[640]{0:T(1024)(128)(2,1)} %param.13) | copy-start | bytes 3844
  11.2 20.2 %all-to-all-start = ((f32[8,8,128]{2,1,0:T(8,128)}), f32[8,8,128]{2,1,0:T(8,128)S(1)}, u32[]{:S(2)}, u32[]{:S(2)}) async-start(f32[8,8,128]{2,1,0:T(8,128)} %get-tuple-element.17.after_ref), calls=%async_computation | async-start | bytes 65536 | tf_op jit(solution)/shard_map/all_to_all | solution.py:353
  21.2 0.7 copy-start.7
  21.9 9.5 %copy-start = (bf16[256,640]{1,0:T(8,128)(2,1)S(1)}, bf16[256,640]{1,0:T(8,128)(2,1)}, u32[]{:S(2)}) copy-start(bf16[256,640]{1,0:T(8,128)(2,1)} %v_ref.3) | copy-start | bytes 983044
  21.9 9.5 %copy-start.1 = (bf16[256,640]{1,0:T(8,128)(2,1)S(1)}, bf16[256,640]{1,0:T(8,128)(2,1)}, u32[]{:S(2)}) copy-start(bf16[256,640]{1,0:T(8,128)(2,1)} %q_ref.9) | copy-start | bytes 983044
  21.9 9.5 %copy-start.2 = (bf16[256,640]{1,0:T(8,128)(2,1)S(1)}, bf16[256,640]{1,0:T(8,128)(2,1)}, u32[]{:S(2)}) copy-start(bf16[256,640]{1,0:T(8,128)(2,1)} %k_ref.9) | copy-start | bytes 983044
  21.9 9.5 %copy-start.4 = (s32[5]{0:T(128)S(1)}, s32[5]{0:T(128)}, u32[]{:S(2)}) copy-start(s32[5]{0:T(128)} %cls_ref.13) | copy-start | bytes 64
  21.9 9.5 %copy-start.5 = (s32[5]{0:T(128)S(1)}, s32[5]{0:T(128)}, u32[]{:S(2)}) copy-start(s32[5]{0:T(128)} %band_ref.13) | copy-start | bytes 64
  33.0 8.2 %copy-start.13 = (bf16[4,256,128]{2,1,0:T(8,128)(2,1)S(1)}, bf16[4,256,128]{2,1,0:T(8,128)(2,1)}, u32[]{:S(2)}) copy-start(bf16[4,256,128]{2,1,0:T(8,128)(2,1)} %get-tuple-element.18) | copy-start | bytes 786436
  33.0 28.3 %all-to-all-start.1 = ((bf16[64,4,8,128]{3,2,1,0:T(8,128)(2,1)}), bf16[64,4,8,128]{3,2,1,0:T(8,128)(2,1)S(1)}, u32[]{:S(2)}, u32[]{:S(2)}) async-start(bf16[64,4,8,128]{3,2,1,0:T(8,128)(2,1)} %get-tuple-element.20), calls=%async_computation.1 | async-start | bytes 1048576 | tf_op jit(solution)/shard_map/all_to_all | solution.py:361
  41.2 9.1 %collective-permute-start.3 = (bf16[4,256,128]{2,1,0:T(8,128)(2,1)S(1)}, bf16[4,256,128]{2,1,0:T(8,128)(2,1)S(1)}, u32[]{:S(2)}, u32[]{:S(2)}) collective-permute-start(bf16[4,256,128]{2,1,0:T(8,128)(2,1)S(1)} %copy-done.13), channel_id=1, source_target_pairs={{0,8},{8,0},{16,24},{24,16},{32,40},{40,32},{48,56},{56,48},{64,72... | collective-permute-start | bytes 786440 | tf_op jit(solution)/shard_map/ppermute | solution.py:351
  43.3 13.7 %collective-permute-start.2 = (f32[8,128]{1,0:T(8,128)S(1)}, f32[8,128]{1,0:T(8,128)S(1)}, u32[]{:S(2)}, u32[]{:S(2)}) collective-permute-start(f32[8,128]{1,0:T(8,128)S(1)} %get-tuple-element.19.inv_ref), channel_id=1, source_target_pairs={{8,16},{16,8},{24,32},{32,24},{40,48},{48,40},{56,64},{64,56},{72,... | collective-permute-start | bytes 12296 | tf_op jit(solution)/shard_map/ppermute | solution.py:363
  48.4 8.5 %collective-permute-start.1 = (f32[8,128]{1,0:T(8,128)S(1)}, f32[8,128]{1,0:T(8,128)S(1)}, u32[]{:S(2)}, u32[]{:S(2)}) collective-permute-start(f32[8,128]{1,0:T(8,128)S(1)} %get-tuple-element.19.inv_ref), channel_id=1, source_target_pairs={{0,8},{8,0},{16,24},{24,16},{32,40},{40,32},{48,56},{56,48},{64,72... | collective-permute-start | bytes 12296 | tf_op jit(solution)/shard_map/ppermute | solution.py:362
  59.9 0.7 copy-start.9
  60.6 0.7 copy-start.11
  63.7 23.4 %copy-start.10 = (bf16[2,256,128]{2,1,0:T(8,128)(2,1)S(1)}, bf16[2,256,128]{2,1,0:T(8,128)(2,1)}, u32[]{:S(2)}) copy-start(bf16[2,256,128]{2,1,0:T(8,128)(2,1)} %copy-done.9) | copy-start | bytes 393220
  63.7 23.4 %copy-start.12 = (bf16[3,256,128]{2,1,0:T(8,128)(2,1)S(1)}, bf16[3,256,128]{2,1,0:T(8,128)(2,1)}, u32[]{:S(2)}) copy-start(bf16[3,256,128]{2,1,0:T(8,128)(2,1)} %copy-done.11) | copy-start | bytes 589828
  63.7 24.2 %all-to-all-start.2 = ((bf16[64,3,8,128]{3,2,1,0:T(8,128)(2,1)}), bf16[64,3,8,128]{3,2,1,0:T(8,128)(2,1)S(1)}, u32[]{:S(2)}, u32[]{:S(2)}) async-start(bf16[64,3,8,128]{3,2,1,0:T(8,128)(2,1)} %temporal.1), calls=%async_computation.2 | async-start | bytes 786432 | tf_op jit(solution)/shard_map/all_to_all | solution.py:395
  70.8 7.2 %collective-permute-start.4 = (bf16[4,256,128]{2,1,0:T(8,128)(2,1)S(1)}, bf16[4,256,128]{2,1,0:T(8,128)(2,1)S(1)}, u32[]{:S(2)}, u32[]{:S(2)}) collective-permute-start(bf16[4,256,128]{2,1,0:T(8,128)(2,1)S(1)} %get-tuple-element.25), channel_id=1, source_target_pairs={{0,8},{8,0},{16,24},{24,16},{32,40},{40,32},{48,56},{56,48},{64,72... | collective-permute-start | bytes 786440 | tf_op jit(solution)/shard_map/ppermute | solution.py:392
  72.9 14.2 %collective-permute-start.5 = (bf16[4,256,128]{2,1,0:T(8,128)(2,1)S(1)}, bf16[4,256,128]{2,1,0:T(8,128)(2,1)S(1)}, u32[]{:S(2)}, u32[]{:S(2)}) collective-permute-start(bf16[4,256,128]{2,1,0:T(8,128)(2,1)S(1)} %get-tuple-element.26), channel_id=1, source_target_pairs={{8,16},{16,8},{24,32},{32,24},{40,48},{48,40},{56,64},{64,56},{72,... | collective-permute-start | bytes 786440 | tf_op jit(solution)/shard_map/ppermute | solution.py:393
  89.5 13.5 %all-to-all-start.3 = ((f32[8,8,128]{2,1,0:T(8,128)}), f32[8,8,128]{2,1,0:T(8,128)S(1)}, u32[]{:S(2)}, u32[]{:S(2)}) async-start(f32[8,8,128]{2,1,0:T(8,128)} %inner.1), calls=%async_computation.3 | async-start | bytes 65536 | tf_op jit(solution)/shard_map/all_to_all | solution.py:406

commit v3 on v2

--- a/solution.py
+++ b/solution.py
@@ -106,14 +106,13 @@
     return lax.rsqrt(jnp.sum(sums_ref[...], axis=0) / FULL + EPSILON)
 
 
-def squares_body(cls_ref, band_ref, q_hbm, k_hbm, v_hbm, out_ref, halo_ref, q_ref, k_ref, v_ref, sems):
+def squares_body(q_hbm, k_hbm, out_ref, q_ref, k_ref, sems):
     copies = [
         pltpu.make_async_copy(source, target, sems.at[i])
-        for i, (source, target) in enumerate(((q_hbm, q_ref), (k_hbm, k_ref), (v_hbm, v_ref)))
+        for i, (source, target) in enumerate(((q_hbm, q_ref), (k_hbm, k_ref)))
     ]
     for copy in copies:
         copy.start()
-    slots, _ = head_slots(cls_ref, band_ref)
     sums = []
     for copy, ref in zip(copies, (q_ref, k_ref)):
         copy.wait()
@@ -123,13 +122,16 @@
             total += wide * wide
         sums.append(lane_sums(total))
     out_ref[...] = jnp.broadcast_to(rows_of(*sums)[None], (8, 8, HD))
-    copies[2].wait()
+
+
+def halo_body(cls_ref, band_ref, after_ref, q_ref, k_ref, v_ref, g_ref, halo_ref):
+    slots, _ = head_slots(cls_ref, band_ref)
     for s in (1, 2):
         halo_ref[2 * s - 2] = k_ref[:, columns(slots[s])]
         halo_ref[2 * s - 1] = v_ref[:, columns(slots[s])]
 
 
-def gains_body(q_ref, k_ref, after_ref, g_ref, out_ref):
+def gains_body(q_ref, k_ref, after_ref, out_ref):
     out_ref[0] = q_ref[...].astype(F32)
     out_ref[1] = k_ref[...].astype(F32)
 
@@ -198,9 +200,7 @@
     own_ref,
     to_near_ref,
     to_far_ref,
-    done_ref,
 ):
-    done_ref[...] = inv_ref[...]
     slots, bands = head_slots(cls_ref, band_ref)
     frame = frame_ref[0]
     inv = inv_ref[...]
@@ -233,7 +233,7 @@
         dq_ref[s] = d_q.astype(BF)
 
 
-def temporal_body(in_ref, after_ref, out_ref):
+def temporal_body(in_ref, out_ref):
     rows = FRAMES * 8
     q, k, v, g = (in_ref[:, a].reshape(rows, HD) for a in range(4))
     d_k = jnp.zeros((rows, HD), F32)
@@ -336,17 +336,20 @@
     chip = [(i, ((i - 1) ^ 1) + 1) for i in range(1, FRAMES - 1)]
     block = (4, TOK, HD)
 
-    sums, halo = pl.pallas_call(
+    sums = pl.pallas_call(
         squares_body,
-        out_shape=(shape((8, 8, HD), F32), shape(block, BF)),
-        in_specs=[SM, SM] + [ANY] * 3,
-        out_specs=(VM,) * 2,
-        scratch_shapes=[pltpu.VMEM((TOK, WIDTH), BF)] * 3 + [pltpu.SemaphoreType.DMA((3,))],
+        out_shape=shape((8, 8, HD), F32),
+        in_specs=[ANY] * 2,
+        out_specs=VM,
+        scratch_shapes=[pltpu.VMEM((TOK, WIDTH), BF)] * 2 + [pltpu.SemaphoreType.DMA((2,))],
         name="squares",
         compiler_params=pltpu.CompilerParams(vmem_limit_bytes=56 << 20),
-    )(head_class, head_band, query_pre, key_pre, value)
-    gains = call(gains_body, shape((2, HEADS_DEV, HD), F32), [VM, VM, ANY, VM], "gains", 1)(
-        gain_q.reshape(HEADS_DEV, HD), gain_k.reshape(HEADS_DEV, HD), sums, d_out
+    )(query_pre, key_pre)
+    halo = call(halo_body, shape(block, BF), [SM, SM, ANY] + [VM] * 4, "halo", 2)(
+        head_class, head_band, sums, query_pre, key_pre, value, d_out
+    )
+    gains = call(gains_body, shape((2, HEADS_DEV, HD), F32), [VM, VM, ANY], "gains", 8)(
+        gain_q.reshape(HEADS_DEV, HD), gain_k.reshape(HEADS_DEV, HD), sums
     )
     near = lax.ppermute(halo, "seq", core)
     far = lax.ppermute(halo, "seq", chip)
@@ -361,7 +364,7 @@
     held = lax.all_to_all(send, "seq", 0, 0, tiled=True)
     inv_near = lax.ppermute(inv, "seq", core)
     inv_far = lax.ppermute(inv, "seq", chip)
-    dq, fin, own, to_near, to_far, done = call(
+    dq, fin, own, to_near, to_far = call(
         spatial_body,
         (
             shape((3, TOK, HD), BF),
@@ -369,7 +372,6 @@
             shape(block, F32),
             shape(block, BF),
             shape(block, BF),
-            shape((8, HD), F32),
         ),
         [SM] * 3 + [VM] * 10,
         "spatial",
@@ -391,7 +393,7 @@
     )
     from_near = lax.ppermute(to_near, "seq", core)
     from_far = lax.ppermute(to_far, "seq", chip)
-    grads = call(temporal_body, shape((FRAMES, 3, 8, HD), BF), [VM, ANY], "temporal", 3)(held, done)
+    grads = call(temporal_body, shape((FRAMES, 3, 8, HD), BF), [VM], "temporal", 3)(held)
     back = lax.all_to_all(grads, "seq", 0, 0, tiled=True)
     grad, part = call(
         spatial_sums_body,

time: 105 us -> 108 us (1.029)
  the two profiles are of different devices: /device:TPU:24 before, /device:TPU:8 now
where the time goes in v3:
time: 108 us
  starting transfers between devices  59.8 us (55%)
  waiting for transfers between devices  29.7 us (28%)
  Pallas kernels  15.3 us (14%)
  local copies, waits for them, and re-layouts  1.99 us (2%)
    all_to_all x1, starting transfers between devices, per_device(): sums = lax.all_to_all(sums, 'head', 0, 0, tiled=True)  12.9 us
    all_to_all x1, starting transfers between devices, per_device(): held = lax.all_to_all(send, 'seq', 0, 0, tiled=True)  10.8 us
    all_to_all x1, starting transfers between devices, per_device(): inner = lax.all_to_all(inner, 'head', 0, 0, tiled=True)  9.6 us
    all_to_all x1, waiting for transfers between devices, per_device(): inner = lax.all_to_all(inner, 'head', 0, 0, tiled=True)  8.83 us
    all_to_all x1, waiting for transfers between devices, per_device(): held = lax.all_to_all(send, 'seq', 0, 0, tiled=True)  8.18 us
    ppermute x1, waiting for transfers between devices, per_device(): from_far = lax.ppermute(to_far, 'seq', chip)  6.44 us
    all_to_all x1, starting transfers between devices, per_device(): back = lax.all_to_all(grads, 'seq', 0, 0, tiled=True)  5.97 us
    ppermute x1, starting transfers between devices, per_device(): from_far = lax.ppermute(to_far, 'seq', chip)  5.13 us
  transfers between devices with their start and end apart: 10, of which 5 were waited for; matrix products, arithmetic and copies ran while one was open for 0% of the time, Pallas kernels for 8%

profile of v3, /device:TPU:8, one launch (start us, length us, event | category | flops | bytes accessed | tf_op | source)
XLA Modules:
  0.0 107.7 jit_solution(9983896610054917394)
XLA Ops:
  0.6 2.4 %squares.1.after_ref = f32[8,8,128]{2,1,0:T(8,128)} custom-call(bf16[256,640]{1,0:T(8,128)(2,1)} %q_ref.11, bf16[256,640]{1,0:T(8,128)(2,1)} %k_ref.11), custom_call_target="tpu_custom_call" | custom-call | tf_op jit(solution)/shard_map/squares/pallas_call | solution.py:339
  3.1 12.9 %all-to-all-start = ((f32[8,8,128]{2,1,0:T(8,128)}), f32[8,8,128]{2,1,0:T(8,128)S(1)}, u32[]{:S(2)}, u32[]{:S(2)}) async-start(f32[8,8,128]{2,1,0:T(8,128)} %squares.1.after_ref), calls=%async_computation | async-start | bytes 65536 | tf_op jit(solution)/shard_map/all_to_all | solution.py:356
  16.0 1.0 copy-done.3
  17.0 1.0 copy-done.5
  18.6 4.2 %collective-permute-start = (bf16[4,256,128]{2,1,0:T(8,128)(2,1)S(1)}, bf16[4,256,128]{2,1,0:T(8,128)(2,1)S(1)}, u32[]{:S(2)}, u32[]{:S(2)}) collective-permute-start(bf16[4,256,128]{2,1,0:T(8,128)(2,1)S(1)} %halo.1), channel_id=1, source_target_pairs={{8,16},{16,8},{24,32},{32,24},{40,48},{48,40},{56,64},{64,56},{72,... | collective-permute-start | bytes 786440 | tf_op jit(solution)/shard_map/ppermute | solution.py:355
  22.9 3.2 %all-to-all-done.sums_ref = f32[8,8,128]{2,1,0:T(8,128)S(1)} async-done(((f32[8,8,128]{2,1,0:T(8,128)}), f32[8,8,128]{2,1,0:T(8,128)S(1)}, u32[]{:S(2)}, u32[]{:S(2)}) %all-to-all-start) | async-done | bytes 32800 | tf_op jit(solution)/shard_map/all_to_all | solution.py:356
  26.1 3.0 %collective-permute-done.after_ref.far_ref = bf16[4,256,128]{2,1,0:T(8,128)(2,1)S(1)} collective-permute-done((bf16[4,256,128]{2,1,0:T(8,128)(2,1)S(1)}, bf16[4,256,128]{2,1,0:T(8,128)(2,1)S(1)}, u32[]{:S(2)}, u32[]{:S(2)}) %collective-permute-start) | collective-permute-done | bytes 262176 | tf_op jit(solution)/shard_map/ppermute | solution.py:355
  29.1 1.5 %norm.1 = (bf16[64,4,8,128]{3,2,1,0:T(8,128)(2,1)}, f32[8,128]{1,0:T(8,128)S(1)}) custom-call(s32[5]{0:T(128)S(1)} %copy-done.9, s32[5]{0:T(128)S(1)} %copy-done.10, f32[8,8,128]{2,1,0:T(8,128)S(1)} %all-to-all-done.sums_ref, f32[2,5,128]{2,1,0:T(8,128)S(1)} %gains.1.gain_ref, bf16[256,640]{1,0:T(8,128)(2,1)S(1)} %copy-done, bf16[256,640]{1,0:T(8,128)(2,1)S(1)} %copy-done.1, ...), custom_call_target="tpu_custom_call" | custom-call | flops 2000000000 | bytes 2000000 | tf_op jit(solution)/shard_map/norm/pallas_call | solution.py:357
  30.7 10.8 %all-to-all-start.1 = ((bf16[64,4,8,128]{3,2,1,0:T(8,128)(2,1)}), bf16[64,4,8,128]{3,2,1,0:T(8,128)(2,1)S(1)}, u32[]{:S(2)}, u32[]{:S(2)}) async-start(bf16[64,4,8,128]{3,2,1,0:T(8,128)(2,1)} %get-tuple-element.15), calls=%async_computation.1 | async-start | bytes 1048576 | tf_op jit(solution)/shard_map/all_to_all | solution.py:364
  41.5 2.1 %collective-permute-start.3 = (bf16[4,256,128]{2,1,0:T(8,128)(2,1)S(1)}, bf16[4,256,128]{2,1,0:T(8,128)(2,1)S(1)}, u32[]{:S(2)}, u32[]{:S(2)}) collective-permute-start(bf16[4,256,128]{2,1,0:T(8,128)(2,1)S(1)} %halo.1), channel_id=1, source_target_pairs={{0,8},{8,0},{16,24},{24,16},{32,40},{40,32},{48,56},{56,48},{64,72... | collective-permute-start | bytes 786440 | tf_op jit(solution)/shard_map/ppermute | solution.py:354
  43.5 5.1 %collective-permute-start.2 = (f32[8,128]{1,0:T(8,128)S(1)}, f32[8,128]{1,0:T(8,128)S(1)}, u32[]{:S(2)}, u32[]{:S(2)}) collective-permute-start(f32[8,128]{1,0:T(8,128)S(1)} %get-tuple-element.14.inv_ref), channel_id=1, source_target_pairs={{8,16},{16,8},{24,32},{32,24},{40,48},{48,40},{56,64},{64,56},{72,... | collective-permute-start | bytes 12296 | tf_op jit(solution)/shard_map/ppermute | solution.py:366
  48.7 1.9 %collective-permute-start.1 = (f32[8,128]{1,0:T(8,128)S(1)}, f32[8,128]{1,0:T(8,128)S(1)}, u32[]{:S(2)}, u32[]{:S(2)}) collective-permute-start(f32[8,128]{1,0:T(8,128)S(1)} %get-tuple-element.14.inv_ref), channel_id=1, source_target_pairs={{0,8},{8,0},{16,24},{24,16},{32,40},{40,32},{48,56},{56,48},{64,72... | collective-permute-start | bytes 12296 | tf_op jit(solution)/shard_map/ppermute | solution.py:365
  50.6 8.2 %all-to-all-done.1.in_ref = bf16[64,4,8,128]{3,2,1,0:T(8,128)(2,1)S(1)} async-done(((bf16[64,4,8,128]{3,2,1,0:T(8,128)(2,1)}), bf16[64,4,8,128]{3,2,1,0:T(8,128)(2,1)S(1)}, u32[]{:S(2)}, u32[]{:S(2)}) %all-to-all-start.1) | async-done | bytes 524320 | tf_op jit(solution)/shard_map/all_to_all | solution.py:364
  58.8 2.5 %temporal.1 = bf16[64,3,8,128]{3,2,1,0:T(8,128)(2,1)} custom-call(bf16[64,4,8,128]{3,2,1,0:T(8,128)(2,1)S(1)} %all-to-all-done.1.in_ref), custom_call_target="tpu_custom_call" | custom-call | flops 3000000000 | bytes 3000000 | tf_op jit(solution)/shard_map/temporal/pallas_call | solution.py:396
  61.3 6.0 %all-to-all-start.2 = ((bf16[64,3,8,128]{3,2,1,0:T(8,128)(2,1)}), bf16[64,3,8,128]{3,2,1,0:T(8,128)(2,1)S(1)}, u32[]{:S(2)}, u32[]{:S(2)}) async-start(bf16[64,3,8,128]{3,2,1,0:T(8,128)(2,1)} %temporal.1), calls=%async_computation.2 | async-start | bytes 786432 | tf_op jit(solution)/shard_map/all_to_all | solution.py:397
  67.3 3.0 %spatial.1 = (bf16[3,256,128]{2,1,0:T(8,128)(2,1)S(1)}, bf16[2,256,128]{2,1,0:T(8,128)(2,1)S(1)}, f32[4,256,128]{2,1,0:T(8,128)S(1)}, bf16[4,256,128]{2,1,0:T(8,128)(2,1)S(1)}, bf16[4,256,128]{2,1,0:T(8,128)(2,1)S(1)}) custom-call(s32[5]{0:T(128)S(1)} %copy-done.9, s32[5]{0:T(128)S(1)} %copy-done.10, s32[1]{0:T(128)} %bitcast.2.frame_ref, ...), custom_call_target="tpu_custom_call" | custom-call | flops 4000000000 | bytes 4000000 | tf_op jit(solution)/shard_map/spatial/pallas_call | solution.py:367
  70.3 2.1 %collective-permute-start.4 = (bf16[4,256,128]{2,1,0:T(8,128)(2,1)S(1)}, bf16[4,256,128]{2,1,0:T(8,128)(2,1)S(1)}, u32[]{:S(2)}, u32[]{:S(2)}) collective-permute-start(bf16[4,256,128]{2,1,0:T(8,128)(2,1)S(1)} %get-tuple-element.19), channel_id=1, source_target_pairs={{0,8},{8,0},{16,24},{24,16},{32,40},{40,32},{48,56},{56,48},{64,72... | collective-permute-start | bytes 786440 | tf_op jit(solution)/shard_map/ppermute | solution.py:394
  72.3 5.1 %collective-permute-start.5 = (bf16[4,256,128]{2,1,0:T(8,128)(2,1)S(1)}, bf16[4,256,128]{2,1,0:T(8,128)(2,1)S(1)}, u32[]{:S(2)}, u32[]{:S(2)}) collective-permute-start(bf16[4,256,128]{2,1,0:T(8,128)(2,1)S(1)} %get-tuple-element.20), channel_id=1, source_target_pairs={{8,16},{16,8},{24,32},{32,24},{40,48},{48,40},{56,64},{64,56},{72,... | collective-permute-start | bytes 786440 | tf_op jit(solution)/shard_map/ppermute | solution.py:395
  77.5 6.4 %collective-permute-done.5.far_ref = bf16[4,256,128]{2,1,0:T(8,128)(2,1)S(1)} collective-permute-done((bf16[4,256,128]{2,1,0:T(8,128)(2,1)S(1)}, bf16[4,256,128]{2,1,0:T(8,128)(2,1)S(1)}, u32[]{:S(2)}, u32[]{:S(2)}) %collective-permute-start.5) | collective-permute-done | bytes 262176 | tf_op jit(solution)/shard_map/ppermute | solution.py:395
  84.7 1.6 %inner.1 = f32[8,8,128]{2,1,0:T(8,128)} custom-call(s32[5]{0:T(128)S(1)} %copy-done.9, s32[5]{0:T(128)S(1)} %copy-done.10, f32[2,5,128]{2,1,0:T(8,128)S(1)} %gains.1.gain_ref, bf16[256,640]{1,0:T(8,128)(2,1)S(1)} %copy-done, bf16[256,640]{1,0:T(8,128)(2,1)S(1)} %copy-done.1, bf16[64,3,8,128]{3,2,1,0:T(8,128)(2,1)S(1)} %all-to-all-done.2.back_ref, ...), custom_call_target="tpu_custom_call" | custom-call | flops 2000000000 | bytes 2000000 | tf_op jit(solution)/shard_map/inner/pallas_call | solution.py:405
  86.3 9.6 %all-to-all-start.3 = ((f32[8,8,128]{2,1,0:T(8,128)}), f32[8,8,128]{2,1,0:T(8,128)S(1)}, u32[]{:S(2)}, u32[]{:S(2)}) async-start(f32[8,8,128]{2,1,0:T(8,128)} %inner.1), calls=%async_computation.3 | async-start | bytes 65536 | tf_op jit(solution)/shard_map/all_to_all | solution.py:408
  95.9 1.3 %value.1 = bf16[256,640]{1,0:T(8,128)(2,1)} custom-call(s32[5]{0:T(128)S(1)} %copy-done.9, s32[5]{0:T(128)S(1)} %copy-done.10, bf16[64,3,8,128]{3,2,1,0:T(8,128)(2,1)S(1)} %all-to-all-done.2.back_ref, bf16[2,256,128]{2,1,0:T(8,128)(2,1)S(1)} %get-tuple-element.17.fin_ref, bf16[4,256,128]{2,1,0:T(8,128)(2,1)S(1)} %get-tuple-element.22.grad_ref), custom_call_target="tpu_custom_call" | custom-call | flops 2000000000 | bytes 2000000 | tf_op jit(solution)/shard_map/value/pallas_call | solution.py:409
  97.2 8.8 %all-to-all-done.3.inner_ref = f32[8,8,128]{2,1,0:T(8,128)S(1)} async-done(((f32[8,8,128]{2,1,0:T(8,128)}), f32[8,8,128]{2,1,0:T(8,128)S(1)}, u32[]{:S(2)}, u32[]{:S(2)}) %all-to-all-start.3) | async-done | bytes 32800 | tf_op jit(solution)/shard_map/all_to_all | solution.py:408
  106.1 1.7 %final.1 = (bf16[256,640]{1,0:T(8,128)(2,1)}, bf16[256,640]{1,0:T(8,128)(2,1)}) custom-call(s32[5]{0:T(128)S(1)} %copy-done.9, s32[5]{0:T(128)S(1)} %copy-done.10, f32[2,5,128]{2,1,0:T(8,128)S(1)} %gains.1.gain_ref, f32[8,128]{1,0:T(8,128)S(1)} %get-tuple-element.14.inv_ref, f32[8,8,128]{2,1,0:T(8,128)S(1)} %all-to-all-done.3.inner_ref, ...), custom_call_target="tpu_custom_call" | custom-call | flops 3000000000 | bytes 3000000 | tf_op jit(solution)/shard_map/final/pallas_call | solution.py:412
  (28 shorter events, 1.5 us)
Async XLA Ops:
  0.6 15.3 %copy-start.1 = (bf16[256,640]{1,0:T(8,128)(2,1)S(1)}, bf16[256,640]{1,0:T(8,128)(2,1)}, u32[]{:S(2)}) copy-start(bf16[256,640]{1,0:T(8,128)(2,1)} %k_ref.11) | copy-start | bytes 983044
  0.6 15.3 %copy-start = (bf16[256,640]{1,0:T(8,128)(2,1)S(1)}, bf16[256,640]{1,0:T(8,128)(2,1)}, u32[]{:S(2)}) copy-start(bf16[256,640]{1,0:T(8,128)(2,1)} %q_ref.11) | copy-start | bytes 983044
  3.0 12.9 %copy-start.2 = (f32[8,8,128]{2,1,0:T(8,128)S(1)}, f32[8,8,128]{2,1,0:T(8,128)}, u32[]{:S(2)}) copy-start(f32[8,8,128]{2,1,0:T(8,128)} %squares.1.after_ref) | copy-start | bytes 98308
  3.1 12.9 %copy-start.9 = (s32[5]{0:T(128)S(1)}, s32[5]{0:T(128)}, u32[]{:S(2)}) copy-start(s32[5]{0:T(128)} %cls_ref.13) | copy-start | bytes 64
  3.1 12.9 %copy-start.10 = (s32[5]{0:T(128)S(1)}, s32[5]{0:T(128)}, u32[]{:S(2)}) copy-start(s32[5]{0:T(128)} %band_ref.13) | copy-start | bytes 64
  3.1 23.1 %all-to-all-start = ((f32[8,8,128]{2,1,0:T(8,128)}), f32[8,8,128]{2,1,0:T(8,128)S(1)}, u32[]{:S(2)}, u32[]{:S(2)}) async-start(f32[8,8,128]{2,1,0:T(8,128)} %squares.1.after_ref), calls=%async_computation | async-start | bytes 65536 | tf_op jit(solution)/shard_map/all_to_all | solution.py:356
  16.0 1.0 copy-start.3
  17.0 1.0 copy-start.5
  18.0 4.9 %copy-start.8 = (bf16[640]{0:T(1024)(128)(2,1)S(1)}, bf16[640]{0:T(1024)(128)(2,1)}, u32[]{:S(2)}) copy-start(bf16[640]{0:T(1024)(128)(2,1)} %param.13) | copy-start | bytes 3844
  18.6 4.3 %copy-start.7 = (bf16[640]{0:T(1024)(128)(2,1)S(1)}, bf16[640]{0:T(1024)(128)(2,1)}, u32[]{:S(2)}) copy-start(bf16[640]{0:T(1024)(128)(2,1)} %param.12) | copy-start | bytes 3844
  18.6 10.5 %collective-permute-start = (bf16[4,256,128]{2,1,0:T(8,128)(2,1)S(1)}, bf16[4,256,128]{2,1,0:T(8,128)(2,1)S(1)}, u32[]{:S(2)}, u32[]{:S(2)}) collective-permute-start(bf16[4,256,128]{2,1,0:T(8,128)(2,1)S(1)} %halo.1), channel_id=1, source_target_pairs={{8,16},{16,8},{24,32},{32,24},{40,48},{48,40},{56,64},{64,56},{72,... | collective-permute-start | bytes 786440 | tf_op jit(solution)/shard_map/ppermute | solution.py:355
  22.9 6.3 %copy-start.4 = (bf16[256,640]{1,0:T(8,128)(2,1)S(1)}, bf16[256,640]{1,0:T(8,128)(2,1)}, u32[]{:S(2)}) copy-start(bf16[256,640]{1,0:T(8,128)(2,1)} %v_ref.5) | copy-start | bytes 983044
  22.9 6.3 %copy-start.6 = (bf16[256,640]{1,0:T(8,128)(2,1)S(1)}, bf16[256,640]{1,0:T(8,128)(2,1)}, u32[]{:S(2)}) copy-start(bf16[256,640]{1,0:T(8,128)(2,1)} %g_ref.5) | copy-start | bytes 983044
  30.7 28.1 %all-to-all-start.1 = ((bf16[64,4,8,128]{3,2,1,0:T(8,128)(2,1)}), bf16[64,4,8,128]{3,2,1,0:T(8,128)(2,1)S(1)}, u32[]{:S(2)}, u32[]{:S(2)}) async-start(bf16[64,4,8,128]{3,2,1,0:T(8,128)(2,1)} %get-tuple-element.15), calls=%async_computation.1 | async-start | bytes 1048576 | tf_op jit(solution)/shard_map/all_to_all | solution.py:364
  41.5 25.8 %collective-permute-start.3 = (bf16[4,256,128]{2,1,0:T(8,128)(2,1)S(1)}, bf16[4,256,128]{2,1,0:T(8,128)(2,1)S(1)}, u32[]{:S(2)}, u32[]{:S(2)}) collective-permute-start(bf16[4,256,128]{2,1,0:T(8,128)(2,1)S(1)} %halo.1), channel_id=1, source_target_pairs={{0,8},{8,0},{16,24},{24,16},{32,40},{40,32},{48,56},{56,48},{64,72... | collective-permute-start | bytes 786440 | tf_op jit(solution)/shard_map/ppermute | solution.py:354
  43.5 23.7 %collective-permute-start.2 = (f32[8,128]{1,0:T(8,128)S(1)}, f32[8,128]{1,0:T(8,128)S(1)}, u32[]{:S(2)}, u32[]{:S(2)}) collective-permute-start(f32[8,128]{1,0:T(8,128)S(1)} %get-tuple-element.14.inv_ref), channel_id=1, source_target_pairs={{8,16},{16,8},{24,32},{32,24},{40,48},{48,40},{56,64},{64,56},{72,... | collective-permute-start | bytes 12296 | tf_op jit(solution)/shard_map/ppermute | solution.py:366
  48.7 18.6 %collective-permute-start.1 = (f32[8,128]{1,0:T(8,128)S(1)}, f32[8,128]{1,0:T(8,128)S(1)}, u32[]{:S(2)}, u32[]{:S(2)}) collective-permute-start(f32[8,128]{1,0:T(8,128)S(1)} %get-tuple-element.14.inv_ref), channel_id=1, source_target_pairs={{0,8},{8,0},{16,24},{24,16},{32,40},{40,32},{48,56},{56,48},{64,72... | collective-permute-start | bytes 12296 | tf_op jit(solution)/shard_map/ppermute | solution.py:365
  61.3 23.5 %all-to-all-start.2 = ((bf16[64,3,8,128]{3,2,1,0:T(8,128)(2,1)}), bf16[64,3,8,128]{3,2,1,0:T(8,128)(2,1)S(1)}, u32[]{:S(2)}, u32[]{:S(2)}) async-start(bf16[64,3,8,128]{3,2,1,0:T(8,128)(2,1)} %temporal.1), calls=%async_computation.2 | async-start | bytes 786432 | tf_op jit(solution)/shard_map/all_to_all | solution.py:397
  70.3 7.2 %collective-permute-start.4 = (bf16[4,256,128]{2,1,0:T(8,128)(2,1)S(1)}, bf16[4,256,128]{2,1,0:T(8,128)(2,1)S(1)}, u32[]{:S(2)}, u32[]{:S(2)}) collective-permute-start(bf16[4,256,128]{2,1,0:T(8,128)(2,1)S(1)} %get-tuple-element.19), channel_id=1, source_target_pairs={{0,8},{8,0},{16,24},{24,16},{32,40},{40,32},{48,56},{56,48},{64,72... | collective-permute-start | bytes 786440 | tf_op jit(solution)/shard_map/ppermute | solution.py:394
  72.3 11.6 %collective-permute-start.5 = (bf16[4,256,128]{2,1,0:T(8,128)(2,1)S(1)}, bf16[4,256,128]{2,1,0:T(8,128)(2,1)S(1)}, u32[]{:S(2)}, u32[]{:S(2)}) collective-permute-start(bf16[4,256,128]{2,1,0:T(8,128)(2,1)S(1)} %get-tuple-element.20), channel_id=1, source_target_pairs={{8,16},{16,8},{24,32},{32,24},{40,48},{48,40},{56,64},{64,56},{72,... | collective-permute-start | bytes 786440 | tf_op jit(solution)/shard_map/ppermute | solution.py:395
  86.3 19.8 %all-to-all-start.3 = ((f32[8,8,128]{2,1,0:T(8,128)}), f32[8,8,128]{2,1,0:T(8,128)S(1)}, u32[]{:S(2)}, u32[]{:S(2)}) async-start(f32[8,8,128]{2,1,0:T(8,128)} %inner.1), calls=%async_computation.3 | async-start | bytes 65536 | tf_op jit(solution)/shard_map/all_to_all | solution.py:408

commit v4 on v3

--- a/solution.py
+++ b/solution.py
@@ -127,8 +127,8 @@
 def halo_body(cls_ref, band_ref, after_ref, q_ref, k_ref, v_ref, g_ref, halo_ref):
     slots, _ = head_slots(cls_ref, band_ref)
     for s in (1, 2):
-        halo_ref[2 * s - 2] = k_ref[:, columns(slots[s])]
-        halo_ref[2 * s - 1] = v_ref[:, columns(slots[s])]
+        for a, ref in enumerate((k_ref, v_ref, q_ref, g_ref)):
+            halo_ref[4 * s - 4 + a] = ref[:, columns(slots[s])]
 
 
 def gains_body(q_ref, k_ref, after_ref, out_ref):
@@ -141,7 +141,7 @@
 
 
 def norm_body(
-    cls_ref, band_ref, sums_ref, gain_ref, q_ref, k_ref, v_ref, g_ref, after_ref, send_ref, inv_ref
+    cls_ref, band_ref, sums_ref, gain_ref, q_ref, k_ref, v_ref, g_ref, send_ref, inv_ref
 ):
     slots, _ = head_slots(cls_ref, band_ref)
     inv = inverses(sums_ref)
@@ -169,16 +169,31 @@
         jnp.maximum, [jnp.max(score, axis=0, keepdims=True) for score in scores]
     )
     powers = [jnp.exp2((score - largest) * (SCALE * LOG2E)) for score in scores]
-    totals = sum(jnp.sum(power, axis=0, keepdims=True) for power in powers)
-    inverse = 1.0 / totals
+    inverse = 1.0 / sum(jnp.sum(power, axis=0, keepdims=True) for power in powers)
     probs = [power * inverse for power in powers]
     d_probs = [dot_nt(value, g) for value in values]
     deltas = sum(jnp.sum(p * d, axis=0, keepdims=True) for p, d in zip(probs, d_probs))
     d_scores = [(p * (d - deltas)).astype(BF) for p, d in zip(probs, d_probs)]
     d_q = sum(dot_tn(d, key) for d, key in zip(d_scores, keys)) * SCALE
-    d_keys = [dot_nn(d, q) * SCALE for d in d_scores]
-    d_values = [dot_nn(p.astype(BF), g) for p in probs]
-    return d_q, d_keys, d_values
+    return d_q, d_scores, probs, (largest, inverse, deltas)
+
+
+def own_body(cls_ref, band_ref, gain_ref, inv_ref, q_ref, k_ref, v_ref, g_ref, out_ref):
+    slots, _ = head_slots(cls_ref, band_ref)
+    inv = inv_ref[...]
+    cols = columns(slots[0])
+    q = normed(q_ref[:, cols], spread(inv, 0), gain_ref[0, pl.ds(slots[0], 1), :])
+    k = normed(k_ref[:, cols], spread(inv, 2), gain_ref[1, pl.ds(slots[0], 1), :])
+    g = g_ref[:, cols]
+    d_q, d_scores, probs, _ = attend(q, g, [k], [v_ref[:, cols]], [None])
+    out_ref[0] = d_q.astype(BF)
+    out_ref[1] = (dot_nn(d_scores[0], q) * SCALE).astype(BF)
+    out_ref[2] = dot_nn(probs[0].astype(BF), g).astype(BF)
+
+
+def reach(bands, s, frame):
+    wide = bands[s - 1] > 0
+    return wide, wide & (frame > 0) & (frame < FRAMES - 1)
 
 
 def spatial_body(
@@ -196,44 +211,89 @@
     near_ref,
     far_ref,
     dq_ref,
-    fin_ref,
-    own_ref,
-    to_near_ref,
-    to_far_ref,
+    part_ref,
+    norm_ref,
+    stat_ref,
 ):
     slots, bands = head_slots(cls_ref, band_ref)
-    frame = frame_ref[0]
     inv = inv_ref[...]
     q_inv, k_inv = spread(inv, 0), spread(inv, 2)
     near_inv, far_inv = spread(inv_near_ref[...], 2), spread(inv_far_ref[...], 2)
-    for s in range(3):
+    stats = []
+    for s in (1, 2):
+        cols = columns(slots[s])
+        k_gain = gain_ref[1, pl.ds(slots[s], 1), :]
+        q = normed(q_ref[:, cols], q_inv, gain_ref[0, pl.ds(slots[s], 1), :])
+        k = normed(k_ref[:, cols], k_inv, k_gain)
+        g = g_ref[:, cols]
+        at = 4 * s - 4
+        near_ok, far_ok = reach(bands, s, frame_ref[0])
+        keys = [k, normed(near_ref[at], near_inv, k_gain), normed(far_ref[at], far_inv, k_gain)]
+        values = [v_ref[:, cols], near_ref[at + 1], far_ref[at + 1]]
+        d_q, d_scores, probs, stat = attend(q, g, keys, values, [None, near_ok, far_ok])
+        dq_ref[s - 1] = d_q.astype(BF)
+        norm_ref[s - 1] = k
+        part_ref[2 * s - 2] = dot_nn(d_scores[0], q)
+        part_ref[2 * s - 1] = dot_nn(probs[0].astype(BF), g)
+        stats.extend(stat)
+    stat_ref[...] = jnp.concatenate(stats + stats[:2], axis=0)
+
+
+def product(gain_ref, which, slot, grad, ref):
+    gain = gain_ref[which, pl.ds(slot, 1), :]
+    return gain * grad.astype(F32) * ref[:, columns(slot)].astype(F32)
+
+
+def beside_body(
+    cls_ref,
+    band_ref,
+    frame_ref,
+    gain_ref,
+    inv_near_ref,
+    inv_far_ref,
+    stat_near_ref,
+    stat_far_ref,
+    near_ref,
+    far_ref,
+    q_ref,
+    k_ref,
+    v_ref,
+    norm_ref,
+    own_ref,
+    dq_ref,
+    part_ref,
+    grad_ref,
+    sum_ref,
+):
+    slots, bands = head_slots(cls_ref, band_ref)
+    q_invs = spread(inv_near_ref[...], 0), spread(inv_far_ref[...], 0)
+    q_total = product(gain_ref, 0, slots[0], own_ref[0], q_ref)
+    k_total = product(gain_ref, 1, slots[0], own_ref[1], k_ref)
+    for s in (1, 2):
         slot = slots[s]
-        cols = columns(slot)
-        k_gain = gain_ref[1, pl.ds(slot, 1), :]
-        q = normed(q_ref[:, cols], q_inv, gain_ref[0, pl.ds(slot, 1), :])
-        k = normed(k_ref[:, cols], k_inv, k_gain)
-        v, g = v_ref[:, cols], g_ref[:, cols]
-        if s == 0:
-            d_q, d_k, d_v = attend(q, g, [k], [v], [None])
-            fin_ref[0] = d_k[0].astype(BF)
-            fin_ref[1] = d_v[0].astype(BF)
-        else:
-            at = 2 * s - 2
-            wide = bands[s - 1] > 0
-            keys = [normed(near_ref[at], near_inv, k_gain), k, normed(far_ref[at], far_inv, k_gain)]
-            values = [near_ref[at + 1], v, far_ref[at + 1]]
-            allowed = [wide, None, wide & (frame > 0) & (frame < FRAMES - 1)]
-            d_q, d_k, d_v = attend(q, g, keys, values, allowed)
-            to_near_ref[at] = d_k[0].astype(BF)
-            to_near_ref[at + 1] = d_v[0].astype(BF)
-            own_ref[at] = d_k[1]
-            own_ref[at + 1] = d_v[1]
-            to_far_ref[at] = d_k[2].astype(BF)
-            to_far_ref[at + 1] = d_v[2].astype(BF)
-        dq_ref[s] = d_q.astype(BF)
-
-
-def temporal_body(in_ref, out_ref):
+        q_gain = gain_ref[0, pl.ds(slot, 1), :]
+        k, v = norm_ref[s - 1], v_ref[:, columns(slot)]
+        d_k, d_v = part_ref[2 * s - 2], part_ref[2 * s - 1]
+        at, row = 4 * s - 4, 3 * s - 3
+        sides = zip((near_ref, far_ref), (stat_near_ref, stat_far_ref), q_invs, reach(bands, s, frame_ref[0]))
+        for ref, stat, q_inv, ok in sides:
+            q, g = normed(ref[at + 2], q_inv, q_gain), ref[at + 3]
+            largest, inverse, delta = (stat[row + i : row + i + 1, :] for i in range(3))
+            score = jnp.where(ok, dot_nt(k, q), NEG)
+            prob = jnp.exp2((score - largest) * (SCALE * LOG2E)) * inverse
+            d_score = (prob * (dot_nt(v, g) - delta)).astype(BF)
+            d_k += dot_nn(d_score, q)
+            d_v += dot_nn(prob.astype(BF), g)
+        d_k = (d_k * SCALE).astype(BF)
+        grad_ref[2 * s - 2] = d_k
+        grad_ref[2 * s - 1] = d_v.astype(BF)
+        q_total += product(gain_ref, 0, slot, dq_ref[s - 1], q_ref)
+        k_total += product(gain_ref, 1, slot, d_k, k_ref)
+    sum_ref[0] = q_total
+    sum_ref[1] = k_total
+
+
+def temporal_body(in_ref, after_ref, out_ref):
     rows = FRAMES * 8
     q, k, v, g = (in_ref[:, a].reshape(rows, HD) for a in range(4))
     d_k = jnp.zeros((rows, HD), F32)
@@ -243,36 +303,13 @@
         q_part, g_part = q[part * step : (part + 1) * step], g[part * step : (part + 1) * step]
         key_tile = lax.broadcasted_iota(jnp.int32, (rows, step), 0) & 4
         query_tile = lax.broadcasted_iota(jnp.int32, (rows, step), 1) & 4
-        d_q, d_keys, d_values = attend(q_part, g_part, [k], [v], [key_tile == query_tile])
+        d_q, d_scores, probs, _ = attend(q_part, g_part, [k], [v], [key_tile == query_tile])
         frames = step // 8
         out_ref[part * frames : (part + 1) * frames, 0] = d_q.astype(BF).reshape(frames, 8, HD)
-        d_k += d_keys[0]
-        d_v += d_values[0]
-    out_ref[:, 1] = d_k.astype(BF).reshape(FRAMES, 8, HD)
+        d_k += dot_nn(d_scores[0], q_part)
+        d_v += dot_nn(probs[0].astype(BF), g_part)
+    out_ref[:, 1] = (d_k * SCALE).astype(BF).reshape(FRAMES, 8, HD)
     out_ref[:, 2] = d_v.astype(BF).reshape(FRAMES, 8, HD)
-
-
-def product(gain_ref, which, slot, grad, ref):
-    gain = gain_ref[which, pl.ds(slot, 1), :]
-    return gain * grad.astype(F32) * ref[:, columns(slot)].astype(F32)
-
-
-def spatial_sums_body(
-    cls_ref, band_ref, gain_ref, q_ref, k_ref, dq_ref, fin_ref, own_ref, near_ref, far_ref, grad_ref, part_ref
-):
-    slots, _ = head_slots(cls_ref, band_ref)
-    q_total = product(gain_ref, 0, slots[0], dq_ref[0], q_ref)
-    k_total = product(gain_ref, 1, slots[0], fin_ref[0], k_ref)
-    for s in (1, 2):
-        for b in range(2):
-            at = 2 * s - 2 + b
-            grad_ref[at] = (
-                own_ref[at] + near_ref[at].astype(F32) + far_ref[at].astype(F32)
-            ).astype(BF)
-        q_total += product(gain_ref, 0, slots[s], dq_ref[s], q_ref)
-        k_total += product(gain_ref, 1, slots[s], grad_ref[2 * s - 2], k_ref)
-    part_ref[0] = q_total
-    part_ref[1] = k_total
 
 
 def inner_body(cls_ref, band_ref, gain_ref, q_ref, k_ref, back_ref, part_ref, out_ref):
@@ -287,9 +324,9 @@
     out_ref[...] = jnp.broadcast_to(rows_of(*sums)[None], (8, 8, HD))
 
 
-def value_body(cls_ref, band_ref, back_ref, fin_ref, grad_ref, out_ref):
-    slots, _ = head_slots(cls_ref, band_ref)
-    out_ref[:, columns(slots[0])] = fin_ref[1]
+def value_body(cls_ref, band_ref, back_ref, own_ref, grad_ref, out_ref):
+    slots, _ = head_slots(cls_ref, band_ref)
+    out_ref[:, columns(slots[0])] = own_ref[2]
     for s in (1, 2):
         out_ref[:, columns(slots[s])] = grad_ref[2 * s - 1]
     for s in range(2):
@@ -305,8 +342,8 @@
     q_ref,
     k_ref,
     back_ref,
+    own_ref,
     dq_ref,
-    fin_ref,
     grad_ref,
     out_q_ref,
     out_k_ref,
@@ -319,10 +356,10 @@
         for s in range(HEADS_DEV):
             if s >= 3:
                 grad = back_ref[(s - 3) * 32 : (s - 2) * 32, which].reshape(TOK, HD)
-            elif which == 0:
-                grad = dq_ref[s]
+            elif s == 0:
+                grad = own_ref[which]
             else:
-                grad = fin_ref[0] if s == 0 else grad_ref[2 * s - 2]
+                grad = dq_ref[s - 1] if which == 0 else grad_ref[2 * s - 2]
             gain = gain_ref[which, pl.ds(slots[s], 1), :]
             at = columns(slots[s])
             out[:, at] = (
@@ -334,7 +371,6 @@
     frame = lax.axis_index("seq").astype(jnp.int32).reshape(1)
     core = [(i, i ^ 1) for i in range(FRAMES)]
     chip = [(i, ((i - 1) ^ 1) + 1) for i in range(1, FRAMES - 1)]
-    block = (4, TOK, HD)
 
     sums = pl.pallas_call(
         squares_body,
@@ -345,7 +381,7 @@
         name="squares",
         compiler_params=pltpu.CompilerParams(vmem_limit_bytes=56 << 20),
     )(query_pre, key_pre)
-    halo = call(halo_body, shape(block, BF), [SM, SM, ANY] + [VM] * 4, "halo", 2)(
+    halo = call(halo_body, shape((8, TOK, HD), BF), [SM, SM, ANY] + [VM] * 4, "halo", 2)(
         head_class, head_band, sums, query_pre, key_pre, value, d_out
     )
     gains = call(gains_body, shape((2, HEADS_DEV, HD), F32), [VM, VM, ANY], "gains", 8)(
@@ -357,25 +393,27 @@
     send, inv = call(
         norm_body,
         (shape((FRAMES, 4, 8, HD), BF), shape((8, HD), F32)),
-        [SM, SM] + [VM] * 6 + [ANY],
+        [SM, SM] + [VM] * 6,
         "norm",
         2,
-    )(head_class, head_band, sums, gains, query_pre, key_pre, value, d_out, far)
+    )(head_class, head_band, sums, gains, query_pre, key_pre, value, d_out)
     held = lax.all_to_all(send, "seq", 0, 0, tiled=True)
     inv_near = lax.ppermute(inv, "seq", core)
     inv_far = lax.ppermute(inv, "seq", chip)
-    dq, fin, own, to_near, to_far = call(
+    own = call(own_body, shape((3, TOK, HD), BF), [SM, SM] + [VM] * 6, "own", 2)(
+        head_class, head_band, gains, inv, query_pre, key_pre, value, d_out
+    )
+    dq, part, k_norm, stat = call(
         spatial_body,
         (
-            shape((3, TOK, HD), BF),
             shape((2, TOK, HD), BF),
-            shape(block, F32),
-            shape(block, BF),
-            shape(block, BF),
+            shape((4, TOK, HD), F32),
+            shape((2, TOK, HD), BF),
+            shape((8, TOK), F32),
         ),
         [SM] * 3 + [VM] * 10,
         "spatial",
-        4,
+        8,
     )(
         head_class,
         head_band,
@@ -391,27 +429,45 @@
         near,
         far,
     )
-    from_near = lax.ppermute(to_near, "seq", core)
-    from_far = lax.ppermute(to_far, "seq", chip)
-    grads = call(temporal_body, shape((FRAMES, 3, 8, HD), BF), [VM], "temporal", 3)(held)
+    grads = call(temporal_body, shape((FRAMES, 3, 8, HD), BF), [VM, ANY], "temporal", 3)(held, stat)
+    stat_near = lax.ppermute(stat, "seq", core)
+    stat_far = lax.ppermute(stat, "seq", chip)
     back = lax.all_to_all(grads, "seq", 0, 0, tiled=True)
     grad, part = call(
-        spatial_sums_body,
-        (shape(block, BF), shape((2, TOK, HD), F32)),
-        [SM, SM] + [VM] * 8,
-        "spatial_sums",
+        beside_body,
+        (shape((4, TOK, HD), BF), shape((2, TOK, HD), F32)),
+        [SM] * 3 + [VM] * 14,
+        "beside",
         3,
-    )(head_class, head_band, gains, query_pre, key_pre, dq, fin, own, from_near, from_far)
+    )(
+        head_class,
+        head_band,
+        frame,
+        gains,
+        inv_near,
+        inv_far,
+        stat_near,
+        stat_far,
+        near,
+        far,
+        query_pre,
+        key_pre,
+        value,
+        k_norm,
+        own,
+        dq,
+        part,
+    )
     inner = call(inner_body, shape((8, 8, HD), F32), [SM, SM] + [VM] * 5, "inner", 2)(
         head_class, head_band, gains, query_pre, key_pre, back, part
     )
     inner = lax.all_to_all(inner, "head", 0, 0, tiled=True)
     d_value = call(value_body, shape((TOK, WIDTH), BF), [SM, SM] + [VM] * 3, "value", 2)(
-        head_class, head_band, back, fin, grad
+        head_class, head_band, back, own, grad
     )
     d_query, d_key = call(
         final_body, (shape((TOK, WIDTH), BF),) * 2, [SM, SM] + [VM] * 9, "final", 3
-    )(head_class, head_band, gains, inv, inner, query_pre, key_pre, back, dq, fin, grad)
+    )(head_class, head_band, gains, inv, inner, query_pre, key_pre, back, own, dq, grad)
     return d_query, d_key, d_value
 
 

time: 108 us -> 104 us (0.963)
  the two profiles are of different devices: /device:TPU:8 before, /device:TPU:40 now
where the time goes in v4:
time: 104 us; the launch traced here: 103 us
  starting transfers between devices  60.7 us (58%)
  waiting for transfers between devices  20.4 us (20%)
  Pallas kernels  16.8 us (16%)
  local copies, waits for them, and re-layouts  4.15 us (4%)
    all_to_all x1, starting transfers between devices, per_device(): sums = lax.all_to_all(sums, 'head', 0, 0, tiled=True)  12.9 us
    all_to_all x1, starting transfers between devices, per_device(): held = lax.all_to_all(send, 'seq', 0, 0, tiled=True)  9.86 us
    all_to_all x1, waiting for transfers between devices, per_device(): inner = lax.all_to_all(inner, 'head', 0, 0, tiled=True)  8.81 us
    all_to_all x1, starting transfers between devices, per_device(): inner = lax.all_to_all(inner, 'head', 0, 0, tiled=True)  7.79 us
    ppermute x1, waiting for transfers between devices, per_device(): inv_far = lax.ppermute(inv, 'seq', chip)  7.51 us
    all_to_all x1, starting transfers between devices, per_device(): back = lax.all_to_all(grads, 'seq', 0, 0, tiled=True)  7.47 us
    ppermute x1, starting transfers between devices, per_device(): stat_far = lax.ppermute(stat, 'seq', chip)  5.94 us
    ppermute x1, starting transfers between devices, per_device(): inv_far = lax.ppermute(inv, 'seq', chip)  5.81 us
  transfers between devices with their start and end apart: 10, of which 4 were waited for; matrix products, arithmetic and copies ran while one was open for 0% of the time, Pallas kernels for 9%

profile of v4, /device:TPU:40, one launch (start us, length us, event | category | flops | bytes accessed | tf_op | source)
XLA Modules:
  0.0 103.0 jit_solution(12518075039234229564)
XLA Ops:
  0.6 2.4 %squares.1.after_ref = f32[8,8,128]{2,1,0:T(8,128)} custom-call(bf16[256,640]{1,0:T(8,128)(2,1)} %q_ref.13, bf16[256,640]{1,0:T(8,128)(2,1)} %k_ref.13), custom_call_target="tpu_custom_call" | custom-call | tf_op jit(solution)/shard_map/squares/pallas_call | solution.py:375
  3.1 12.9 %all-to-all-start = ((f32[8,8,128]{2,1,0:T(8,128)}), f32[8,8,128]{2,1,0:T(8,128)S(1)}, u32[]{:S(2)}, u32[]{:S(2)}) async-start(f32[8,8,128]{2,1,0:T(8,128)} %squares.1.after_ref), calls=%async_computation | async-start | bytes 65536 | tf_op jit(solution)/shard_map/all_to_all | solution.py:392
  16.0 1.0 copy-done.3
  17.0 1.0 copy-done.5
  18.6 5.1 %collective-permute-start.3 = (bf16[8,256,128]{2,1,0:T(8,128)(2,1)S(1)}, bf16[8,256,128]{2,1,0:T(8,128)(2,1)S(1)}, u32[]{:S(2)}, u32[]{:S(2)}) collective-permute-start(bf16[8,256,128]{2,1,0:T(8,128)(2,1)S(1)} %halo.1), channel_id=1, source_target_pairs={{8,16},{16,8},{24,32},{32,24},{40,48},{48,40},{56,64},{64,56},{72,... | collective-permute-start | bytes 1572872 | tf_op jit(solution)/shard_map/ppermute | solution.py:391
  23.8 1.9 %collective-permute-start.2 = (bf16[8,256,128]{2,1,0:T(8,128)(2,1)S(1)}, bf16[8,256,128]{2,1,0:T(8,128)(2,1)S(1)}, u32[]{:S(2)}, u32[]{:S(2)}) collective-permute-start(bf16[8,256,128]{2,1,0:T(8,128)(2,1)S(1)} %halo.1), channel_id=1, source_target_pairs={{0,8},{8,0},{16,24},{24,16},{32,40},{40,32},{48,56},{56,48},{64,72... | collective-permute-start | bytes 1572872 | tf_op jit(solution)/shard_map/ppermute | solution.py:390
  26.8 1.5 %norm.1 = (bf16[64,4,8,128]{3,2,1,0:T(8,128)(2,1)}, f32[8,128]{1,0:T(8,128)S(1)}) custom-call(s32[5]{0:T(128)S(1)} %copy-done.9, s32[5]{0:T(128)S(1)} %copy-done.10, f32[8,8,128]{2,1,0:T(8,128)S(1)} %all-to-all-done.sums_ref, f32[2,5,128]{2,1,0:T(8,128)S(1)} %gains.1.gain_ref, bf16[256,640]{1,0:T(8,128)(2,1)S(1)} %copy-done, bf16[256,640]{1,0:T(8,128)(2,1)S(1)} %copy-done.1, ...), custom_call_target="tpu_custom_call" | custom-call | flops 2000000000 | bytes 2000000 | tf_op jit(solution)/shard_map/norm/pallas_call | solution.py:393
  28.3 9.9 %all-to-all-start.1 = ((bf16[64,4,8,128]{3,2,1,0:T(8,128)(2,1)}), bf16[64,4,8,128]{3,2,1,0:T(8,128)(2,1)S(1)}, u32[]{:S(2)}, u32[]{:S(2)}) async-start(bf16[64,4,8,128]{3,2,1,0:T(8,128)(2,1)} %get-tuple-element.14), calls=%async_computation.1 | async-start | bytes 1048576 | tf_op jit(solution)/shard_map/all_to_all | solution.py:400
  38.2 5.8 %collective-permute-start.1 = (f32[8,128]{1,0:T(8,128)S(1)}, f32[8,128]{1,0:T(8,128)S(1)}, u32[]{:S(2)}, u32[]{:S(2)}) collective-permute-start(f32[8,128]{1,0:T(8,128)S(1)} %get-tuple-element.13.inv_ref), channel_id=1, source_target_pairs={{8,16},{16,8},{24,32},{32,24},{40,48},{48,40},{56,64},{64,56},{72,... | collective-permute-start | bytes 12296 | tf_op jit(solution)/shard_map/ppermute | solution.py:402
  44.0 1.9 %collective-permute-start = (f32[8,128]{1,0:T(8,128)S(1)}, f32[8,128]{1,0:T(8,128)S(1)}, u32[]{:S(2)}, u32[]{:S(2)}) collective-permute-start(f32[8,128]{1,0:T(8,128)S(1)} %get-tuple-element.13.inv_ref), channel_id=1, source_target_pairs={{0,8},{8,0},{16,24},{24,16},{32,40},{40,32},{48,56},{56,48},{64,72... | collective-permute-start | bytes 12296 | tf_op jit(solution)/shard_map/ppermute | solution.py:401
  46.0 7.5 %collective-permute-done.1.inv_far_ref = f32[8,128]{1,0:T(8,128)S(1)} collective-permute-done((f32[8,128]{1,0:T(8,128)S(1)}, f32[8,128]{1,0:T(8,128)S(1)}, u32[]{:S(2)}, u32[]{:S(2)}) %collective-permute-start.1) | collective-permute-done | bytes 4128 | tf_op jit(solution)/shard_map/ppermute | solution.py:402
  53.5 2.4 %spatial.1 = (bf16[2,256,128]{2,1,0:T(8,128)(2,1)S(1)}, f32[4,256,128]{2,1,0:T(8,128)S(1)}, bf16[2,256,128]{2,1,0:T(8,128)(2,1)S(1)}, f32[8,256]{1,0:T(8,128)S(1)}) custom-call(s32[5]{0:T(128)S(1)} %copy-done.9, s32[5]{0:T(128)S(1)} %copy-done.10, s32[1]{0:T(128)} %bitcast.2.frame_ref, f32[2,5,128]{2,1,0:T(8,128)S(1)} %gains.1.gain_ref, ...), custom_call_target="tpu_custom_call" | custom-call | flops 8000000000 | bytes 8000000 | tf_op jit(solution)/shard_map/spatial/pallas_call | solution.py:406
  56.7 2.4 %temporal.1 = bf16[64,3,8,128]{3,2,1,0:T(8,128)(2,1)} custom-call(bf16[64,4,8,128]{3,2,1,0:T(8,128)(2,1)S(1)} %all-to-all-done.1.in_ref, f32[8,256]{1,0:T(8,128)S(1)} %get-tuple-element.15.after_ref), custom_call_target="tpu_custom_call" | custom-call | flops 3000000000 | bytes 3000000 | tf_op jit(solution)/shard_map/temporal/pallas_call | solution.py:432
  59.0 7.5 %all-to-all-start.2 = ((bf16[64,3,8,128]{3,2,1,0:T(8,128)(2,1)}), bf16[64,3,8,128]{3,2,1,0:T(8,128)(2,1)S(1)}, u32[]{:S(2)}, u32[]{:S(2)}) async-start(bf16[64,3,8,128]{3,2,1,0:T(8,128)(2,1)} %temporal.1), calls=%async_computation.2 | async-start | bytes 786432 | tf_op jit(solution)/shard_map/all_to_all | solution.py:435
  66.5 5.9 %collective-permute-start.5 = (f32[8,256]{1,0:T(8,128)S(1)}, f32[8,256]{1,0:T(8,128)S(1)}, u32[]{:S(2)}, u32[]{:S(2)}) collective-permute-start(f32[8,256]{1,0:T(8,128)S(1)} %get-tuple-element.15.after_ref), channel_id=1, source_target_pairs={{8,16},{16,8},{24,32},{32,24},{40,48},{48,40},{56,64},{64,56},{72,... | collective-permute-start | bytes 24584 | tf_op jit(solution)/shard_map/ppermute | solution.py:434
  72.5 1.9 %collective-permute-start.4 = (f32[8,256]{1,0:T(8,128)S(1)}, f32[8,256]{1,0:T(8,128)S(1)}, u32[]{:S(2)}, u32[]{:S(2)}) collective-permute-start(f32[8,256]{1,0:T(8,128)S(1)} %get-tuple-element.15.after_ref), channel_id=1, source_target_pairs={{0,8},{8,0},{16,24},{24,16},{32,40},{40,32},{48,56},{56,48},{64,72... | collective-permute-start | bytes 24584 | tf_op jit(solution)/shard_map/ppermute | solution.py:433
  74.4 1.2 %own.1.own_ref = bf16[3,256,128]{2,1,0:T(8,128)(2,1)S(1)} custom-call(s32[5]{0:T(128)S(1)} %copy-done.9, s32[5]{0:T(128)S(1)} %copy-done.10, f32[2,5,128]{2,1,0:T(8,128)S(1)} %gains.1.gain_ref, f32[8,128]{1,0:T(8,128)S(1)} %get-tuple-element.13.inv_ref, bf16[256,640]{1,0:T(8,128)(2,1)S(1)} %copy-done, bf16[256,640]{1,0:T(8,128)(2,1)S(1)} %copy-done.1, ...), custom_call_target="tpu_custom_call" | custom-call | flops 2000000000 | bytes 2000000 | tf_op jit(solution)/shard_map/own/pallas_call | solution.py:403
  75.7 3.7 %collective-permute-done.5.stat_far_ref = f32[8,256]{1,0:T(8,128)S(1)} collective-permute-done((f32[8,256]{1,0:T(8,128)S(1)}, f32[8,256]{1,0:T(8,128)S(1)}, u32[]{:S(2)}, u32[]{:S(2)}) %collective-permute-start.5) | collective-permute-done | bytes 8224 | tf_op jit(solution)/shard_map/ppermute | solution.py:434
  79.4 1.7 %beside.1 = (bf16[4,256,128]{2,1,0:T(8,128)(2,1)S(1)}, f32[2,256,128]{2,1,0:T(8,128)S(1)}) custom-call(s32[5]{0:T(128)S(1)} %copy-done.9, s32[5]{0:T(128)S(1)} %copy-done.10, s32[1]{0:T(128)} %bitcast.2.frame_ref, f32[2,5,128]{2,1,0:T(8,128)S(1)} %gains.1.gain_ref, f32[8,128]{1,0:T(8,128)S(1)} %collective-permute-done.inv_near_ref, ...), custom_call_target="tpu_custom_call" | custom-call | flops 3000000000 | bytes 3000000 | tf_op jit(solution)/shard_map/beside/pallas_call | solution.py:436
  81.8 1.6 %inner.1 = f32[8,8,128]{2,1,0:T(8,128)} custom-call(s32[5]{0:T(128)S(1)} %copy-done.9, s32[5]{0:T(128)S(1)} %copy-done.10, f32[2,5,128]{2,1,0:T(8,128)S(1)} %gains.1.gain_ref, bf16[256,640]{1,0:T(8,128)(2,1)S(1)} %copy-done, bf16[256,640]{1,0:T(8,128)(2,1)S(1)} %copy-done.1, bf16[64,3,8,128]{3,2,1,0:T(8,128)(2,1)S(1)} %all-to-all-done.2.back_ref, ...), custom_call_target="tpu_custom_call" | custom-call | flops 2000000000 | bytes 2000000 | tf_op jit(solution)/shard_map/inner/pallas_call | solution.py:461
  83.3 7.8 %all-to-all-start.3 = ((f32[8,8,128]{2,1,0:T(8,128)}), f32[8,8,128]{2,1,0:T(8,128)S(1)}, u32[]{:S(2)}, u32[]{:S(2)}) async-start(f32[8,8,128]{2,1,0:T(8,128)} %inner.1), calls=%async_computation.3 | async-start | bytes 65536 | tf_op jit(solution)/shard_map/all_to_all | solution.py:464
  91.2 1.3 %value.1 = bf16[256,640]{1,0:T(8,128)(2,1)} custom-call(s32[5]{0:T(128)S(1)} %copy-done.9, s32[5]{0:T(128)S(1)} %copy-done.10, bf16[64,3,8,128]{3,2,1,0:T(8,128)(2,1)S(1)} %all-to-all-done.2.back_ref, bf16[3,256,128]{2,1,0:T(8,128)(2,1)S(1)} %copy-done.14, bf16[4,256,128]{2,1,0:T(8,128)(2,1)S(1)} %get-tuple-element.20.grad_ref), custom_call_target="tpu_custom_call" | custom-call | flops 2000000000 | bytes 2000000 | tf_op jit(solution)/shard_map/value/pallas_call | solution.py:465
  92.5 8.8 %all-to-all-done.3.inner_ref = f32[8,8,128]{2,1,0:T(8,128)S(1)} async-done(((f32[8,8,128]{2,1,0:T(8,128)}), f32[8,8,128]{2,1,0:T(8,128)S(1)}, u32[]{:S(2)}, u32[]{:S(2)}) %all-to-all-start.3) | async-done | bytes 32800 | tf_op jit(solution)/shard_map/all_to_all | solution.py:464
  101.3 1.7 %final.1 = (bf16[256,640]{1,0:T(8,128)(2,1)}, bf16[256,640]{1,0:T(8,128)(2,1)}) custom-call(s32[5]{0:T(128)S(1)} %copy-done.9, s32[5]{0:T(128)S(1)} %copy-done.10, f32[2,5,128]{2,1,0:T(8,128)S(1)} %gains.1.gain_ref, f32[8,128]{1,0:T(8,128)S(1)} %get-tuple-element.13.inv_ref, f32[8,8,128]{2,1,0:T(8,128)S(1)} %all-to-all-done.3.inner_ref, ...), custom_call_target="tpu_custom_call" | custom-call | flops 3000000000 | bytes 3000000 | tf_op jit(solution)/shard_map/final/pallas_call | solution.py:468
  (47 shorter events, 3.3 us)
Async XLA Ops:
  0.6 15.3 %copy-start.1 = (bf16[256,640]{1,0:T(8,128)(2,1)S(1)}, bf16[256,640]{1,0:T(8,128)(2,1)}, u32[]{:S(2)}) copy-start(bf16[256,640]{1,0:T(8,128)(2,1)} %k_ref.13) | copy-start | bytes 983044
  0.6 15.3 %copy-start = (bf16[256,640]{1,0:T(8,128)(2,1)S(1)}, bf16[256,640]{1,0:T(8,128)(2,1)}, u32[]{:S(2)}) copy-start(bf16[256,640]{1,0:T(8,128)(2,1)} %q_ref.13) | copy-start | bytes 983044
  3.0 12.9 %copy-start.2 = (f32[8,8,128]{2,1,0:T(8,128)S(1)}, f32[8,8,128]{2,1,0:T(8,128)}, u32[]{:S(2)}) copy-start(f32[8,8,128]{2,1,0:T(8,128)} %squares.1.after_ref) | copy-start | bytes 98308
  3.1 12.9 %copy-start.9 = (s32[5]{0:T(128)S(1)}, s32[5]{0:T(128)}, u32[]{:S(2)}) copy-start(s32[5]{0:T(128)} %cls_ref.15) | copy-start | bytes 64
  3.1 12.9 %copy-start.10 = (s32[5]{0:T(128)S(1)}, s32[5]{0:T(128)}, u32[]{:S(2)}) copy-start(s32[5]{0:T(128)} %band_ref.15) | copy-start | bytes 64
  3.1 23.1 %all-to-all-start = ((f32[8,8,128]{2,1,0:T(8,128)}), f32[8,8,128]{2,1,0:T(8,128)S(1)}, u32[]{:S(2)}, u32[]{:S(2)}) async-start(f32[8,8,128]{2,1,0:T(8,128)} %squares.1.after_ref), calls=%async_computation | async-start | bytes 65536 | tf_op jit(solution)/shard_map/all_to_all | solution.py:392
  18.0 7.8 %copy-start.8 = (bf16[640]{0:T(1024)(128)(2,1)S(1)}, bf16[640]{0:T(1024)(128)(2,1)}, u32[]{:S(2)}) copy-start(bf16[640]{0:T(1024)(128)(2,1)} %param.13) | copy-start | bytes 3844
  18.6 7.1 %copy-start.7 = (bf16[640]{0:T(1024)(128)(2,1)S(1)}, bf16[640]{0:T(1024)(128)(2,1)}, u32[]{:S(2)}) copy-start(bf16[640]{0:T(1024)(128)(2,1)} %param.12) | copy-start | bytes 3844
  18.6 34.8 %collective-permute-start.3 = (bf16[8,256,128]{2,1,0:T(8,128)(2,1)S(1)}, bf16[8,256,128]{2,1,0:T(8,128)(2,1)S(1)}, u32[]{:S(2)}, u32[]{:S(2)}) collective-permute-start(bf16[8,256,128]{2,1,0:T(8,128)(2,1)S(1)} %halo.1), channel_id=1, source_target_pairs={{8,16},{16,8},{24,32},{32,24},{40,48},{48,40},{56,64},{64,56},{72,... | collective-permute-start | bytes 1572872 | tf_op jit(solution)/shard_map/ppermute | solution.py:391
  23.8 29.7 %collective-permute-start.2 = (bf16[8,256,128]{2,1,0:T(8,128)(2,1)S(1)}, bf16[8,256,128]{2,1,0:T(8,128)(2,1)S(1)}, u32[]{:S(2)}, u32[]{:S(2)}) collective-permute-start(bf16[8,256,128]{2,1,0:T(8,128)(2,1)S(1)} %halo.1), channel_id=1, source_target_pairs={{0,8},{8,0},{16,24},{24,16},{32,40},{40,32},{48,56},{56,48},{64,72... | collective-permute-start | bytes 1572872 | tf_op jit(solution)/shard_map/ppermute | solution.py:390
  28.3 28.3 %all-to-all-start.1 = ((bf16[64,4,8,128]{3,2,1,0:T(8,128)(2,1)}), bf16[64,4,8,128]{3,2,1,0:T(8,128)(2,1)S(1)}, u32[]{:S(2)}, u32[]{:S(2)}) async-start(bf16[64,4,8,128]{3,2,1,0:T(8,128)(2,1)} %get-tuple-element.14), calls=%async_computation.1 | async-start | bytes 1048576 | tf_op jit(solution)/shard_map/all_to_all | solution.py:400
  38.2 15.3 %collective-permute-start.1 = (f32[8,128]{1,0:T(8,128)S(1)}, f32[8,128]{1,0:T(8,128)S(1)}, u32[]{:S(2)}, u32[]{:S(2)}) collective-permute-start(f32[8,128]{1,0:T(8,128)S(1)} %get-tuple-element.13.inv_ref), channel_id=1, source_target_pairs={{8,16},{16,8},{24,32},{32,24},{40,48},{48,40},{56,64},{64,56},{72,... | collective-permute-start | bytes 12296 | tf_op jit(solution)/shard_map/ppermute | solution.py:402
  44.0 9.4 %collective-permute-start = (f32[8,128]{1,0:T(8,128)S(1)}, f32[8,128]{1,0:T(8,128)S(1)}, u32[]{:S(2)}, u32[]{:S(2)}) collective-permute-start(f32[8,128]{1,0:T(8,128)S(1)} %get-tuple-element.13.inv_ref), channel_id=1, source_target_pairs={{0,8},{8,0},{16,24},{24,16},{32,40},{40,32},{48,56},{56,48},{64,72... | collective-permute-start | bytes 12296 | tf_op jit(solution)/shard_map/ppermute | solution.py:401
  56.7 2.4 %copy-start.15 = (bf16[2,256,128]{2,1,0:T(8,128)(2,1)}, bf16[2,256,128]{2,1,0:T(8,128)(2,1)S(1)}, u32[]{:S(2)}) copy-start(bf16[2,256,128]{2,1,0:T(8,128)(2,1)S(1)} %get-tuple-element.17.dq_ref) | copy-start | bytes 393220
  56.7 2.4 %copy-start.18 = (bf16[2,256,128]{2,1,0:T(8,128)(2,1)}, bf16[2,256,128]{2,1,0:T(8,128)(2,1)S(1)}, u32[]{:S(2)}) copy-start(bf16[2,256,128]{2,1,0:T(8,128)(2,1)S(1)} %get-tuple-element.16.norm_ref) | copy-start | bytes 393220
  59.0 22.7 %all-to-all-start.2 = ((bf16[64,3,8,128]{3,2,1,0:T(8,128)(2,1)}), bf16[64,3,8,128]{3,2,1,0:T(8,128)(2,1)S(1)}, u32[]{:S(2)}, u32[]{:S(2)}) async-start(bf16[64,3,8,128]{3,2,1,0:T(8,128)(2,1)} %temporal.1), calls=%async_computation.2 | async-start | bytes 786432 | tf_op jit(solution)/shard_map/all_to_all | solution.py:435
  66.5 12.9 %copy-start.12 = (f32[4,256,128]{2,1,0:T(8,128)S(1)}, f32[4,256,128]{2,1,0:T(8,128)}, u32[]{:S(2)}) copy-start(f32[4,256,128]{2,1,0:T(8,128)} %copy-done.11) | copy-start | bytes 1572868
  66.5 12.9 %copy-start.16 = (bf16[2,256,128]{2,1,0:T(8,128)(2,1)S(1)}, bf16[2,256,128]{2,1,0:T(8,128)(2,1)}, u32[]{:S(2)}) copy-start(bf16[2,256,128]{2,1,0:T(8,128)(2,1)} %copy-done.15) | copy-start | bytes 393220
  66.5 12.9 %copy-start.19 = (bf16[2,256,128]{2,1,0:T(8,128)(2,1)S(1)}, bf16[2,256,128]{2,1,0:T(8,128)(2,1)}, u32[]{:S(2)}) copy-start(bf16[2,256,128]{2,1,0:T(8,128)(2,1)} %copy-done.18) | copy-start | bytes 393220
  66.5 12.8 %collective-permute-start.5 = (f32[8,256]{1,0:T(8,128)S(1)}, f32[8,256]{1,0:T(8,128)S(1)}, u32[]{:S(2)}, u32[]{:S(2)}) collective-permute-start(f32[8,256]{1,0:T(8,128)S(1)} %get-tuple-element.15.after_ref), channel_id=1, source_target_pairs={{8,16},{16,8},{24,32},{32,24},{40,48},{48,40},{56,64},{64,56},{72,... | collective-permute-start | bytes 24584 | tf_op jit(solution)/shard_map/ppermute | solution.py:434
  72.5 6.9 %collective-permute-start.4 = (f32[8,256]{1,0:T(8,128)S(1)}, f32[8,256]{1,0:T(8,128)S(1)}, u32[]{:S(2)}, u32[]{:S(2)}) collective-permute-start(f32[8,256]{1,0:T(8,128)S(1)} %get-tuple-element.15.after_ref), channel_id=1, source_target_pairs={{0,8},{8,0},{16,24},{24,16},{32,40},{40,32},{48,56},{56,48},{64,72... | collective-permute-start | bytes 24584 | tf_op jit(solution)/shard_map/ppermute | solution.py:433
  81.8 9.4 %copy-start.14 = (bf16[3,256,128]{2,1,0:T(8,128)(2,1)S(1)}, bf16[3,256,128]{2,1,0:T(8,128)(2,1)}, u32[]{:S(2)}) copy-start(bf16[3,256,128]{2,1,0:T(8,128)(2,1)} %copy-done.13) | copy-start | bytes 589828
  83.3 18.0 %all-to-all-start.3 = ((f32[8,8,128]{2,1,0:T(8,128)}), f32[8,8,128]{2,1,0:T(8,128)S(1)}, u32[]{:S(2)}, u32[]{:S(2)}) async-start(f32[8,8,128]{2,1,0:T(8,128)} %inner.1), calls=%async_computation.3 | async-start | bytes 65536 | tf_op jit(solution)/shard_map/all_to_all | solution.py:464
  91.1 10.2 %copy-start.17 = (bf16[2,256,128]{2,1,0:T(8,128)(2,1)S(1)}, bf16[2,256,128]{2,1,0:T(8,128)(2,1)}, u32[]{:S(2)}) copy-start(bf16[2,256,128]{2,1,0:T(8,128)(2,1)} %copy-done.15) | copy-start | bytes 393220
  (6 other events, 5.5 us)

commit v5 on v3

--- a/solution.py
+++ b/solution.py
@@ -124,14 +124,7 @@
     out_ref[...] = jnp.broadcast_to(rows_of(*sums)[None], (8, 8, HD))
 
 
-def halo_body(cls_ref, band_ref, after_ref, q_ref, k_ref, v_ref, g_ref, halo_ref):
-    slots, _ = head_slots(cls_ref, band_ref)
-    for s in (1, 2):
-        halo_ref[2 * s - 2] = k_ref[:, columns(slots[s])]
-        halo_ref[2 * s - 1] = v_ref[:, columns(slots[s])]
-
-
-def gains_body(q_ref, k_ref, after_ref, out_ref):
+def gains_body(q_ref, k_ref, after_ref, g_ref, out_ref):
     out_ref[0] = q_ref[...].astype(F32)
     out_ref[1] = k_ref[...].astype(F32)
 
@@ -141,7 +134,7 @@
 
 
 def norm_body(
-    cls_ref, band_ref, sums_ref, gain_ref, q_ref, k_ref, v_ref, g_ref, after_ref, send_ref, inv_ref
+    cls_ref, band_ref, sums_ref, gain_ref, q_ref, k_ref, v_ref, g_ref, send_ref, halo_ref, inv_ref
 ):
     slots, _ = head_slots(cls_ref, band_ref)
     inv = inverses(sums_ref)
@@ -158,6 +151,10 @@
         )
         for a, part in enumerate(parts):
             send_ref[s * 32 : (s + 1) * 32, a] = part.reshape(32, 8, HD)
+    for s in (1, 2):
+        at = columns(slots[s])
+        halo_ref[2 * s - 2] = normed(k_ref[:, at], k_inv, gain_ref[1, pl.ds(slots[s], 1), :])
+        halo_ref[2 * s - 1] = v_ref[:, at]
 
 
 def attend(q, g, keys, values, allowed):
@@ -187,12 +184,11 @@
     frame_ref,
     gain_ref,
     inv_ref,
-    inv_near_ref,
-    inv_far_ref,
     q_ref,
     k_ref,
     v_ref,
     g_ref,
+    halo_ref,
     near_ref,
     far_ref,
     dq_ref,
@@ -204,24 +200,21 @@
     slots, bands = head_slots(cls_ref, band_ref)
     frame = frame_ref[0]
     inv = inv_ref[...]
-    q_inv, k_inv = spread(inv, 0), spread(inv, 2)
-    near_inv, far_inv = spread(inv_near_ref[...], 2), spread(inv_far_ref[...], 2)
+    q_inv = spread(inv, 0)
     for s in range(3):
-        slot = slots[s]
-        cols = columns(slot)
-        k_gain = gain_ref[1, pl.ds(slot, 1), :]
-        q = normed(q_ref[:, cols], q_inv, gain_ref[0, pl.ds(slot, 1), :])
-        k = normed(k_ref[:, cols], k_inv, k_gain)
-        v, g = v_ref[:, cols], g_ref[:, cols]
+        cols = columns(slots[s])
+        q = normed(q_ref[:, cols], q_inv, gain_ref[0, pl.ds(slots[s], 1), :])
+        g = g_ref[:, cols]
         if s == 0:
-            d_q, d_k, d_v = attend(q, g, [k], [v], [None])
+            k = normed(k_ref[:, cols], spread(inv, 2), gain_ref[1, pl.ds(slots[s], 1), :])
+            d_q, d_k, d_v = attend(q, g, [k], [v_ref[:, cols]], [None])
             fin_ref[0] = d_k[0].astype(BF)
             fin_ref[1] = d_v[0].astype(BF)
         else:
             at = 2 * s - 2
             wide = bands[s - 1] > 0
-            keys = [normed(near_ref[at], near_inv, k_gain), k, normed(far_ref[at], far_inv, k_gain)]
-            values = [near_ref[at + 1], v, far_ref[at + 1]]
+            keys = [near_ref[at], halo_ref[at], far_ref[at]]
+            values = [near_ref[at + 1], halo_ref[at + 1], far_ref[at + 1]]
             allowed = [wide, None, wide & (frame > 0) & (frame < FRAMES - 1)]
             d_q, d_k, d_v = attend(q, g, keys, values, allowed)
             to_near_ref[at] = d_k[0].astype(BF)
@@ -287,15 +280,6 @@
     out_ref[...] = jnp.broadcast_to(rows_of(*sums)[None], (8, 8, HD))
 
 
-def value_body(cls_ref, band_ref, back_ref, fin_ref, grad_ref, out_ref):
-    slots, _ = head_slots(cls_ref, band_ref)
-    out_ref[:, columns(slots[0])] = fin_ref[1]
-    for s in (1, 2):
-        out_ref[:, columns(slots[s])] = grad_ref[2 * s - 1]
-    for s in range(2):
-        out_ref[:, columns(slots[3 + s])] = back_ref[s * 32 : (s + 1) * 32, 2].reshape(TOK, HD)
-
-
 def final_body(
     cls_ref,
     band_ref,
@@ -310,6 +294,7 @@
     grad_ref,
     out_q_ref,
     out_k_ref,
+    out_v_ref,
 ):
     slots, _ = head_slots(cls_ref, band_ref)
     inv = inv_ref[...]
@@ -328,6 +313,11 @@
             out[:, at] = (
                 inverse * gain * grad.astype(F32) - ref[:, at].astype(F32) * pulled
             ).astype(BF)
+    out_v_ref[:, columns(slots[0])] = fin_ref[1]
+    for s in (1, 2):
+        out_v_ref[:, columns(slots[s])] = grad_ref[2 * s - 1]
+    for s in range(2):
+        out_v_ref[:, columns(slots[3 + s])] = back_ref[s * 32 : (s + 1) * 32, 2].reshape(TOK, HD)
 
 
 def per_device(query_pre, key_pre, value, d_out, gain_q, gain_k, head_class, head_band):
@@ -345,25 +335,20 @@
         name="squares",
         compiler_params=pltpu.CompilerParams(vmem_limit_bytes=56 << 20),
     )(query_pre, key_pre)
-    halo = call(halo_body, shape(block, BF), [SM, SM, ANY] + [VM] * 4, "halo", 2)(
-        head_class, head_band, sums, query_pre, key_pre, value, d_out
-    )
-    gains = call(gains_body, shape((2, HEADS_DEV, HD), F32), [VM, VM, ANY], "gains", 8)(
-        gain_q.reshape(HEADS_DEV, HD), gain_k.reshape(HEADS_DEV, HD), sums
-    )
+    gains = call(gains_body, shape((2, HEADS_DEV, HD), F32), [VM, VM, ANY, VM], "gains", 1)(
+        gain_q.reshape(HEADS_DEV, HD), gain_k.reshape(HEADS_DEV, HD), sums, d_out
+    )
+    sums = lax.all_to_all(sums, "head", 0, 0, tiled=True)
+    send, halo, inv = call(
+        norm_body,
+        (shape((FRAMES, 4, 8, HD), BF), shape(block, BF), shape((8, HD), F32)),
+        [SM, SM] + [VM] * 6,
+        "norm",
+        2,
+    )(head_class, head_band, sums, gains, query_pre, key_pre, value, d_out)
+    held = lax.all_to_all(send, "seq", 0, 0, tiled=True)
     near = lax.ppermute(halo, "seq", core)
     far = lax.ppermute(halo, "seq", chip)
-    sums = lax.all_to_all(sums, "head", 0, 0, tiled=True)
-    send, inv = call(
-        norm_body,
-        (shape((FRAMES, 4, 8, HD), BF), shape((8, HD), F32)),
-        [SM, SM] + [VM] * 6 + [ANY],
-        "norm",
-        2,
-    )(head_class, head_band, sums, gains, query_pre, key_pre, value, d_out, far)
-    held = lax.all_to_all(send, "seq", 0, 0, tiled=True)
-    inv_near = lax.ppermute(inv, "seq", core)
-    inv_far = lax.ppermute(inv, "seq", chip)
     dq, fin, own, to_near, to_far = call(
         spatial_body,
         (
@@ -373,26 +358,25 @@
             shape(block, BF),
             shape(block, BF),
         ),
-        [SM] * 3 + [VM] * 10,
+        [SM] * 3 + [VM] * 9,
         "spatial",
-        4,
+        6,
     )(
         head_class,
         head_band,
         frame,
         gains,
         inv,
-        inv_near,
-        inv_far,
         query_pre,
         key_pre,
         value,
         d_out,
+        halo,
         near,
         far,
     )
+    from_far = lax.ppermute(to_far, "seq", chip)
     from_near = lax.ppermute(to_near, "seq", core)
-    from_far = lax.ppermute(to_far, "seq", chip)
     grads = call(temporal_body, shape((FRAMES, 3, 8, HD), BF), [VM], "temporal", 3)(held)
     back = lax.all_to_all(grads, "seq", 0, 0, tiled=True)
     grad, part = call(
@@ -401,18 +385,18 @@
         [SM, SM] + [VM] * 8,
         "spatial_sums",
         3,
-    )(head_class, head_band, gains, query_pre, key_pre, dq, fin, own, from_near, from_far)
+    )(head_class, head_band, gains, query_pre, key_pre, dq, fin, own, from_far, from_near)
     inner = call(inner_body, shape((8, 8, HD), F32), [SM, SM] + [VM] * 5, "inner", 2)(
         head_class, head_band, gains, query_pre, key_pre, back, part
     )
     inner = lax.all_to_all(inner, "head", 0, 0, tiled=True)
-    d_value = call(value_body, shape((TOK, WIDTH), BF), [SM, SM] + [VM] * 3, "value", 2)(
-        head_class, head_band, back, fin, grad
-    )
-    d_query, d_key = call(
-        final_body, (shape((TOK, WIDTH), BF),) * 2, [SM, SM] + [VM] * 9, "final", 3
+    return call(
+        final_body,
+        (shape((TOK, WIDTH), BF),) * 3,
+        [SM, SM] + [VM] * 9,
+        "final",
+        3,
     )(head_class, head_band, gains, inv, inner, query_pre, key_pre, back, dq, fin, grad)
-    return d_query, d_key, d_value
 
 
 def solution(mesh):

time: 108 us -> 97.8 us (0.906)
  the two profiles are of different devices: /device:TPU:8 before, /device:TPU:25 now
where the time goes in v5:
time: 97.8 us; the launch traced here: 97.3 us
  starting transfers between devices  45.8 us (47%)
  waiting for transfers between devices  25.2 us (26%)
  Pallas kernels  12.9 us (13%)
  blocking collectives  11.8 us (12%)
    all_to_all x1, starting transfers between devices, per_device(): sums = lax.all_to_all(sums, 'head', 0, 0, tiled=True)  12.5 us
    all_to_all x1, starting transfers between devices, per_device(): held = lax.all_to_all(send, 'seq', 0, 0, tiled=True)  12.4 us
    all_to_all x1, blocking collectives, per_device(): inner = lax.all_to_all(inner, 'head', 0, 0, tiled=True)  11.8 us
    all_to_all x1, waiting for transfers between devices, per_device(): held = lax.all_to_all(send, 'seq', 0, 0, tiled=True)  10 us
    all_to_all x1, waiting for transfers between devices, per_device(): sums = lax.all_to_all(sums, 'head', 0, 0, tiled=True)  8.3 us
    ppermute x1, waiting for transfers between devices, per_device(): from_far = lax.ppermute(to_far, 'seq', chip)  6.87 us
    all_to_all x1, starting transfers between devices, per_device(): back = lax.all_to_all(grads, 'seq', 0, 0, tiled=True)  6.58 us
    ppermute x1, starting transfers between devices, per_device(): from_near = lax.ppermute(to_near, 'seq', core)  3.83 us
  transfers between devices with their start and end apart: 7, of which 3 were waited for; matrix products, arithmetic and copies ran while one was open for 0% of the time, Pallas kernels for 6%

profile of v5, /device:TPU:25, one launch (start us, length us, event | category | flops | bytes accessed | tf_op | source)
XLA Modules:
  0.0 97.3 jit_solution(15051460274789544228)
XLA Ops:
  0.6 2.4 %squares.1.after_ref = f32[8,8,128]{2,1,0:T(8,128)} custom-call(bf16[256,640]{1,0:T(8,128)(2,1)} %q_ref.9, bf16[256,640]{1,0:T(8,128)(2,1)} %k_ref.9), custom_call_target="tpu_custom_call" | custom-call | tf_op jit(solution)/shard_map/squares/pallas_call | solution.py:329
  3.0 0.0 copy-start.2
  3.0 0.0 copy-start.6
  3.0 12.5 %all-to-all-start = ((f32[8,8,128]{2,1,0:T(8,128)}), f32[8,8,128]{2,1,0:T(8,128)S(1)}, u32[]{:S(2)}, u32[]{:S(2)}) async-start(f32[8,8,128]{2,1,0:T(8,128)} %squares.1.after_ref), calls=%async_computation | async-start | bytes 65536 | tf_op jit(solution)/shard_map/all_to_all | solution.py:341
  15.6 0.6 copy-done.5
  16.2 0.0 copy-start.8
  16.2 8.3 %all-to-all-done.sums_ref = f32[8,8,128]{2,1,0:T(8,128)S(1)} async-done(((f32[8,8,128]{2,1,0:T(8,128)}), f32[8,8,128]{2,1,0:T(8,128)S(1)}, u32[]{:S(2)}, u32[]{:S(2)}) %all-to-all-start) | async-done | bytes 32800 | tf_op jit(solution)/shard_map/all_to_all | solution.py:341
  24.6 1.6 %norm.1 = (bf16[64,4,8,128]{3,2,1,0:T(8,128)(2,1)}, bf16[4,256,128]{2,1,0:T(8,128)(2,1)S(1)}, f32[8,128]{1,0:T(8,128)S(1)}) custom-call(s32[5]{0:T(128)S(1)} %copy-done.7, s32[5]{0:T(128)S(1)} %copy-done.8, f32[8,8,128]{2,1,0:T(8,128)S(1)} %all-to-all-done.sums_ref, f32[2,5,128]{2,1,0:T(8,128)S(1)} %gains.1.gain_ref, bf16[256,640]{1,0:T(8,128)(2,1)S(1)} %copy-done, ...), custom_call_target="tpu_custom_call" | custom-call | flops 2000000000 | bytes 2000000 | tf_op jit(solution)/shard_map/norm/pallas_call | solution.py:342
  26.2 12.4 %all-to-all-start.1 = ((bf16[64,4,8,128]{3,2,1,0:T(8,128)(2,1)}), bf16[64,4,8,128]{3,2,1,0:T(8,128)(2,1)S(1)}, u32[]{:S(2)}, u32[]{:S(2)}) async-start(bf16[64,4,8,128]{3,2,1,0:T(8,128)(2,1)} %get-tuple-element.14), calls=%async_computation.1 | async-start | bytes 1048576 | tf_op jit(solution)/shard_map/all_to_all | solution.py:349
  38.6 3.4 %collective-permute-start.1 = (bf16[4,256,128]{2,1,0:T(8,128)(2,1)S(1)}, bf16[4,256,128]{2,1,0:T(8,128)(2,1)S(1)}, u32[]{:S(2)}, u32[]{:S(2)}) collective-permute-start(bf16[4,256,128]{2,1,0:T(8,128)(2,1)S(1)} %get-tuple-element.15.halo_ref), channel_id=1, source_target_pairs={{8,16},{16,8},{24,32},{32,24},{40,48},{48,40},{56,64},{64,56},{72,... | collective-permute-start | bytes 786440 | tf_op jit(solution)/shard_map/ppermute | solution.py:351
  41.9 3.8 %collective-permute-start = (bf16[4,256,128]{2,1,0:T(8,128)(2,1)S(1)}, bf16[4,256,128]{2,1,0:T(8,128)(2,1)S(1)}, u32[]{:S(2)}, u32[]{:S(2)}) collective-permute-start(bf16[4,256,128]{2,1,0:T(8,128)(2,1)S(1)} %get-tuple-element.15.halo_ref), channel_id=1, source_target_pairs={{0,8},{8,0},{16,24},{24,16},{32,40},{40,32},{48,56},{56,48},{64,72... | collective-permute-start | bytes 786440 | tf_op jit(solution)/shard_map/ppermute | solution.py:350
  45.7 10.0 %all-to-all-done.1.in_ref = bf16[64,4,8,128]{3,2,1,0:T(8,128)(2,1)S(1)} async-done(((bf16[64,4,8,128]{3,2,1,0:T(8,128)(2,1)}), bf16[64,4,8,128]{3,2,1,0:T(8,128)(2,1)S(1)}, u32[]{:S(2)}, u32[]{:S(2)}) %all-to-all-start.1) | async-done | bytes 524320 | tf_op jit(solution)/shard_map/all_to_all | solution.py:349
  55.8 2.5 %temporal.1 = bf16[64,3,8,128]{3,2,1,0:T(8,128)(2,1)} custom-call(bf16[64,4,8,128]{3,2,1,0:T(8,128)(2,1)S(1)} %all-to-all-done.1.in_ref), custom_call_target="tpu_custom_call" | custom-call | flops 3000000000 | bytes 3000000 | tf_op jit(solution)/shard_map/temporal/pallas_call | solution.py:380
  58.2 6.6 %all-to-all-start.2 = ((bf16[64,3,8,128]{3,2,1,0:T(8,128)(2,1)}), bf16[64,3,8,128]{3,2,1,0:T(8,128)(2,1)S(1)}, u32[]{:S(2)}, u32[]{:S(2)}) async-start(bf16[64,3,8,128]{3,2,1,0:T(8,128)(2,1)} %temporal.1), calls=%async_computation.2 | async-start | bytes 786432 | tf_op jit(solution)/shard_map/all_to_all | solution.py:381
  64.8 0.0 collective-permute-done.near_ref
  64.8 3.0 %spatial.1 = (bf16[3,256,128]{2,1,0:T(8,128)(2,1)S(1)}, bf16[2,256,128]{2,1,0:T(8,128)(2,1)S(1)}, f32[4,256,128]{2,1,0:T(8,128)S(1)}, bf16[4,256,128]{2,1,0:T(8,128)(2,1)S(1)}, bf16[4,256,128]{2,1,0:T(8,128)(2,1)S(1)}) custom-call(s32[5]{0:T(128)S(1)} %copy-done.7, s32[5]{0:T(128)S(1)} %copy-done.8, s32[1]{0:T(128)} %bitcast.2.frame_ref, ...), custom_call_target="tpu_custom_call" | custom-call | flops 6000000000 | bytes 6000000 | tf_op jit(solution)/shard_map/spatial/pallas_call | solution.py:352
  67.8 3.3 %collective-permute-start.2 = (bf16[4,256,128]{2,1,0:T(8,128)(2,1)S(1)}, bf16[4,256,128]{2,1,0:T(8,128)(2,1)S(1)}, u32[]{:S(2)}, u32[]{:S(2)}) collective-permute-start(bf16[4,256,128]{2,1,0:T(8,128)(2,1)S(1)} %get-tuple-element.19), channel_id=1, source_target_pairs={{8,16},{16,8},{24,32},{32,24},{40,48},{48,40},{56,64},{64,56},{72,... | collective-permute-start | bytes 786440 | tf_op jit(solution)/shard_map/ppermute | solution.py:378
  71.2 3.8 %collective-permute-start.3 = (bf16[4,256,128]{2,1,0:T(8,128)(2,1)S(1)}, bf16[4,256,128]{2,1,0:T(8,128)(2,1)S(1)}, u32[]{:S(2)}, u32[]{:S(2)}) collective-permute-start(bf16[4,256,128]{2,1,0:T(8,128)(2,1)S(1)} %get-tuple-element.20), channel_id=1, source_target_pairs={{0,8},{8,0},{16,24},{24,16},{32,40},{40,32},{48,56},{56,48},{64,72... | collective-permute-start | bytes 786440 | tf_op jit(solution)/shard_map/ppermute | solution.py:379
  75.0 6.9 %collective-permute-done.2.near_ref = bf16[4,256,128]{2,1,0:T(8,128)(2,1)S(1)} collective-permute-done((bf16[4,256,128]{2,1,0:T(8,128)(2,1)S(1)}, bf16[4,256,128]{2,1,0:T(8,128)(2,1)S(1)}, u32[]{:S(2)}, u32[]{:S(2)}) %collective-permute-start.2) | collective-permute-done | bytes 262176 | tf_op jit(solution)/shard_map/ppermute | solution.py:378
  81.9 0.0 collective-permute-done.3.far_ref
  81.9 0.8 spatial_sums.1
  82.7 0.9 inner.1
  83.6 11.8 %all_to_all.20.inner_ref = f32[8,8,128]{2,1,0:T(8,128)S(1)} all-to-all(f32[8,8,128]{2,1,0:T(8,128)S(1)} %inner.1), channel_id=1, replica_groups=mesh['seq'=64,'head'=8] {'head'}, dimensions={0} | all-to-all | bytes 65536 | tf_op jit(solution)/shard_map/all_to_all | solution.py:392
  95.5 1.8 %final.1 = (bf16[256,640]{1,0:T(8,128)(2,1)}, bf16[256,640]{1,0:T(8,128)(2,1)}, bf16[256,640]{1,0:T(8,128)(2,1)}) custom-call(s32[5]{0:T(128)S(1)} %copy-done.7, s32[5]{0:T(128)S(1)} %copy-done.8, f32[2,5,128]{2,1,0:T(8,128)S(1)} %gains.1.gain_ref, f32[8,128]{1,0:T(8,128)S(1)} %get-tuple-element.13.inv_ref, f32[8,8,128]{2,1,0:T(8,128)S(1)} %all_to_all.20.inner_ref, ...), custom_call_target="tpu_custom_call" | custom-call | flops 3000000000 | bytes 3000000 | tf_op jit(solution)/shard_map/final/pallas_call | solution.py:393
  (17 shorter events, 0.0 us)
Async XLA Ops:
  0.6 14.9 %copy-start.3 = (bf16[256,640]{1,0:T(8,128)(2,1)S(1)}, bf16[256,640]{1,0:T(8,128)(2,1)}, u32[]{:S(2)}) copy-start(bf16[256,640]{1,0:T(8,128)(2,1)} %g_ref.5) | copy-start | bytes 983044
  3.0 12.5 %copy-start.2 = (f32[8,8,128]{2,1,0:T(8,128)S(1)}, f32[8,8,128]{2,1,0:T(8,128)}, u32[]{:S(2)}) copy-start(f32[8,8,128]{2,1,0:T(8,128)} %squares.1.after_ref) | copy-start | bytes 98308
  3.0 12.5 %copy-start.6 = (bf16[640]{0:T(1024)(128)(2,1)S(1)}, bf16[640]{0:T(1024)(128)(2,1)}, u32[]{:S(2)}) copy-start(bf16[640]{0:T(1024)(128)(2,1)} %param.13) | copy-start | bytes 3844
  3.0 21.5 %all-to-all-start = ((f32[8,8,128]{2,1,0:T(8,128)}), f32[8,8,128]{2,1,0:T(8,128)S(1)}, u32[]{:S(2)}, u32[]{:S(2)}) async-start(f32[8,8,128]{2,1,0:T(8,128)} %squares.1.after_ref), calls=%async_computation | async-start | bytes 65536 | tf_op jit(solution)/shard_map/all_to_all | solution.py:341
  15.5 0.7 copy-start.5
  16.2 8.3 %copy-start = (bf16[256,640]{1,0:T(8,128)(2,1)S(1)}, bf16[256,640]{1,0:T(8,128)(2,1)}, u32[]{:S(2)}) copy-start(bf16[256,640]{1,0:T(8,128)(2,1)} %q_ref.9) | copy-start | bytes 983044
  16.2 8.3 %copy-start.1 = (bf16[256,640]{1,0:T(8,128)(2,1)S(1)}, bf16[256,640]{1,0:T(8,128)(2,1)}, u32[]{:S(2)}) copy-start(bf16[256,640]{1,0:T(8,128)(2,1)} %k_ref.9) | copy-start | bytes 983044
  16.2 8.3 %copy-start.4 = (bf16[256,640]{1,0:T(8,128)(2,1)S(1)}, bf16[256,640]{1,0:T(8,128)(2,1)}, u32[]{:S(2)}) copy-start(bf16[256,640]{1,0:T(8,128)(2,1)} %v_ref.3) | copy-start | bytes 983044
  16.2 8.3 %copy-start.7 = (s32[5]{0:T(128)S(1)}, s32[5]{0:T(128)}, u32[]{:S(2)}) copy-start(s32[5]{0:T(128)} %cls_ref.9) | copy-start | bytes 64
  16.2 8.4 %copy-start.8 = (s32[5]{0:T(128)S(1)}, s32[5]{0:T(128)}, u32[]{:S(2)}) copy-start(s32[5]{0:T(128)} %band_ref.9) | copy-start | bytes 64
  26.2 29.6 %all-to-all-start.1 = ((bf16[64,4,8,128]{3,2,1,0:T(8,128)(2,1)}), bf16[64,4,8,128]{3,2,1,0:T(8,128)(2,1)S(1)}, u32[]{:S(2)}, u32[]{:S(2)}) async-start(bf16[64,4,8,128]{3,2,1,0:T(8,128)(2,1)} %get-tuple-element.14), calls=%async_computation.1 | async-start | bytes 1048576 | tf_op jit(solution)/shard_map/all_to_all | solution.py:349
  38.6 26.3 %collective-permute-start.1 = (bf16[4,256,128]{2,1,0:T(8,128)(2,1)S(1)}, bf16[4,256,128]{2,1,0:T(8,128)(2,1)S(1)}, u32[]{:S(2)}, u32[]{:S(2)}) collective-permute-start(bf16[4,256,128]{2,1,0:T(8,128)(2,1)S(1)} %get-tuple-element.15.halo_ref), channel_id=1, source_target_pairs={{8,16},{16,8},{24,32},{32,24},{40,48},{48,40},{56,64},{64,56},{72,... | collective-permute-start | bytes 786440 | tf_op jit(solution)/shard_map/ppermute | solution.py:351
  41.9 22.9 %collective-permute-start = (bf16[4,256,128]{2,1,0:T(8,128)(2,1)S(1)}, bf16[4,256,128]{2,1,0:T(8,128)(2,1)S(1)}, u32[]{:S(2)}, u32[]{:S(2)}) collective-permute-start(bf16[4,256,128]{2,1,0:T(8,128)(2,1)S(1)} %get-tuple-element.15.halo_ref), channel_id=1, source_target_pairs={{0,8},{8,0},{16,24},{24,16},{32,40},{40,32},{48,56},{56,48},{64,72... | collective-permute-start | bytes 786440 | tf_op jit(solution)/shard_map/ppermute | solution.py:350
  58.2 24.5 %all-to-all-start.2 = ((bf16[64,3,8,128]{3,2,1,0:T(8,128)(2,1)}), bf16[64,3,8,128]{3,2,1,0:T(8,128)(2,1)S(1)}, u32[]{:S(2)}, u32[]{:S(2)}) async-start(bf16[64,3,8,128]{3,2,1,0:T(8,128)(2,1)} %temporal.1), calls=%async_computation.2 | async-start | bytes 786432 | tf_op jit(solution)/shard_map/all_to_all | solution.py:381
  67.8 14.1 %collective-permute-start.2 = (bf16[4,256,128]{2,1,0:T(8,128)(2,1)S(1)}, bf16[4,256,128]{2,1,0:T(8,128)(2,1)S(1)}, u32[]{:S(2)}, u32[]{:S(2)}) collective-permute-start(bf16[4,256,128]{2,1,0:T(8,128)(2,1)S(1)} %get-tuple-element.19), channel_id=1, source_target_pairs={{8,16},{16,8},{24,32},{32,24},{40,48},{48,40},{56,64},{64,56},{72,... | collective-permute-start | bytes 786440 | tf_op jit(solution)/shard_map/ppermute | solution.py:378
  71.2 10.7 %collective-permute-start.3 = (bf16[4,256,128]{2,1,0:T(8,128)(2,1)S(1)}, bf16[4,256,128]{2,1,0:T(8,128)(2,1)S(1)}, u32[]{:S(2)}, u32[]{:S(2)}) collective-permute-start(bf16[4,256,128]{2,1,0:T(8,128)(2,1)S(1)} %get-tuple-element.20), channel_id=1, source_target_pairs={{0,8},{8,0},{16,24},{24,16},{32,40},{40,32},{48,56},{56,48},{64,72... | collective-permute-start | bytes 786440 | tf_op jit(solution)/shard_map/ppermute | solution.py:379

commit v6 on v5

--- a/solution.py
+++ b/solution.py
@@ -124,6 +124,13 @@
     out_ref[...] = jnp.broadcast_to(rows_of(*sums)[None], (8, 8, HD))
 
 
+def halo_body(cls_ref, band_ref, after_ref, k_ref, v_ref, halo_ref):
+    slots, _ = head_slots(cls_ref, band_ref)
+    for s in (1, 2):
+        halo_ref[2 * s - 2] = k_ref[:, columns(slots[s])]
+        halo_ref[2 * s - 1] = v_ref[:, columns(slots[s])]
+
+
 def gains_body(q_ref, k_ref, after_ref, g_ref, out_ref):
     out_ref[0] = q_ref[...].astype(F32)
     out_ref[1] = k_ref[...].astype(F32)
@@ -178,55 +185,62 @@
     return d_q, d_keys, d_values
 
 
+def own_body(
+    cls_ref, band_ref, gain_ref, inv_ref, q_ref, k_ref, v_ref, g_ref, after_ref, dq_ref, fin_ref, done_ref
+):
+    slots, _ = head_slots(cls_ref, band_ref)
+    inv = inv_ref[...]
+    done_ref[...] = inv
+    cols = columns(slots[0])
+    q = normed(q_ref[:, cols], spread(inv, 0), gain_ref[0, pl.ds(slots[0], 1), :])
+    k = normed(k_ref[:, cols], spread(inv, 2), gain_ref[1, pl.ds(slots[0], 1), :])
+    d_q, d_k, d_v = attend(q, g_ref[:, cols], [k], [v_ref[:, cols]], [None])
+    dq_ref[...] = d_q.astype(BF)
+    fin_ref[0] = d_k[0].astype(BF)
+    fin_ref[1] = d_v[0].astype(BF)
+
+
 def spatial_body(
     cls_ref,
     band_ref,
     frame_ref,
     gain_ref,
     inv_ref,
+    inv_far_ref,
     q_ref,
-    k_ref,
-    v_ref,
     g_ref,
     halo_ref,
     near_ref,
     far_ref,
     dq_ref,
-    fin_ref,
     own_ref,
     to_near_ref,
     to_far_ref,
 ):
     slots, bands = head_slots(cls_ref, band_ref)
     frame = frame_ref[0]
-    inv = inv_ref[...]
-    q_inv = spread(inv, 0)
-    for s in range(3):
+    q_inv = spread(inv_ref[...], 0)
+    far_inv = spread(inv_far_ref[...], 2)
+    for s in (1, 2):
         cols = columns(slots[s])
         q = normed(q_ref[:, cols], q_inv, gain_ref[0, pl.ds(slots[s], 1), :])
-        g = g_ref[:, cols]
-        if s == 0:
-            k = normed(k_ref[:, cols], spread(inv, 2), gain_ref[1, pl.ds(slots[s], 1), :])
-            d_q, d_k, d_v = attend(q, g, [k], [v_ref[:, cols]], [None])
-            fin_ref[0] = d_k[0].astype(BF)
-            fin_ref[1] = d_v[0].astype(BF)
-        else:
-            at = 2 * s - 2
-            wide = bands[s - 1] > 0
-            keys = [near_ref[at], halo_ref[at], far_ref[at]]
-            values = [near_ref[at + 1], halo_ref[at + 1], far_ref[at + 1]]
-            allowed = [wide, None, wide & (frame > 0) & (frame < FRAMES - 1)]
-            d_q, d_k, d_v = attend(q, g, keys, values, allowed)
-            to_near_ref[at] = d_k[0].astype(BF)
-            to_near_ref[at + 1] = d_v[0].astype(BF)
-            own_ref[at] = d_k[1]
-            own_ref[at + 1] = d_v[1]
-            to_far_ref[at] = d_k[2].astype(BF)
-            to_far_ref[at + 1] = d_v[2].astype(BF)
-        dq_ref[s] = d_q.astype(BF)
-
-
-def temporal_body(in_ref, out_ref):
+        at = 2 * s - 2
+        wide = bands[s - 1] > 0
+        far = normed(far_ref[at], far_inv, gain_ref[1, pl.ds(slots[s], 1), :])
+        keys = [near_ref[at], halo_ref[at], far]
+        values = [near_ref[at + 1], halo_ref[at + 1], far_ref[at + 1]]
+        allowed = [wide, None, wide & (frame > 0) & (frame < FRAMES - 1)]
+        d_q, d_k, d_v = attend(q, g_ref[:, cols], keys, values, allowed)
+        dq_ref[s - 1] = d_q.astype(BF)
+        to_near_ref[at] = d_k[0].astype(BF)
+        to_near_ref[at + 1] = d_v[0].astype(BF)
+        own_ref[at] = d_k[1]
+        own_ref[at + 1] = d_v[1]
+        to_far_ref[at] = d_k[2].astype(BF)
+        to_far_ref[at + 1] = d_v[2].astype(BF)
+
+
+def temporal_body(in_ref, after_ref, out_ref):
     rows = FRAMES * 8
     q, k, v, g = (in_ref[:, a].reshape(rows, HD) for a in range(4))
     d_k = jnp.zeros((rows, HD), F32)
@@ -251,18 +265,30 @@
 
 
 def spatial_sums_body(
-    cls_ref, band_ref, gain_ref, q_ref, k_ref, dq_ref, fin_ref, own_ref, near_ref, far_ref, grad_ref, part_ref
+    cls_ref,
+    band_ref,
+    gain_ref,
+    q_ref,
+    k_ref,
+    dq0_ref,
+    dq_ref,
+    fin_ref,
+    own_ref,
+    far_ref,
+    near_ref,
+    grad_ref,
+    part_ref,
 ):
     slots, _ = head_slots(cls_ref, band_ref)
-    q_total = product(gain_ref, 0, slots[0], dq_ref[0], q_ref)
+    q_total = product(gain_ref, 0, slots[0], dq0_ref[...], q_ref)
     k_total = product(gain_ref, 1, slots[0], fin_ref[0], k_ref)
     for s in (1, 2):
         for b in range(2):
             at = 2 * s - 2 + b
             grad_ref[at] = (
-                own_ref[at] + near_ref[at].astype(F32) + far_ref[at].astype(F32)
+                own_ref[at] + far_ref[at].astype(F32) + near_ref[at].astype(F32)
             ).astype(BF)
-        q_total += product(gain_ref, 0, slots[s], dq_ref[s], q_ref)
+        q_total += product(gain_ref, 0, slots[s], dq_ref[s - 1], q_ref)
         k_total += product(gain_ref, 1, slots[s], grad_ref[2 * s - 2], k_ref)
     part_ref[0] = q_total
     part_ref[1] = k_total
@@ -289,6 +315,7 @@
     q_ref,
     k_ref,
     back_ref,
+    dq0_ref,
     dq_ref,
     fin_ref,
     grad_ref,
@@ -305,7 +332,7 @@
             if s >= 3:
                 grad = back_ref[(s - 3) * 32 : (s - 2) * 32, which].reshape(TOK, HD)
             elif which == 0:
-                grad = dq_ref[s]
+                grad = dq0_ref[...] if s == 0 else dq_ref[s - 1]
             else:
                 grad = fin_ref[0] if s == 0 else grad_ref[2 * s - 2]
             gain = gain_ref[which, pl.ds(slots[s], 1), :]
@@ -335,7 +362,11 @@
         name="squares",
         compiler_params=pltpu.CompilerParams(vmem_limit_bytes=56 << 20),
     )(query_pre, key_pre)
-    gains = call(gains_body, shape((2, HEADS_DEV, HD), F32), [VM, VM, ANY, VM], "gains", 1)(
+    halo = call(halo_body, shape(block, BF), [SM, SM, ANY, VM, VM], "halo", 2)(
+        head_class, head_band, sums, key_pre, value
+    )
+    far = lax.ppermute(halo, "seq", chip)
+    gains = call(gains_body, shape((2, HEADS_DEV, HD), F32), [VM, VM, ANY, VM], "gains", 8)(
         gain_q.reshape(HEADS_DEV, HD), gain_k.reshape(HEADS_DEV, HD), sums, d_out
     )
     sums = lax.all_to_all(sums, "head", 0, 0, tiled=True)
@@ -348,44 +379,39 @@
     )(head_class, head_band, sums, gains, query_pre, key_pre, value, d_out)
     held = lax.all_to_all(send, "seq", 0, 0, tiled=True)
     near = lax.ppermute(halo, "seq", core)
-    far = lax.ppermute(halo, "seq", chip)
-    dq, fin, own, to_near, to_far = call(
+    inv_far = lax.ppermute(inv, "seq", chip)
+    dq0, fin, done = call(
+        own_body,
+        (shape((TOK, HD), BF), shape((2, TOK, HD), BF), shape((8, HD), F32)),
+        [SM, SM] + [VM] * 6 + [ANY],
+        "own",
+        10,
+    )(head_class, head_band, gains, inv, query_pre, key_pre, value, d_out, far)
+    dq, own, to_near, to_far = call(
         spatial_body,
         (
-            shape((3, TOK, HD), BF),
             shape((2, TOK, HD), BF),
             shape(block, F32),
             shape(block, BF),
             shape(block, BF),
         ),
-        [SM] * 3 + [VM] * 9,
+        [SM] * 3 + [VM] * 8,
         "spatial",
         6,
     )(
-        head_class,
-        head_band,
-        frame,
-        gains,
-        inv,
-        query_pre,
-        key_pre,
-        value,
-        d_out,
-        halo,
-        near,
-        far,
+        head_class, head_band, frame, gains, inv, inv_far, query_pre, d_out, halo, near, far
     )
     from_far = lax.ppermute(to_far, "seq", chip)
     from_near = lax.ppermute(to_near, "seq", core)
-    grads = call(temporal_body, shape((FRAMES, 3, 8, HD), BF), [VM], "temporal", 3)(held)
+    grads = call(temporal_body, shape((FRAMES, 3, 8, HD), BF), [VM, ANY], "temporal", 3)(held, done)
     back = lax.all_to_all(grads, "seq", 0, 0, tiled=True)
     grad, part = call(
         spatial_sums_body,
         (shape(block, BF), shape((2, TOK, HD), F32)),
-        [SM, SM] + [VM] * 8,
+        [SM, SM] + [VM] * 9,
         "spatial_sums",
         3,
-    )(head_class, head_band, gains, query_pre, key_pre, dq, fin, own, from_far, from_near)
+    )(head_class, head_band, gains, query_pre, key_pre, dq0, dq, fin, own, from_far, from_near)
     inner = call(inner_body, shape((8, 8, HD), F32), [SM, SM] + [VM] * 5, "inner", 2)(
         head_class, head_band, gains, query_pre, key_pre, back, part
     )
@@ -393,10 +419,10 @@
     return call(
         final_body,
         (shape((TOK, WIDTH), BF),) * 3,
-        [SM, SM] + [VM] * 9,
+        [SM, SM] + [VM] * 10,
         "final",
         3,
-    )(head_class, head_band, gains, inv, inner, query_pre, key_pre, back, dq, fin, grad)
+    )(head_class, head_band, gains, inv, inner, query_pre, key_pre, back, dq0, dq, fin, grad)
 
 
 def solution(mesh):

time: 97.8 us -> 98 us (level)
  the two profiles are of different devices: /device:TPU:25 before, /device:TPU:24 now
where the time goes in v6:
time: 98 us; the launch traced here: 97.4 us
  starting transfers between devices  48.2 us (49%)
  waiting for transfers between devices  20.4 us (21%)
  Pallas kernels  14.4 us (15%)
  blocking collectives  13.4 us (14%)
    all_to_all x1, blocking collectives, per_device(): inner = lax.all_to_all(inner, 'head', 0, 0, tiled=True)  13.4 us
    all_to_all x1, starting transfers between devices, per_device(): sums = lax.all_to_all(sums, 'head', 0, 0, tiled=True)  12.9 us
    all_to_all x1, starting transfers between devices, per_device(): held = lax.all_to_all(send, 'seq', 0, 0, tiled=True)  10.6 us
    all_to_all x1, waiting for transfers between devices, per_device(): held = lax.all_to_all(send, 'seq', 0, 0, tiled=True)  8.4 us
    ppermute x1, waiting for transfers between devices, per_device(): from_far = lax.ppermute(to_far, 'seq', chip)  6.84 us
    all_to_all x1, starting transfers between devices, per_device(): back = lax.all_to_all(grads, 'seq', 0, 0, tiled=True)  6.79 us
    all_to_all x1, waiting for transfers between devices, per_device(): sums = lax.all_to_all(sums, 'head', 0, 0, tiled=True)  5.16 us
    ppermute x1, starting transfers between devices, per_device(): inv_far = lax.ppermute(inv, 'seq', chip)  4.91 us
  transfers between devices with their start and end apart: 8, of which 3 were waited for; matrix products, arithmetic and copies ran while one was open for 0% of the time, Pallas kernels for 9%

profile of v6, /device:TPU:24, one launch (start us, length us, event | category | flops | bytes accessed | tf_op | source)
XLA Modules:
  0.0 97.4 jit_solution(1888106448806590333)
XLA Ops:
  0.7 2.4 %squares.1.after_ref = f32[8,8,128]{2,1,0:T(8,128)} custom-call(bf16[256,640]{1,0:T(8,128)(2,1)} %q_ref.11, bf16[256,640]{1,0:T(8,128)(2,1)} %k_ref.11), custom_call_target="tpu_custom_call" | custom-call | tf_op jit(solution)/shard_map/squares/pallas_call | solution.py:356
  3.0 0.0 copy-start.2
  3.1 12.9 %all-to-all-start = ((f32[8,8,128]{2,1,0:T(8,128)}), f32[8,8,128]{2,1,0:T(8,128)S(1)}, u32[]{:S(2)}, u32[]{:S(2)}) async-start(f32[8,8,128]{2,1,0:T(8,128)} %squares.1.after_ref), calls=%async_computation | async-start | bytes 65536 | tf_op jit(solution)/shard_map/all_to_all | solution.py:372
  16.0 0.0 copy-start.4
  16.0 0.6 halo.1
  16.7 0.0 copy-start.5
  16.7 4.2 %collective-permute-start = (bf16[4,256,128]{2,1,0:T(8,128)(2,1)S(1)}, bf16[4,256,128]{2,1,0:T(8,128)(2,1)S(1)}, u32[]{:S(2)}, u32[]{:S(2)}) collective-permute-start(bf16[4,256,128]{2,1,0:T(8,128)(2,1)S(1)} %halo.1), channel_id=1, source_target_pairs={{8,16},{16,8},{24,32},{32,24},{40,48},{48,40},{56,64},{64,56},{72,... | collective-permute-start | bytes 786440 | tf_op jit(solution)/shard_map/ppermute | solution.py:368
  21.0 5.2 %all-to-all-done.sums_ref = f32[8,8,128]{2,1,0:T(8,128)S(1)} async-done(((f32[8,8,128]{2,1,0:T(8,128)}), f32[8,8,128]{2,1,0:T(8,128)S(1)}, u32[]{:S(2)}, u32[]{:S(2)}) %all-to-all-start) | async-done | bytes 32800 | tf_op jit(solution)/shard_map/all_to_all | solution.py:372
  26.1 1.6 %norm.1 = (bf16[64,4,8,128]{3,2,1,0:T(8,128)(2,1)}, bf16[4,256,128]{2,1,0:T(8,128)(2,1)S(1)}, f32[8,128]{1,0:T(8,128)S(1)}) custom-call(s32[5]{0:T(128)S(1)} %copy-done.7, s32[5]{0:T(128)S(1)} %copy-done.8, f32[8,8,128]{2,1,0:T(8,128)S(1)} %all-to-all-done.sums_ref, f32[2,5,128]{2,1,0:T(8,128)S(1)} %gains.1.gain_ref, bf16[256,640]{1,0:T(8,128)(2,1)S(1)} %copy-done, ...), custom_call_target="tpu_custom_call" | custom-call | flops 2000000000 | bytes 2000000 | tf_op jit(solution)/shard_map/norm/pallas_call | solution.py:373
  27.7 10.6 %all-to-all-start.1 = ((bf16[64,4,8,128]{3,2,1,0:T(8,128)(2,1)}), bf16[64,4,8,128]{3,2,1,0:T(8,128)(2,1)S(1)}, u32[]{:S(2)}, u32[]{:S(2)}) async-start(bf16[64,4,8,128]{3,2,1,0:T(8,128)(2,1)} %get-tuple-element.16), calls=%async_computation.1 | async-start | bytes 1048576 | tf_op jit(solution)/shard_map/all_to_all | solution.py:380
  38.4 4.9 %collective-permute-start.1 = (f32[8,128]{1,0:T(8,128)S(1)}, f32[8,128]{1,0:T(8,128)S(1)}, u32[]{:S(2)}, u32[]{:S(2)}) collective-permute-start(f32[8,128]{1,0:T(8,128)S(1)} %get-tuple-element.15.inv_ref), channel_id=1, source_target_pairs={{8,16},{16,8},{24,32},{32,24},{40,48},{48,40},{56,64},{64,56},{72,... | collective-permute-start | bytes 12296 | tf_op jit(solution)/shard_map/ppermute | solution.py:382
  43.3 1.9 %collective-permute-start.2 = (bf16[4,256,128]{2,1,0:T(8,128)(2,1)S(1)}, bf16[4,256,128]{2,1,0:T(8,128)(2,1)S(1)}, u32[]{:S(2)}, u32[]{:S(2)}) collective-permute-start(bf16[4,256,128]{2,1,0:T(8,128)(2,1)S(1)} %get-tuple-element.19.halo_ref), channel_id=1, source_target_pairs={{0,8},{8,0},{16,24},{24,16},{32,40},{40,32},{48,56},{56,48},{64,72... | collective-permute-start | bytes 786440 | tf_op jit(solution)/shard_map/ppermute | solution.py:381
  45.2 1.2 %own.1 = (bf16[256,128]{1,0:T(8,128)(2,1)S(1)}, bf16[2,256,128]{2,1,0:T(8,128)(2,1)S(1)}, f32[8,128]{1,0:T(8,128)S(1)}) custom-call(s32[5]{0:T(128)S(1)} %copy-done.7, s32[5]{0:T(128)S(1)} %copy-done.8, f32[2,5,128]{2,1,0:T(8,128)S(1)} %gains.1.gain_ref, f32[8,128]{1,0:T(8,128)S(1)} %get-tuple-element.15.inv_ref, bf16[256,640]{1,0:T(8,128)(2,1)S(1)} %copy-done, ...), custom_call_target="tpu_custom_call" | custom-call | flops 10000000000 | bytes 10000000 | tf_op jit(solution)/shard_map/own/pallas_call | solution.py:383
  46.5 8.4 %all-to-all-done.1.in_ref = bf16[64,4,8,128]{3,2,1,0:T(8,128)(2,1)S(1)} async-done(((bf16[64,4,8,128]{3,2,1,0:T(8,128)(2,1)}), bf16[64,4,8,128]{3,2,1,0:T(8,128)(2,1)S(1)}, u32[]{:S(2)}, u32[]{:S(2)}) %all-to-all-start.1) | async-done | bytes 524320 | tf_op jit(solution)/shard_map/all_to_all | solution.py:380
  54.9 2.5 %temporal.1 = bf16[64,3,8,128]{3,2,1,0:T(8,128)(2,1)} custom-call(bf16[64,4,8,128]{3,2,1,0:T(8,128)(2,1)S(1)} %all-to-all-done.1.in_ref, f32[8,128]{1,0:T(8,128)S(1)} %get-tuple-element.17.after_ref), custom_call_target="tpu_custom_call" | custom-call | flops 3000000000 | bytes 3000000 | tf_op jit(solution)/shard_map/temporal/pallas_call | solution.py:406
  57.3 6.8 %all-to-all-start.2 = ((bf16[64,3,8,128]{3,2,1,0:T(8,128)(2,1)}), bf16[64,3,8,128]{3,2,1,0:T(8,128)(2,1)S(1)}, u32[]{:S(2)}, u32[]{:S(2)}) async-start(bf16[64,3,8,128]{3,2,1,0:T(8,128)(2,1)} %temporal.1), calls=%async_computation.2 | async-start | bytes 786432 | tf_op jit(solution)/shard_map/all_to_all | solution.py:407
  64.2 2.6 %spatial.1 = (bf16[2,256,128]{2,1,0:T(8,128)(2,1)S(1)}, f32[4,256,128]{2,1,0:T(8,128)S(1)}, bf16[4,256,128]{2,1,0:T(8,128)(2,1)S(1)}, bf16[4,256,128]{2,1,0:T(8,128)(2,1)S(1)}) custom-call(s32[5]{0:T(128)S(1)} %copy-done.7, s32[5]{0:T(128)S(1)} %copy-done.8, s32[1]{0:T(128)} %bitcast.2.frame_ref, f32[2,5,128]{2,1,0:T(8,128)S(1)} %gains.1.gain_ref, ...), custom_call_target="tpu_custom_call" | custom-call | flops 6000000000 | bytes 6000000 | tf_op jit(solution)/shard_map/spatial/pallas_call | solution.py:390
  66.7 4.9 %collective-permute-start.3 = (bf16[4,256,128]{2,1,0:T(8,128)(2,1)S(1)}, bf16[4,256,128]{2,1,0:T(8,128)(2,1)S(1)}, u32[]{:S(2)}, u32[]{:S(2)}) collective-permute-start(bf16[4,256,128]{2,1,0:T(8,128)(2,1)S(1)} %get-tuple-element.23), channel_id=1, source_target_pairs={{8,16},{16,8},{24,32},{32,24},{40,48},{48,40},{56,64},{64,56},{72,... | collective-permute-start | bytes 786440 | tf_op jit(solution)/shard_map/ppermute | solution.py:404
  71.6 1.9 %collective-permute-start.4 = (bf16[4,256,128]{2,1,0:T(8,128)(2,1)S(1)}, bf16[4,256,128]{2,1,0:T(8,128)(2,1)S(1)}, u32[]{:S(2)}, u32[]{:S(2)}) collective-permute-start(bf16[4,256,128]{2,1,0:T(8,128)(2,1)S(1)} %get-tuple-element.24), channel_id=1, source_target_pairs={{0,8},{8,0},{16,24},{24,16},{32,40},{40,32},{48,56},{56,48},{64,72... | collective-permute-start | bytes 786440 | tf_op jit(solution)/shard_map/ppermute | solution.py:405
  73.6 6.8 %collective-permute-done.3.far_ref = bf16[4,256,128]{2,1,0:T(8,128)(2,1)S(1)} collective-permute-done((bf16[4,256,128]{2,1,0:T(8,128)(2,1)S(1)}, bf16[4,256,128]{2,1,0:T(8,128)(2,1)S(1)}, u32[]{:S(2)}, u32[]{:S(2)}) %collective-permute-start.3) | collective-permute-done | bytes 262176 | tf_op jit(solution)/shard_map/ppermute | solution.py:404
  80.4 0.8 spatial_sums.1
  81.2 0.9 inner.1
  82.1 13.4 %all_to_all.20.inner_ref = f32[8,8,128]{2,1,0:T(8,128)S(1)} all-to-all(f32[8,8,128]{2,1,0:T(8,128)S(1)} %inner.1), channel_id=1, replica_groups=mesh['seq'=64,'head'=8] {'head'}, dimensions={0} | all-to-all | bytes 65536 | tf_op jit(solution)/shard_map/all_to_all | solution.py:418
  95.6 1.8 %final.1 = (bf16[256,640]{1,0:T(8,128)(2,1)}, bf16[256,640]{1,0:T(8,128)(2,1)}, bf16[256,640]{1,0:T(8,128)(2,1)}) custom-call(s32[5]{0:T(128)S(1)} %copy-done.7, s32[5]{0:T(128)S(1)} %copy-done.8, f32[2,5,128]{2,1,0:T(8,128)S(1)} %gains.1.gain_ref, f32[8,128]{1,0:T(8,128)S(1)} %get-tuple-element.15.inv_ref, f32[8,8,128]{2,1,0:T(8,128)S(1)} %all_to_all.20.inner_ref, ...), custom_call_target="tpu_custom_call" | custom-call | flops 3000000000 | bytes 3000000 | tf_op jit(solution)/shard_map/final/pallas_call | solution.py:419
  (21 shorter events, 0.1 us)
Async XLA Ops:
  0.6 15.3 %copy-start.1 = (bf16[256,640]{1,0:T(8,128)(2,1)S(1)}, bf16[256,640]{1,0:T(8,128)(2,1)}, u32[]{:S(2)}) copy-start(bf16[256,640]{1,0:T(8,128)(2,1)} %k_ref.11) | copy-start | bytes 983044
  0.6 15.3 %copy-start.3 = (bf16[256,640]{1,0:T(8,128)(2,1)S(1)}, bf16[256,640]{1,0:T(8,128)(2,1)}, u32[]{:S(2)}) copy-start(bf16[256,640]{1,0:T(8,128)(2,1)} %v_ref.5) | copy-start | bytes 983044
  3.0 12.9 %copy-start.2 = (f32[8,8,128]{2,1,0:T(8,128)S(1)}, f32[8,8,128]{2,1,0:T(8,128)}, u32[]{:S(2)}) copy-start(f32[8,8,128]{2,1,0:T(8,128)} %squares.1.after_ref) | copy-start | bytes 98308
  3.1 12.9 %copy-start.7 = (s32[5]{0:T(128)S(1)}, s32[5]{0:T(128)}, u32[]{:S(2)}) copy-start(s32[5]{0:T(128)} %cls_ref.13) | copy-start | bytes 64
  3.1 12.9 %copy-start.8 = (s32[5]{0:T(128)S(1)}, s32[5]{0:T(128)}, u32[]{:S(2)}) copy-start(s32[5]{0:T(128)} %band_ref.13) | copy-start | bytes 64
  3.1 23.1 %all-to-all-start = ((f32[8,8,128]{2,1,0:T(8,128)}), f32[8,8,128]{2,1,0:T(8,128)S(1)}, u32[]{:S(2)}, u32[]{:S(2)}) async-start(f32[8,8,128]{2,1,0:T(8,128)} %squares.1.after_ref), calls=%async_computation | async-start | bytes 65536 | tf_op jit(solution)/shard_map/all_to_all | solution.py:372
  16.0 4.9 %copy-start.4 = (bf16[256,640]{1,0:T(8,128)(2,1)S(1)}, bf16[256,640]{1,0:T(8,128)(2,1)}, u32[]{:S(2)}) copy-start(bf16[256,640]{1,0:T(8,128)(2,1)} %g_ref.7) | copy-start | bytes 983044
  16.0 4.9 %copy-start.6 = (bf16[640]{0:T(1024)(128)(2,1)S(1)}, bf16[640]{0:T(1024)(128)(2,1)}, u32[]{:S(2)}) copy-start(bf16[640]{0:T(1024)(128)(2,1)} %param.13) | copy-start | bytes 3844
  16.7 4.3 %copy-start.5 = (bf16[640]{0:T(1024)(128)(2,1)S(1)}, bf16[640]{0:T(1024)(128)(2,1)}, u32[]{:S(2)}) copy-start(bf16[640]{0:T(1024)(128)(2,1)} %param.12) | copy-start | bytes 3844
  16.7 28.6 %collective-permute-start = (bf16[4,256,128]{2,1,0:T(8,128)(2,1)S(1)}, bf16[4,256,128]{2,1,0:T(8,128)(2,1)S(1)}, u32[]{:S(2)}, u32[]{:S(2)}) collective-permute-start(bf16[4,256,128]{2,1,0:T(8,128)(2,1)S(1)} %halo.1), channel_id=1, source_target_pairs={{8,16},{16,8},{24,32},{32,24},{40,48},{48,40},{56,64},{64,56},{72,... | collective-permute-start | bytes 786440 | tf_op jit(solution)/shard_map/ppermute | solution.py:368
  21.0 5.2 %copy-start = (bf16[256,640]{1,0:T(8,128)(2,1)S(1)}, bf16[256,640]{1,0:T(8,128)(2,1)}, u32[]{:S(2)}) copy-start(bf16[256,640]{1,0:T(8,128)(2,1)} %q_ref.11) | copy-start | bytes 983044
  27.7 27.2 %all-to-all-start.1 = ((bf16[64,4,8,128]{3,2,1,0:T(8,128)(2,1)}), bf16[64,4,8,128]{3,2,1,0:T(8,128)(2,1)S(1)}, u32[]{:S(2)}, u32[]{:S(2)}) async-start(bf16[64,4,8,128]{3,2,1,0:T(8,128)(2,1)} %get-tuple-element.16), calls=%async_computation.1 | async-start | bytes 1048576 | tf_op jit(solution)/shard_map/all_to_all | solution.py:380
  38.4 25.8 %collective-permute-start.1 = (f32[8,128]{1,0:T(8,128)S(1)}, f32[8,128]{1,0:T(8,128)S(1)}, u32[]{:S(2)}, u32[]{:S(2)}) collective-permute-start(f32[8,128]{1,0:T(8,128)S(1)} %get-tuple-element.15.inv_ref), channel_id=1, source_target_pairs={{8,16},{16,8},{24,32},{32,24},{40,48},{48,40},{56,64},{64,56},{72,... | collective-permute-start | bytes 12296 | tf_op jit(solution)/shard_map/ppermute | solution.py:382
  43.3 20.9 %collective-permute-start.2 = (bf16[4,256,128]{2,1,0:T(8,128)(2,1)S(1)}, bf16[4,256,128]{2,1,0:T(8,128)(2,1)S(1)}, u32[]{:S(2)}, u32[]{:S(2)}) collective-permute-start(bf16[4,256,128]{2,1,0:T(8,128)(2,1)S(1)} %get-tuple-element.19.halo_ref), channel_id=1, source_target_pairs={{0,8},{8,0},{16,24},{24,16},{32,40},{40,32},{48,56},{56,48},{64,72... | collective-permute-start | bytes 786440 | tf_op jit(solution)/shard_map/ppermute | solution.py:381
  57.3 23.9 %all-to-all-start.2 = ((bf16[64,3,8,128]{3,2,1,0:T(8,128)(2,1)}), bf16[64,3,8,128]{3,2,1,0:T(8,128)(2,1)S(1)}, u32[]{:S(2)}, u32[]{:S(2)}) async-start(bf16[64,3,8,128]{3,2,1,0:T(8,128)(2,1)} %temporal.1), calls=%async_computation.2 | async-start | bytes 786432 | tf_op jit(solution)/shard_map/all_to_all | solution.py:407
  66.7 13.7 %collective-permute-start.3 = (bf16[4,256,128]{2,1,0:T(8,128)(2,1)S(1)}, bf16[4,256,128]{2,1,0:T(8,128)(2,1)S(1)}, u32[]{:S(2)}, u32[]{:S(2)}) collective-permute-start(bf16[4,256,128]{2,1,0:T(8,128)(2,1)S(1)} %get-tuple-element.23), channel_id=1, source_target_pairs={{8,16},{16,8},{24,32},{32,24},{40,48},{48,40},{56,64},{64,56},{72,... | collective-permute-start | bytes 786440 | tf_op jit(solution)/shard_map/ppermute | solution.py:404
  71.6 8.8 %collective-permute-start.4 = (bf16[4,256,128]{2,1,0:T(8,128)(2,1)S(1)}, bf16[4,256,128]{2,1,0:T(8,128)(2,1)S(1)}, u32[]{:S(2)}, u32[]{:S(2)}) collective-permute-start(bf16[4,256,128]{2,1,0:T(8,128)(2,1)S(1)} %get-tuple-element.24), channel_id=1, source_target_pairs={{0,8},{8,0},{16,24},{24,16},{32,40},{40,32},{48,56},{56,48},{64,72... | collective-permute-start | bytes 786440 | tf_op jit(solution)/shard_map/ppermute | solution.py:405

commit v7 on v6

--- a/solution.py
+++ b/solution.py
@@ -141,7 +141,7 @@
 
 
 def norm_body(
-    cls_ref, band_ref, sums_ref, gain_ref, q_ref, k_ref, v_ref, g_ref, send_ref, halo_ref, inv_ref
+    cls_ref, band_ref, sums_ref, gain_ref, q_ref, k_ref, v_ref, g_ref, send_ref, inv_ref
 ):
     slots, _ = head_slots(cls_ref, band_ref)
     inv = inverses(sums_ref)
@@ -158,10 +158,6 @@
         )
         for a, part in enumerate(parts):
             send_ref[s * 32 : (s + 1) * 32, a] = part.reshape(32, 8, HD)
-    for s in (1, 2):
-        at = columns(slots[s])
-        halo_ref[2 * s - 2] = normed(k_ref[:, at], k_inv, gain_ref[1, pl.ds(slots[s], 1), :])
-        halo_ref[2 * s - 1] = v_ref[:, at]
 
 
 def attend(q, g, keys, values, allowed):
@@ -186,18 +182,23 @@
 
 
 def own_body(
-    cls_ref, band_ref, gain_ref, inv_ref, q_ref, k_ref, v_ref, g_ref, after_ref, dq_ref, fin_ref, done_ref
+    cls_ref, band_ref, gain_ref, inv_ref, q_ref, k_ref, v_ref, g_ref, after_ref, dq_ref, fin_ref, halo_ref, done_ref
 ):
     slots, _ = head_slots(cls_ref, band_ref)
     inv = inv_ref[...]
     done_ref[...] = inv
     cols = columns(slots[0])
     q = normed(q_ref[:, cols], spread(inv, 0), gain_ref[0, pl.ds(slots[0], 1), :])
-    k = normed(k_ref[:, cols], spread(inv, 2), gain_ref[1, pl.ds(slots[0], 1), :])
+    k_inv = spread(inv, 2)
+    k = normed(k_ref[:, cols], k_inv, gain_ref[1, pl.ds(slots[0], 1), :])
     d_q, d_k, d_v = attend(q, g_ref[:, cols], [k], [v_ref[:, cols]], [None])
     dq_ref[...] = d_q.astype(BF)
     fin_ref[0] = d_k[0].astype(BF)
     fin_ref[1] = d_v[0].astype(BF)
+    for s in (1, 2):
+        at = columns(slots[s])
+        halo_ref[2 * s - 2] = normed(k_ref[:, at], k_inv, gain_ref[1, pl.ds(slots[s], 1), :])
+        halo_ref[2 * s - 1] = v_ref[:, at]
 
 
 def spatial_body(
@@ -216,17 +217,20 @@
     own_ref,
     to_near_ref,
     to_far_ref,
+    tick_ref,
 ):
     slots, bands = head_slots(cls_ref, band_ref)
     frame = frame_ref[0]
     q_inv = spread(inv_ref[...], 0)
     far_inv = spread(inv_far_ref[...], 2)
+    far_total = jnp.zeros((TOK, HD), F32)
     for s in (1, 2):
         cols = columns(slots[s])
         q = normed(q_ref[:, cols], q_inv, gain_ref[0, pl.ds(slots[s], 1), :])
         at = 2 * s - 2
         wide = bands[s - 1] > 0
-        far = normed(far_ref[at], far_inv, gain_ref[1, pl.ds(slots[s], 1), :])
+        k_gain = gain_ref[1, pl.ds(slots[s], 1), :]
+        far = normed(far_ref[at], far_inv, k_gain)
         keys = [near_ref[at], halo_ref[at], far]
         values = [near_ref[at + 1], halo_ref[at + 1], far_ref[at + 1]]
         allowed = [wide, None, wide & (frame > 0) & (frame < FRAMES - 1)]
@@ -238,6 +242,8 @@
         own_ref[at + 1] = d_v[1]
         to_far_ref[at] = d_k[2].astype(BF)
         to_far_ref[at + 1] = d_v[2].astype(BF)
+        far_total += k_gain * d_k[2] * far_ref[at].astype(F32)
+    tick_ref[...] = lane_sums(far_total)
 
 
 def temporal_body(in_ref, after_ref, out_ref):
@@ -265,36 +271,20 @@
 
 
 def spatial_sums_body(
-    cls_ref,
-    band_ref,
-    gain_ref,
-    q_ref,
-    k_ref,
-    dq0_ref,
-    dq_ref,
-    fin_ref,
-    own_ref,
-    far_ref,
-    near_ref,
-    grad_ref,
-    part_ref,
+    cls_ref, band_ref, gain_ref, q_ref, k_ref, dq0_ref, dq_ref, fin_ref, own_ref, near_ref, part_ref
 ):
     slots, _ = head_slots(cls_ref, band_ref)
     q_total = product(gain_ref, 0, slots[0], dq0_ref[...], q_ref)
     k_total = product(gain_ref, 1, slots[0], fin_ref[0], k_ref)
     for s in (1, 2):
-        for b in range(2):
-            at = 2 * s - 2 + b
-            grad_ref[at] = (
-                own_ref[at] + far_ref[at].astype(F32) + near_ref[at].astype(F32)
-            ).astype(BF)
+        at = 2 * s - 2
         q_total += product(gain_ref, 0, slots[s], dq_ref[s - 1], q_ref)
-        k_total += product(gain_ref, 1, slots[s], grad_ref[2 * s - 2], k_ref)
+        k_total += product(gain_ref, 1, slots[s], own_ref[at] + near_ref[at].astype(F32), k_ref)
     part_ref[0] = q_total
     part_ref[1] = k_total
 
 
-def inner_body(cls_ref, band_ref, gain_ref, q_ref, k_ref, back_ref, part_ref, out_ref):
+def inner_body(cls_ref, band_ref, gain_ref, q_ref, k_ref, back_ref, part_ref, tick_ref, out_ref):
     slots, _ = head_slots(cls_ref, band_ref)
     sums = []
     for which, ref in enumerate((q_ref, k_ref)):
@@ -303,6 +293,7 @@
             grad = back_ref[s * 32 : (s + 1) * 32, which].reshape(TOK, HD)
             total += product(gain_ref, which, slots[3 + s], grad, ref)
         sums.append(lane_sums(total))
+    sums[1] += tick_ref[...]
     out_ref[...] = jnp.broadcast_to(rows_of(*sums)[None], (8, 8, HD))
 
 
@@ -318,13 +309,19 @@
     dq0_ref,
     dq_ref,
     fin_ref,
-    grad_ref,
+    own_ref,
+    far_ref,
+    near_ref,
     out_q_ref,
     out_k_ref,
     out_v_ref,
 ):
     slots, _ = head_slots(cls_ref, band_ref)
     inv = inv_ref[...]
+    grads = [
+        (own_ref[at] + far_ref[at].astype(F32) + near_ref[at].astype(F32)).astype(BF)
+        for at in range(4)
+    ]
     pull = inv * inv * inv * jnp.sum(inner_ref[...], axis=0) / FULL
     for which, (ref, out) in enumerate(((q_ref, out_q_ref), (k_ref, out_k_ref))):
         inverse, pulled = spread(inv, 2 * which), spread(pull, 2 * which)
@@ -334,7 +331,7 @@
             elif which == 0:
                 grad = dq0_ref[...] if s == 0 else dq_ref[s - 1]
             else:
-                grad = fin_ref[0] if s == 0 else grad_ref[2 * s - 2]
+                grad = fin_ref[0] if s == 0 else grads[2 * s - 2]
             gain = gain_ref[which, pl.ds(slots[s], 1), :]
             at = columns(slots[s])
             out[:, at] = (
@@ -342,7 +339,7 @@
             ).astype(BF)
     out_v_ref[:, columns(slots[0])] = fin_ref[1]
     for s in (1, 2):
-        out_v_ref[:, columns(slots[s])] = grad_ref[2 * s - 1]
+        out_v_ref[:, columns(slots[s])] = grads[2 * s - 1]
     for s in range(2):
         out_v_ref[:, columns(slots[3 + s])] = back_ref[s * 32 : (s + 1) * 32, 2].reshape(TOK, HD)
 
@@ -370,30 +367,36 @@
         gain_q.reshape(HEADS_DEV, HD), gain_k.reshape(HEADS_DEV, HD), sums, d_out
     )
     sums = lax.all_to_all(sums, "head", 0, 0, tiled=True)
-    send, halo, inv = call(
+    send, inv = call(
         norm_body,
-        (shape((FRAMES, 4, 8, HD), BF), shape(block, BF), shape((8, HD), F32)),
+        (shape((FRAMES, 4, 8, HD), BF), shape((8, HD), F32)),
         [SM, SM] + [VM] * 6,
         "norm",
         2,
     )(head_class, head_band, sums, gains, query_pre, key_pre, value, d_out)
     held = lax.all_to_all(send, "seq", 0, 0, tiled=True)
-    near = lax.ppermute(halo, "seq", core)
     inv_far = lax.ppermute(inv, "seq", chip)
-    dq0, fin, done = call(
+    dq0, fin, halo, done = call(
         own_body,
-        (shape((TOK, HD), BF), shape((2, TOK, HD), BF), shape((8, HD), F32)),
+        (
+            shape((TOK, HD), BF),
+            shape((2, TOK, HD), BF),
+            shape(block, BF),
+            shape((8, HD), F32),
+        ),
         [SM, SM] + [VM] * 6 + [ANY],
         "own",
         10,
     )(head_class, head_band, gains, inv, query_pre, key_pre, value, d_out, far)
-    dq, own, to_near, to_far = call(
+    near = lax.ppermute(halo, "seq", core)
+    dq, own, to_near, to_far, tick = call(
         spatial_body,
         (
             shape((2, TOK, HD), BF),
             shape(block, F32),
             shape(block, BF),
             shape(block, BF),
+            shape((8, TOK), F32),
         ),
         [SM] * 3 + [VM] * 8,
         "spatial",
@@ -401,28 +404,40 @@
     )(
         head_class, head_band, frame, gains, inv, inv_far, query_pre, d_out, halo, near, far
     )
+    tick = lax.ppermute(tick, "seq", chip)
     from_far = lax.ppermute(to_far, "seq", chip)
     from_near = lax.ppermute(to_near, "seq", core)
     grads = call(temporal_body, shape((FRAMES, 3, 8, HD), BF), [VM, ANY], "temporal", 3)(held, done)
     back = lax.all_to_all(grads, "seq", 0, 0, tiled=True)
-    grad, part = call(
-        spatial_sums_body,
-        (shape(block, BF), shape((2, TOK, HD), F32)),
-        [SM, SM] + [VM] * 9,
-        "spatial_sums",
-        3,
-    )(head_class, head_band, gains, query_pre, key_pre, dq0, dq, fin, own, from_far, from_near)
-    inner = call(inner_body, shape((8, 8, HD), F32), [SM, SM] + [VM] * 5, "inner", 2)(
-        head_class, head_band, gains, query_pre, key_pre, back, part
+    part = call(
+        spatial_sums_body, shape((2, TOK, HD), F32), [SM, SM] + [VM] * 8, "spatial_sums", 3
+    )(head_class, head_band, gains, query_pre, key_pre, dq0, dq, fin, own, from_near)
+    inner = call(inner_body, shape((8, 8, HD), F32), [SM, SM] + [VM] * 6, "inner", 2)(
+        head_class, head_band, gains, query_pre, key_pre, back, part, tick
     )
     inner = lax.all_to_all(inner, "head", 0, 0, tiled=True)
     return call(
         final_body,
         (shape((TOK, WIDTH), BF),) * 3,
-        [SM, SM] + [VM] * 10,
+        [SM, SM] + [VM] * 12,
         "final",
         3,
-    )(head_class, head_band, gains, inv, inner, query_pre, key_pre, back, dq0, dq, fin, grad)
+    )(
+        head_class,
+        head_band,
+        gains,
+        inv,
+        inner,
+        query_pre,
+        key_pre,
+        back,
+        dq0,
+        dq,
+        fin,
+        own,
+        from_far,
+        from_near,
+    )
 
 
 def solution(mesh):

time: 98 us -> 97.1 us (level)
  the two profiles are of different devices: /device:TPU:24 before, /device:TPU:32 now
where the time goes in v7:
time: 97.1 us; the launch traced here: 96.4 us
  starting transfers between devices  58.7 us (60%)
  waiting for transfers between devices  20.2 us (21%)
  Pallas kernels  15 us (15%)
  local copies, waits for them, and re-layouts  1.38 us (1%)
  between operations  1.02 us (1%)
    all_to_all x1, starting transfers between devices, per_device(): sums = lax.all_to_all(sums, 'head', 0, 0, tiled=True)  12.9 us
    all_to_all x1, starting transfers between devices, per_device(): held = lax.all_to_all(send, 'seq', 0, 0, tiled=True)  10.6 us
    all_to_all x1, starting transfers between devices, per_device(): back = lax.all_to_all(grads, 'seq', 0, 0, tiled=True)  9.1 us
    all_to_all x1, waiting for transfers between devices, per_device(): inner = lax.all_to_all(inner, 'head', 0, 0, tiled=True)  8.74 us
    all_to_all x1, waiting for transfers between devices, per_device(): sums = lax.all_to_all(sums, 'head', 0, 0, tiled=True)  5.15 us
    ppermute x1, starting transfers between devices, per_device(): tick = lax.ppermute(tick, 'seq', chip)  5.12 us
    all_to_all x1, waiting for transfers between devices, per_device(): held = lax.all_to_all(send, 'seq', 0, 0, tiled=True)  4.91 us
    ppermute x1, starting transfers between devices, per_device(): inv_far = lax.ppermute(inv, 'seq', chip)  4.91 us
  transfers between devices with their start and end apart: 10, of which 4 were waited for; matrix products, arithmetic and copies ran while one was open for 0% of the time, Pallas kernels for 11%

profile of v7, /device:TPU:32, one launch (start us, length us, event | category | flops | bytes accessed | tf_op | source)
XLA Modules:
  0.0 96.4 jit_solution(16685847230303297451)
XLA Ops:
  0.7 2.4 %squares.1.after_ref = f32[8,8,128]{2,1,0:T(8,128)} custom-call(bf16[256,640]{1,0:T(8,128)(2,1)} %q_ref.11, bf16[256,640]{1,0:T(8,128)(2,1)} %k_ref.11), custom_call_target="tpu_custom_call" | custom-call | tf_op jit(solution)/shard_map/squares/pallas_call | solution.py:353
  3.1 12.9 %all-to-all-start = ((f32[8,8,128]{2,1,0:T(8,128)}), f32[8,8,128]{2,1,0:T(8,128)S(1)}, u32[]{:S(2)}, u32[]{:S(2)}) async-start(f32[8,8,128]{2,1,0:T(8,128)} %squares.1.after_ref), calls=%async_computation | async-start | bytes 65536 | tf_op jit(solution)/shard_map/all_to_all | solution.py:369
  16.7 4.2 %collective-permute-start = (bf16[4,256,128]{2,1,0:T(8,128)(2,1)S(1)}, bf16[4,256,128]{2,1,0:T(8,128)(2,1)S(1)}, u32[]{:S(2)}, u32[]{:S(2)}) collective-permute-start(bf16[4,256,128]{2,1,0:T(8,128)(2,1)S(1)} %halo.1), channel_id=1, source_target_pairs={{8,16},{16,8},{24,32},{32,24},{40,48},{48,40},{56,64},{64,56},{72,... | collective-permute-start | bytes 786440 | tf_op jit(solution)/shard_map/ppermute | solution.py:365
  21.0 5.2 %all-to-all-done.sums_ref = f32[8,8,128]{2,1,0:T(8,128)S(1)} async-done(((f32[8,8,128]{2,1,0:T(8,128)}), f32[8,8,128]{2,1,0:T(8,128)S(1)}, u32[]{:S(2)}, u32[]{:S(2)}) %all-to-all-start) | async-done | bytes 32800 | tf_op jit(solution)/shard_map/all_to_all | solution.py:369
  26.1 1.5 %norm.1 = (bf16[64,4,8,128]{3,2,1,0:T(8,128)(2,1)}, f32[8,128]{1,0:T(8,128)S(1)}) custom-call(s32[5]{0:T(128)S(1)} %copy-done.7, s32[5]{0:T(128)S(1)} %copy-done.8, f32[8,8,128]{2,1,0:T(8,128)S(1)} %all-to-all-done.sums_ref, f32[2,5,128]{2,1,0:T(8,128)S(1)} %gains.1.gain_ref, bf16[256,640]{1,0:T(8,128)(2,1)S(1)} %copy-done, bf16[256,640]{1,0:T(8,128)(2,1)S(1)} %copy-done.1, ...), custom_call_target="tpu_custom_call" | custom-call | flops 2000000000 | bytes 2000000 | tf_op jit(solution)/shard_map/norm/pallas_call | solution.py:370
  27.7 10.6 %all-to-all-start.1 = ((bf16[64,4,8,128]{3,2,1,0:T(8,128)(2,1)}), bf16[64,4,8,128]{3,2,1,0:T(8,128)(2,1)S(1)}, u32[]{:S(2)}, u32[]{:S(2)}) async-start(bf16[64,4,8,128]{3,2,1,0:T(8,128)(2,1)} %get-tuple-element.15), calls=%async_computation.1 | async-start | bytes 1048576 | tf_op jit(solution)/shard_map/all_to_all | solution.py:377
  38.3 4.9 %collective-permute-start.1 = (f32[8,128]{1,0:T(8,128)S(1)}, f32[8,128]{1,0:T(8,128)S(1)}, u32[]{:S(2)}, u32[]{:S(2)}) collective-permute-start(f32[8,128]{1,0:T(8,128)S(1)} %get-tuple-element.14.inv_ref), channel_id=1, source_target_pairs={{8,16},{16,8},{24,32},{32,24},{40,48},{48,40},{56,64},{64,56},{72,... | collective-permute-start | bytes 12296 | tf_op jit(solution)/shard_map/ppermute | solution.py:378
  43.2 1.3 %own.1 = (bf16[256,128]{1,0:T(8,128)(2,1)S(1)}, bf16[2,256,128]{2,1,0:T(8,128)(2,1)S(1)}, bf16[4,256,128]{2,1,0:T(8,128)(2,1)S(1)}, f32[8,128]{1,0:T(8,128)S(1)}) custom-call(s32[5]{0:T(128)S(1)} %copy-done.7, s32[5]{0:T(128)S(1)} %copy-done.8, f32[2,5,128]{2,1,0:T(8,128)S(1)} %gains.1.gain_ref, f32[8,128]{1,0:T(8,128)S(1)} %get-tuple-element.14.inv_ref, ...), custom_call_target="tpu_custom_call" | custom-call | flops 10000000000 | bytes 10000000 | tf_op jit(solution)/shard_map/own/pallas_call | solution.py:379
  44.5 0.6 copy-done.9
  45.1 0.6 copy-done.14
  45.8 1.9 %collective-permute-start.2 = (bf16[4,256,128]{2,1,0:T(8,128)(2,1)S(1)}, bf16[4,256,128]{2,1,0:T(8,128)(2,1)S(1)}, u32[]{:S(2)}, u32[]{:S(2)}) collective-permute-start(bf16[4,256,128]{2,1,0:T(8,128)(2,1)S(1)} %get-tuple-element.18.halo_ref), channel_id=1, source_target_pairs={{0,8},{8,0},{16,24},{24,16},{32,40},{40,32},{48,56},{56,48},{64,72... | collective-permute-start | bytes 786440 | tf_op jit(solution)/shard_map/ppermute | solution.py:391
  47.7 4.9 %all-to-all-done.1.in_ref = bf16[64,4,8,128]{3,2,1,0:T(8,128)(2,1)S(1)} async-done(((bf16[64,4,8,128]{3,2,1,0:T(8,128)(2,1)}), bf16[64,4,8,128]{3,2,1,0:T(8,128)(2,1)S(1)}, u32[]{:S(2)}, u32[]{:S(2)}) %all-to-all-start.1) | async-done | bytes 524320 | tf_op jit(solution)/shard_map/all_to_all | solution.py:377
  52.6 2.5 %temporal.1 = bf16[64,3,8,128]{3,2,1,0:T(8,128)(2,1)} custom-call(bf16[64,4,8,128]{3,2,1,0:T(8,128)(2,1)S(1)} %all-to-all-done.1.in_ref, f32[8,128]{1,0:T(8,128)S(1)} %get-tuple-element.16.after_ref), custom_call_target="tpu_custom_call" | custom-call | flops 3000000000 | bytes 3000000 | tf_op jit(solution)/shard_map/temporal/pallas_call | solution.py:410
  55.0 9.1 %all-to-all-start.2 = ((bf16[64,3,8,128]{3,2,1,0:T(8,128)(2,1)}), bf16[64,3,8,128]{3,2,1,0:T(8,128)(2,1)S(1)}, u32[]{:S(2)}, u32[]{:S(2)}) async-start(bf16[64,3,8,128]{3,2,1,0:T(8,128)(2,1)} %temporal.1), calls=%async_computation.2 | async-start | bytes 786432 | tf_op jit(solution)/shard_map/all_to_all | solution.py:411
  64.2 2.7 %spatial.1 = (bf16[2,256,128]{2,1,0:T(8,128)(2,1)S(1)}, f32[4,256,128]{2,1,0:T(8,128)S(1)}, bf16[4,256,128]{2,1,0:T(8,128)(2,1)S(1)}, bf16[4,256,128]{2,1,0:T(8,128)(2,1)S(1)}, f32[8,256]{1,0:T(8,128)S(1)}) custom-call(s32[5]{0:T(128)S(1)} %copy-done.7, s32[5]{0:T(128)S(1)} %copy-done.8, s32[1]{0:T(128)} %bitcast.2.frame_ref, f32[2,5,128]{2,1,0:T(8,128)S(1)} %copy-done.18, ...), custom_call_target="tpu_custom_call" | custom-call | flops 6000000000 | bytes 6000000 | tf_op jit(solution)/shard_map/spatial/pallas_call | solution.py:392
  66.9 2.0 %collective-permute-start.3 = (bf16[4,256,128]{2,1,0:T(8,128)(2,1)S(1)}, bf16[4,256,128]{2,1,0:T(8,128)(2,1)S(1)}, u32[]{:S(2)}, u32[]{:S(2)}) collective-permute-start(bf16[4,256,128]{2,1,0:T(8,128)(2,1)S(1)} %get-tuple-element.22), channel_id=1, source_target_pairs={{0,8},{8,0},{16,24},{24,16},{32,40},{40,32},{48,56},{56,48},{64,72... | collective-permute-start | bytes 786440 | tf_op jit(solution)/shard_map/ppermute | solution.py:409
  69.0 5.1 %collective-permute-start.4 = (f32[8,256]{1,0:T(8,128)S(1)}, f32[8,256]{1,0:T(8,128)S(1)}, u32[]{:S(2)}, u32[]{:S(2)}) collective-permute-start(f32[8,256]{1,0:T(8,128)S(1)} %get-tuple-element.23), channel_id=1, source_target_pairs={{8,16},{16,8},{24,32},{32,24},{40,48},{48,40},{56,64},{64,56},{72,... | collective-permute-start | bytes 24584 | tf_op jit(solution)/shard_map/ppermute | solution.py:407
  74.1 4.3 %collective-permute-start.5 = (bf16[4,256,128]{2,1,0:T(8,128)(2,1)S(1)}, bf16[4,256,128]{2,1,0:T(8,128)(2,1)S(1)}, u32[]{:S(2)}, u32[]{:S(2)}) collective-permute-start(bf16[4,256,128]{2,1,0:T(8,128)(2,1)S(1)} %get-tuple-element.24), channel_id=1, source_target_pairs={{8,16},{16,8},{24,32},{32,24},{40,48},{48,40},{56,64},{64,56},{72,... | collective-permute-start | bytes 786440 | tf_op jit(solution)/shard_map/ppermute | solution.py:408
  78.5 0.7 spatial_sums.1.part_ref
  79.3 1.6 %inner.1 = f32[8,8,128]{2,1,0:T(8,128)} custom-call(s32[5]{0:T(128)S(1)} %copy-done.7, s32[5]{0:T(128)S(1)} %copy-done.8, f32[2,5,128]{2,1,0:T(8,128)S(1)} %copy-done.18, bf16[256,640]{1,0:T(8,128)(2,1)S(1)} %copy-done, bf16[256,640]{1,0:T(8,128)(2,1)S(1)} %copy-done.1, bf16[64,3,8,128]{3,2,1,0:T(8,128)(2,1)S(1)} %all-to-all-done.2.back_ref, ...), custom_call_target="tpu_custom_call" | custom-call | flops 2000000000 | bytes 2000000 | tf_op jit(solution)/shard_map/inner/pallas_call | solution.py:415
  80.8 3.6 %all-to-all-start.3 = ((f32[8,8,128]{2,1,0:T(8,128)}), f32[8,8,128]{2,1,0:T(8,128)S(1)}, u32[]{:S(2)}, u32[]{:S(2)}) async-start(f32[8,8,128]{2,1,0:T(8,128)} %inner.1), calls=%async_computation.3 | async-start | bytes 65536 | tf_op jit(solution)/shard_map/all_to_all | solution.py:418
  84.4 1.4 %collective-permute-done.5.far_ref = bf16[4,256,128]{2,1,0:T(8,128)(2,1)S(1)} collective-permute-done((bf16[4,256,128]{2,1,0:T(8,128)(2,1)S(1)}, bf16[4,256,128]{2,1,0:T(8,128)(2,1)S(1)}, u32[]{:S(2)}, u32[]{:S(2)}) %collective-permute-start.5) | collective-permute-done | bytes 262176 | tf_op jit(solution)/shard_map/ppermute | solution.py:408
  85.8 8.7 %all-to-all-done.3.inner_ref = f32[8,8,128]{2,1,0:T(8,128)S(1)} async-done(((f32[8,8,128]{2,1,0:T(8,128)}), f32[8,8,128]{2,1,0:T(8,128)S(1)}, u32[]{:S(2)}, u32[]{:S(2)}) %all-to-all-start.3) | async-done | bytes 32800 | tf_op jit(solution)/shard_map/all_to_all | solution.py:418
  94.6 1.8 %final.1 = (bf16[256,640]{1,0:T(8,128)(2,1)}, bf16[256,640]{1,0:T(8,128)(2,1)}, bf16[256,640]{1,0:T(8,128)(2,1)}) custom-call(s32[5]{0:T(128)S(1)} %copy-done.7, s32[5]{0:T(128)S(1)} %copy-done.8, f32[2,5,128]{2,1,0:T(8,128)S(1)} %copy-done.19, f32[8,128]{1,0:T(8,128)S(1)} %get-tuple-element.14.inv_ref, f32[8,8,128]{2,1,0:T(8,128)S(1)} %all-to-all-done.3.inner_ref, ...), custom_call_target="tpu_custom_call" | custom-call | flops 3000000000 | bytes 3000000 | tf_op jit(solution)/shard_map/final/pallas_call | solution.py:419
  (46 shorter events, 0.7 us)
Async XLA Ops:
  0.6 15.3 %copy-start.1 = (bf16[256,640]{1,0:T(8,128)(2,1)S(1)}, bf16[256,640]{1,0:T(8,128)(2,1)}, u32[]{:S(2)}) copy-start(bf16[256,640]{1,0:T(8,128)(2,1)} %k_ref.11) | copy-start | bytes 983044
  0.6 15.3 %copy-start.3 = (bf16[256,640]{1,0:T(8,128)(2,1)S(1)}, bf16[256,640]{1,0:T(8,128)(2,1)}, u32[]{:S(2)}) copy-start(bf16[256,640]{1,0:T(8,128)(2,1)} %v_ref.5) | copy-start | bytes 983044
  3.0 12.9 %copy-start.2 = (f32[8,8,128]{2,1,0:T(8,128)S(1)}, f32[8,8,128]{2,1,0:T(8,128)}, u32[]{:S(2)}) copy-start(f32[8,8,128]{2,1,0:T(8,128)} %squares.1.after_ref) | copy-start | bytes 98308
  3.1 12.9 %copy-start.7 = (s32[5]{0:T(128)S(1)}, s32[5]{0:T(128)}, u32[]{:S(2)}) copy-start(s32[5]{0:T(128)} %cls_ref.13) | copy-start | bytes 64
  3.1 12.9 %copy-start.8 = (s32[5]{0:T(128)S(1)}, s32[5]{0:T(128)}, u32[]{:S(2)}) copy-start(s32[5]{0:T(128)} %band_ref.13) | copy-start | bytes 64
  3.1 23.1 %all-to-all-start = ((f32[8,8,128]{2,1,0:T(8,128)}), f32[8,8,128]{2,1,0:T(8,128)S(1)}, u32[]{:S(2)}, u32[]{:S(2)}) async-start(f32[8,8,128]{2,1,0:T(8,128)} %squares.1.after_ref), calls=%async_computation | async-start | bytes 65536 | tf_op jit(solution)/shard_map/all_to_all | solution.py:369
  16.7 26.5 %collective-permute-start = (bf16[4,256,128]{2,1,0:T(8,128)(2,1)S(1)}, bf16[4,256,128]{2,1,0:T(8,128)(2,1)S(1)}, u32[]{:S(2)}, u32[]{:S(2)}) collective-permute-start(bf16[4,256,128]{2,1,0:T(8,128)(2,1)S(1)} %halo.1), channel_id=1, source_target_pairs={{8,16},{16,8},{24,32},{32,24},{40,48},{48,40},{56,64},{64,56},{72,... | collective-permute-start | bytes 786440 | tf_op jit(solution)/shard_map/ppermute | solution.py:365
  21.0 22.2 %copy-start.17 = (f32[2,5,128]{2,1,0:T(8,128)}, f32[2,5,128]{2,1,0:T(8,128)S(1)}, u32[]{:S(2)}) copy-start(f32[2,5,128]{2,1,0:T(8,128)S(1)} %gains.1.gain_ref) | copy-start | bytes 15364
  27.7 24.9 %all-to-all-start.1 = ((bf16[64,4,8,128]{3,2,1,0:T(8,128)(2,1)}), bf16[64,4,8,128]{3,2,1,0:T(8,128)(2,1)S(1)}, u32[]{:S(2)}, u32[]{:S(2)}) async-start(bf16[64,4,8,128]{3,2,1,0:T(8,128)(2,1)} %get-tuple-element.15), calls=%async_computation.1 | async-start | bytes 1048576 | tf_op jit(solution)/shard_map/all_to_all | solution.py:377
  38.3 25.9 %collective-permute-start.1 = (f32[8,128]{1,0:T(8,128)S(1)}, f32[8,128]{1,0:T(8,128)S(1)}, u32[]{:S(2)}, u32[]{:S(2)}) collective-permute-start(f32[8,128]{1,0:T(8,128)S(1)} %get-tuple-element.14.inv_ref), channel_id=1, source_target_pairs={{8,16},{16,8},{24,32},{32,24},{40,48},{48,40},{56,64},{64,56},{72,... | collective-permute-start | bytes 12296 | tf_op jit(solution)/shard_map/ppermute | solution.py:378
  45.8 18.4 %collective-permute-start.2 = (bf16[4,256,128]{2,1,0:T(8,128)(2,1)S(1)}, bf16[4,256,128]{2,1,0:T(8,128)(2,1)S(1)}, u32[]{:S(2)}, u32[]{:S(2)}) collective-permute-start(bf16[4,256,128]{2,1,0:T(8,128)(2,1)S(1)} %get-tuple-element.18.halo_ref), channel_id=1, source_target_pairs={{0,8},{8,0},{16,24},{24,16},{32,40},{40,32},{48,56},{56,48},{64,72... | collective-permute-start | bytes 786440 | tf_op jit(solution)/shard_map/ppermute | solution.py:391
  55.0 9.1 %copy-start.18 = (f32[2,5,128]{2,1,0:T(8,128)S(1)}, f32[2,5,128]{2,1,0:T(8,128)}, u32[]{:S(2)}) copy-start(f32[2,5,128]{2,1,0:T(8,128)} %copy-done.17) | copy-start | bytes 15364
  55.0 24.2 %all-to-all-start.2 = ((bf16[64,3,8,128]{3,2,1,0:T(8,128)(2,1)}), bf16[64,3,8,128]{3,2,1,0:T(8,128)(2,1)S(1)}, u32[]{:S(2)}, u32[]{:S(2)}) async-start(bf16[64,3,8,128]{3,2,1,0:T(8,128)(2,1)} %temporal.1), calls=%async_computation.2 | async-start | bytes 786432 | tf_op jit(solution)/shard_map/all_to_all | solution.py:411
  64.2 14.3 %copy-start.10 = (bf16[2,256,128]{2,1,0:T(8,128)(2,1)S(1)}, bf16[2,256,128]{2,1,0:T(8,128)(2,1)}, u32[]{:S(2)}) copy-start(bf16[2,256,128]{2,1,0:T(8,128)(2,1)} %copy-done.9) | copy-start | bytes 393220
  64.2 14.3 %copy-start.15 = (bf16[256,128]{1,0:T(8,128)(2,1)S(1)}, bf16[256,128]{1,0:T(8,128)(2,1)}, u32[]{:S(2)}) copy-start(bf16[256,128]{1,0:T(8,128)(2,1)} %copy-done.14) | copy-start | bytes 196612
  66.9 12.3 %copy-start.12 = (bf16[2,256,128]{2,1,0:T(8,128)(2,1)}, bf16[2,256,128]{2,1,0:T(8,128)(2,1)S(1)}, u32[]{:S(2)}) copy-start(bf16[2,256,128]{2,1,0:T(8,128)(2,1)S(1)} %get-tuple-element.19.dq_ref) | copy-start | bytes 393220
  66.9 11.5 %collective-permute-start.3 = (bf16[4,256,128]{2,1,0:T(8,128)(2,1)S(1)}, bf16[4,256,128]{2,1,0:T(8,128)(2,1)S(1)}, u32[]{:S(2)}, u32[]{:S(2)}) collective-permute-start(bf16[4,256,128]{2,1,0:T(8,128)(2,1)S(1)} %get-tuple-element.22), channel_id=1, source_target_pairs={{0,8},{8,0},{16,24},{24,16},{32,40},{40,32},{48,56},{56,48},{64,72... | collective-permute-start | bytes 786440 | tf_op jit(solution)/shard_map/ppermute | solution.py:409
  69.0 10.3 %collective-permute-start.4 = (f32[8,256]{1,0:T(8,128)S(1)}, f32[8,256]{1,0:T(8,128)S(1)}, u32[]{:S(2)}, u32[]{:S(2)}) collective-permute-start(f32[8,256]{1,0:T(8,128)S(1)} %get-tuple-element.23), channel_id=1, source_target_pairs={{8,16},{16,8},{24,32},{32,24},{40,48},{48,40},{56,64},{64,56},{72,... | collective-permute-start | bytes 24584 | tf_op jit(solution)/shard_map/ppermute | solution.py:407
  74.1 11.7 %collective-permute-start.5 = (bf16[4,256,128]{2,1,0:T(8,128)(2,1)S(1)}, bf16[4,256,128]{2,1,0:T(8,128)(2,1)S(1)}, u32[]{:S(2)}, u32[]{:S(2)}) collective-permute-start(bf16[4,256,128]{2,1,0:T(8,128)(2,1)S(1)} %get-tuple-element.24), channel_id=1, source_target_pairs={{8,16},{16,8},{24,32},{32,24},{40,48},{48,40},{56,64},{64,56},{72,... | collective-permute-start | bytes 786440 | tf_op jit(solution)/shard_map/ppermute | solution.py:408
  79.2 15.4 %copy-start.11 = (bf16[2,256,128]{2,1,0:T(8,128)(2,1)S(1)}, bf16[2,256,128]{2,1,0:T(8,128)(2,1)}, u32[]{:S(2)}) copy-start(bf16[2,256,128]{2,1,0:T(8,128)(2,1)} %copy-done.9) | copy-start | bytes 393220
  79.2 15.3 %copy-start.16 = (bf16[256,128]{1,0:T(8,128)(2,1)S(1)}, bf16[256,128]{1,0:T(8,128)(2,1)}, u32[]{:S(2)}) copy-start(bf16[256,128]{1,0:T(8,128)(2,1)} %copy-done.14) | copy-start | bytes 196612
  79.3 15.3 %copy-start.13 = (bf16[2,256,128]{2,1,0:T(8,128)(2,1)S(1)}, bf16[2,256,128]{2,1,0:T(8,128)(2,1)}, u32[]{:S(2)}) copy-start(bf16[2,256,128]{2,1,0:T(8,128)(2,1)} %copy-done.12) | copy-start | bytes 393220
  80.8 13.7 %copy-start.19 = (f32[2,5,128]{2,1,0:T(8,128)S(1)}, f32[2,5,128]{2,1,0:T(8,128)}, u32[]{:S(2)}) copy-start(f32[2,5,128]{2,1,0:T(8,128)} %copy-done.17) | copy-start | bytes 15364
  80.8 13.7 %all-to-all-start.3 = ((f32[8,8,128]{2,1,0:T(8,128)}), f32[8,8,128]{2,1,0:T(8,128)S(1)}, u32[]{:S(2)}, u32[]{:S(2)}) async-start(f32[8,8,128]{2,1,0:T(8,128)} %inner.1), calls=%async_computation.3 | async-start | bytes 65536 | tf_op jit(solution)/shard_map/all_to_all | solution.py:418
  (6 other events, 20.6 us)

commit v8 on v7

--- a/solution.py
+++ b/solution.py
@@ -69,10 +69,8 @@
     return pl.ds(pl.multiple_of(slot * HD, HD), HD)
 
 
-def dot_nt(a, b, precision=None):
-    return lax.dot_general(
-        a, b, (((1,), (1,)), ((), ())), preferred_element_type=F32, precision=precision
-    )
+def dot_nt(a, b):
+    return lax.dot_general(a, b, (((1,), (1,)), ((), ())), preferred_element_type=F32)
 
 
 def dot_tn(a, b):
@@ -99,7 +97,7 @@
 
 
 def lane_sums(values):
-    return dot_nt(jnp.ones((8, HD), F32), values, lax.Precision.HIGHEST)
+    return jnp.broadcast_to(jnp.sum(values.T, axis=0, keepdims=True), (8, values.shape[0]))
 
 
 def inverses(sums_ref):
@@ -251,7 +249,7 @@
     q, k, v, g = (in_ref[:, a].reshape(rows, HD) for a in range(4))
     d_k = jnp.zeros((rows, HD), F32)
     d_v = jnp.zeros((rows, HD), F32)
-    step = 256
+    step = 512
     for part in range(rows // step):
         q_part, g_part = q[part * step : (part + 1) * step], g[part * step : (part + 1) * step]
         key_tile = lax.broadcasted_iota(jnp.int32, (rows, step), 0) & 4
@@ -271,7 +269,18 @@
 
 
 def spatial_sums_body(
-    cls_ref, band_ref, gain_ref, q_ref, k_ref, dq0_ref, dq_ref, fin_ref, own_ref, near_ref, part_ref
+    cls_ref,
+    band_ref,
+    gain_ref,
+    q_ref,
+    k_ref,
+    dq0_ref,
+    dq_ref,
+    fin_ref,
+    own_ref,
+    tick_ref,
+    near_ref,
+    part_ref,
 ):
     slots, _ = head_slots(cls_ref, band_ref)
     q_total = product(gain_ref, 0, slots[0], dq0_ref[...], q_ref)
@@ -280,20 +289,19 @@
         at = 2 * s - 2
         q_total += product(gain_ref, 0, slots[s], dq_ref[s - 1], q_ref)
         k_total += product(gain_ref, 1, slots[s], own_ref[at] + near_ref[at].astype(F32), k_ref)
-    part_ref[0] = q_total
-    part_ref[1] = k_total
-
-
-def inner_body(cls_ref, band_ref, gain_ref, q_ref, k_ref, back_ref, part_ref, tick_ref, out_ref):
+    part_ref[0] = lane_sums(q_total)
+    part_ref[1] = lane_sums(k_total) + tick_ref[...]
+
+
+def inner_body(cls_ref, band_ref, gain_ref, q_ref, k_ref, back_ref, part_ref, out_ref):
     slots, _ = head_slots(cls_ref, band_ref)
     sums = []
     for which, ref in enumerate((q_ref, k_ref)):
-        total = part_ref[which]
+        total = jnp.zeros((TOK, HD), F32)
         for s in range(2):
             grad = back_ref[s * 32 : (s + 1) * 32, which].reshape(TOK, HD)
             total += product(gain_ref, which, slots[3 + s], grad, ref)
-        sums.append(lane_sums(total))
-    sums[1] += tick_ref[...]
+        sums.append(lane_sums(total) + part_ref[which])
     out_ref[...] = jnp.broadcast_to(rows_of(*sums)[None], (8, 8, HD))
 
 
@@ -410,10 +418,10 @@
     grads = call(temporal_body, shape((FRAMES, 3, 8, HD), BF), [VM, ANY], "temporal", 3)(held, done)
     back = lax.all_to_all(grads, "seq", 0, 0, tiled=True)
     part = call(
-        spatial_sums_body, shape((2, TOK, HD), F32), [SM, SM] + [VM] * 8, "spatial_sums", 3
-    )(head_class, head_band, gains, query_pre, key_pre, dq0, dq, fin, own, from_near)
-    inner = call(inner_body, shape((8, 8, HD), F32), [SM, SM] + [VM] * 6, "inner", 2)(
-        head_class, head_band, gains, query_pre, key_pre, back, part, tick
+        spatial_sums_body, shape((2, 8, TOK), F32), [SM, SM] + [VM] * 9, "spatial_sums", 3
+    )(head_class, head_band, gains, query_pre, key_pre, dq0, dq, fin, own, tick, from_near)
+    inner = call(inner_body, shape((8, 8, HD), F32), [SM, SM] + [VM] * 5, "inner", 2)(
+        head_class, head_band, gains, query_pre, key_pre, back, part
     )
     inner = lax.all_to_all(inner, "head", 0, 0, tiled=True)
     return call(

time: 97.1 us -> 96.7 us (level)
  Pallas kernels: 15 us -> 14 us
where the time goes in v8:
time: 96.7 us; the launch traced here: 96 us
  starting transfers between devices  58.7 us (61%)
  waiting for transfers between devices  20.2 us (21%)
  Pallas kernels  14 us (14%)
  local copies, waits for them, and re-layouts  2.02 us (2%)
  between operations  1 us (1%)
    all_to_all x1, starting transfers between devices, per_device(): sums = lax.all_to_all(sums, 'head', 0, 0, tiled=True)  12.9 us
    all_to_all x1, starting transfers between devices, per_device(): held = lax.all_to_all(send, 'seq', 0, 0, tiled=True)  10.6 us
    all_to_all x1, waiting for transfers between devices, per_device(): inner = lax.all_to_all(inner, 'head', 0, 0, tiled=True)  9.2 us
    all_to_all x1, starting transfers between devices, per_device(): back = lax.all_to_all(grads, 'seq', 0, 0, tiled=True)  9.1 us
    all_to_all x1, waiting for transfers between devices, per_device(): sums = lax.all_to_all(sums, 'head', 0, 0, tiled=True)  5.15 us
    ppermute x1, starting transfers between devices, per_device(): tick = lax.ppermute(tick, 'seq', chip)  5.12 us
    all_to_all x1, waiting for transfers between devices, per_device(): held = lax.all_to_all(send, 'seq', 0, 0, tiled=True)  4.91 us
    ppermute x1, starting transfers between devices, per_device(): inv_far = lax.ppermute(inv, 'seq', chip)  4.91 us
  transfers between devices with their start and end apart: 10, of which 4 were waited for; matrix products, arithmetic and copies ran while one was open for 0% of the time, Pallas kernels for 11%

profile of v8, /device:TPU:32, one launch (start us, length us, event | category | flops | bytes accessed | tf_op | source)
XLA Modules:
  0.0 96.0 jit_solution(2421668641986070855)
XLA Ops:
  0.7 1.9 %squares.1.after_ref = f32[8,8,128]{2,1,0:T(8,128)} custom-call(bf16[256,640]{1,0:T(8,128)(2,1)} %q_ref.11, bf16[256,640]{1,0:T(8,128)(2,1)} %k_ref.11), custom_call_target="tpu_custom_call" | custom-call | tf_op jit(solution)/shard_map/squares/pallas_call | solution.py:361
  2.6 12.9 %all-to-all-start = ((f32[8,8,128]{2,1,0:T(8,128)}), f32[8,8,128]{2,1,0:T(8,128)S(1)}, u32[]{:S(2)}, u32[]{:S(2)}) async-start(f32[8,8,128]{2,1,0:T(8,128)} %squares.1.after_ref), calls=%async_computation | async-start | bytes 65536 | tf_op jit(solution)/shard_map/all_to_all | solution.py:377
  16.2 4.2 %collective-permute-start = (bf16[4,256,128]{2,1,0:T(8,128)(2,1)S(1)}, bf16[4,256,128]{2,1,0:T(8,128)(2,1)S(1)}, u32[]{:S(2)}, u32[]{:S(2)}) collective-permute-start(bf16[4,256,128]{2,1,0:T(8,128)(2,1)S(1)} %halo.1), channel_id=1, source_target_pairs={{8,16},{16,8},{24,32},{32,24},{40,48},{48,40},{56,64},{64,56},{72,... | collective-permute-start | bytes 786440 | tf_op jit(solution)/shard_map/ppermute | solution.py:373
  20.5 5.2 %all-to-all-done.sums_ref = f32[8,8,128]{2,1,0:T(8,128)S(1)} async-done(((f32[8,8,128]{2,1,0:T(8,128)}), f32[8,8,128]{2,1,0:T(8,128)S(1)}, u32[]{:S(2)}, u32[]{:S(2)}) %all-to-all-start) | async-done | bytes 32800 | tf_op jit(solution)/shard_map/all_to_all | solution.py:377
  25.7 1.5 %norm.1 = (bf16[64,4,8,128]{3,2,1,0:T(8,128)(2,1)}, f32[8,128]{1,0:T(8,128)S(1)}) custom-call(s32[5]{0:T(128)S(1)} %copy-done.7, s32[5]{0:T(128)S(1)} %copy-done.8, f32[8,8,128]{2,1,0:T(8,128)S(1)} %all-to-all-done.sums_ref, f32[2,5,128]{2,1,0:T(8,128)S(1)} %gains.1.gain_ref, bf16[256,640]{1,0:T(8,128)(2,1)S(1)} %copy-done, bf16[256,640]{1,0:T(8,128)(2,1)S(1)} %copy-done.1, ...), custom_call_target="tpu_custom_call" | custom-call | flops 2000000000 | bytes 2000000 | tf_op jit(solution)/shard_map/norm/pallas_call | solution.py:378
  27.2 10.6 %all-to-all-start.1 = ((bf16[64,4,8,128]{3,2,1,0:T(8,128)(2,1)}), bf16[64,4,8,128]{3,2,1,0:T(8,128)(2,1)S(1)}, u32[]{:S(2)}, u32[]{:S(2)}) async-start(bf16[64,4,8,128]{3,2,1,0:T(8,128)(2,1)} %get-tuple-element.15), calls=%async_computation.1 | async-start | bytes 1048576 | tf_op jit(solution)/shard_map/all_to_all | solution.py:385
  37.8 4.9 %collective-permute-start.1 = (f32[8,128]{1,0:T(8,128)S(1)}, f32[8,128]{1,0:T(8,128)S(1)}, u32[]{:S(2)}, u32[]{:S(2)}) collective-permute-start(f32[8,128]{1,0:T(8,128)S(1)} %get-tuple-element.14.inv_ref), channel_id=1, source_target_pairs={{8,16},{16,8},{24,32},{32,24},{40,48},{48,40},{56,64},{64,56},{72,... | collective-permute-start | bytes 12296 | tf_op jit(solution)/shard_map/ppermute | solution.py:386
  42.8 1.3 %own.1 = (bf16[256,128]{1,0:T(8,128)(2,1)S(1)}, bf16[2,256,128]{2,1,0:T(8,128)(2,1)S(1)}, bf16[4,256,128]{2,1,0:T(8,128)(2,1)S(1)}, f32[8,128]{1,0:T(8,128)S(1)}) custom-call(s32[5]{0:T(128)S(1)} %copy-done.7, s32[5]{0:T(128)S(1)} %copy-done.8, f32[2,5,128]{2,1,0:T(8,128)S(1)} %gains.1.gain_ref, f32[8,128]{1,0:T(8,128)S(1)} %get-tuple-element.14.inv_ref, ...), custom_call_target="tpu_custom_call" | custom-call | flops 10000000000 | bytes 10000000 | tf_op jit(solution)/shard_map/own/pallas_call | solution.py:387
  44.0 0.6 copy-done.9
  45.3 1.9 %collective-permute-start.2 = (bf16[4,256,128]{2,1,0:T(8,128)(2,1)S(1)}, bf16[4,256,128]{2,1,0:T(8,128)(2,1)S(1)}, u32[]{:S(2)}, u32[]{:S(2)}) collective-permute-start(bf16[4,256,128]{2,1,0:T(8,128)(2,1)S(1)} %get-tuple-element.18.halo_ref), channel_id=1, source_target_pairs={{0,8},{8,0},{16,24},{24,16},{32,40},{40,32},{48,56},{56,48},{64,72... | collective-permute-start | bytes 786440 | tf_op jit(solution)/shard_map/ppermute | solution.py:399
  47.2 4.9 %all-to-all-done.1.in_ref = bf16[64,4,8,128]{3,2,1,0:T(8,128)(2,1)S(1)} async-done(((bf16[64,4,8,128]{3,2,1,0:T(8,128)(2,1)}), bf16[64,4,8,128]{3,2,1,0:T(8,128)(2,1)S(1)}, u32[]{:S(2)}, u32[]{:S(2)}) %all-to-all-start.1) | async-done | bytes 524320 | tf_op jit(solution)/shard_map/all_to_all | solution.py:385
  52.1 2.2 %temporal.1 = bf16[64,3,8,128]{3,2,1,0:T(8,128)(2,1)} custom-call(bf16[64,4,8,128]{3,2,1,0:T(8,128)(2,1)S(1)} %all-to-all-done.1.in_ref, f32[8,128]{1,0:T(8,128)S(1)} %get-tuple-element.16.after_ref), custom_call_target="tpu_custom_call" | custom-call | flops 3000000000 | bytes 3000000 | tf_op jit(solution)/shard_map/temporal/pallas_call | solution.py:418
  54.3 9.1 %all-to-all-start.2 = ((bf16[64,3,8,128]{3,2,1,0:T(8,128)(2,1)}), bf16[64,3,8,128]{3,2,1,0:T(8,128)(2,1)S(1)}, u32[]{:S(2)}, u32[]{:S(2)}) async-start(bf16[64,3,8,128]{3,2,1,0:T(8,128)(2,1)} %temporal.1), calls=%async_computation.2 | async-start | bytes 786432 | tf_op jit(solution)/shard_map/all_to_all | solution.py:419
  63.5 2.6 %spatial.1 = (bf16[2,256,128]{2,1,0:T(8,128)(2,1)S(1)}, f32[4,256,128]{2,1,0:T(8,128)S(1)}, bf16[4,256,128]{2,1,0:T(8,128)(2,1)S(1)}, bf16[4,256,128]{2,1,0:T(8,128)(2,1)S(1)}, f32[8,256]{1,0:T(8,128)S(1)}) custom-call(s32[5]{0:T(128)S(1)} %copy-done.7, s32[5]{0:T(128)S(1)} %copy-done.8, s32[1]{0:T(128)} %bitcast.2.frame_ref, f32[2,5,128]{2,1,0:T(8,128)S(1)} %copy-done.18, ...), custom_call_target="tpu_custom_call" | custom-call | flops 6000000000 | bytes 6000000 | tf_op jit(solution)/shard_map/spatial/pallas_call | solution.py:400
  66.1 2.1 %collective-permute-start.4 = (bf16[4,256,128]{2,1,0:T(8,128)(2,1)S(1)}, bf16[4,256,128]{2,1,0:T(8,128)(2,1)S(1)}, u32[]{:S(2)}, u32[]{:S(2)}) collective-permute-start(bf16[4,256,128]{2,1,0:T(8,128)(2,1)S(1)} %get-tuple-element.23), channel_id=1, source_target_pairs={{0,8},{8,0},{16,24},{24,16},{32,40},{40,32},{48,56},{56,48},{64,72... | collective-permute-start | bytes 786440 | tf_op jit(solution)/shard_map/ppermute | solution.py:417
  68.1 5.1 %collective-permute-start.3 = (f32[8,256]{1,0:T(8,128)S(1)}, f32[8,256]{1,0:T(8,128)S(1)}, u32[]{:S(2)}, u32[]{:S(2)}) collective-permute-start(f32[8,256]{1,0:T(8,128)S(1)} %get-tuple-element.22), channel_id=1, source_target_pairs={{8,16},{16,8},{24,32},{32,24},{40,48},{48,40},{56,64},{64,56},{72,... | collective-permute-start | bytes 24584 | tf_op jit(solution)/shard_map/ppermute | solution.py:415
  73.3 4.3 %collective-permute-start.5 = (bf16[4,256,128]{2,1,0:T(8,128)(2,1)S(1)}, bf16[4,256,128]{2,1,0:T(8,128)(2,1)S(1)}, u32[]{:S(2)}, u32[]{:S(2)}) collective-permute-start(bf16[4,256,128]{2,1,0:T(8,128)(2,1)S(1)} %get-tuple-element.24), channel_id=1, source_target_pairs={{8,16},{16,8},{24,32},{32,24},{40,48},{48,40},{56,64},{64,56},{72,... | collective-permute-start | bytes 786440 | tf_op jit(solution)/shard_map/ppermute | solution.py:416
  77.6 0.8 spatial_sums.1.part_ref
  78.4 0.6 copy-done.12
  79.1 1.3 %inner.1 = f32[8,8,128]{2,1,0:T(8,128)} custom-call(s32[5]{0:T(128)S(1)} %copy-done.7, s32[5]{0:T(128)S(1)} %copy-done.8, f32[2,5,128]{2,1,0:T(8,128)S(1)} %copy-done.18, bf16[256,640]{1,0:T(8,128)(2,1)S(1)} %copy-done, bf16[256,640]{1,0:T(8,128)(2,1)S(1)} %copy-done.1, bf16[64,3,8,128]{3,2,1,0:T(8,128)(2,1)S(1)} %all-to-all-done.2.back_ref, ...), custom_call_target="tpu_custom_call" | custom-call | flops 2000000000 | bytes 2000000 | tf_op jit(solution)/shard_map/inner/pallas_call | solution.py:423
  80.4 3.6 %all-to-all-start.3 = ((f32[8,8,128]{2,1,0:T(8,128)}), f32[8,8,128]{2,1,0:T(8,128)S(1)}, u32[]{:S(2)}, u32[]{:S(2)}) async-start(f32[8,8,128]{2,1,0:T(8,128)} %inner.1), calls=%async_computation.3 | async-start | bytes 65536 | tf_op jit(solution)/shard_map/all_to_all | solution.py:426
  84.0 1.0 %collective-permute-done.5.far_ref = bf16[4,256,128]{2,1,0:T(8,128)(2,1)S(1)} collective-permute-done((bf16[4,256,128]{2,1,0:T(8,128)(2,1)S(1)}, bf16[4,256,128]{2,1,0:T(8,128)(2,1)S(1)}, u32[]{:S(2)}, u32[]{:S(2)}) %collective-permute-start.5) | collective-permute-done | bytes 262176 | tf_op jit(solution)/shard_map/ppermute | solution.py:416
  84.9 9.2 %all-to-all-done.3.inner_ref = f32[8,8,128]{2,1,0:T(8,128)S(1)} async-done(((f32[8,8,128]{2,1,0:T(8,128)}), f32[8,8,128]{2,1,0:T(8,128)S(1)}, u32[]{:S(2)}, u32[]{:S(2)}) %all-to-all-start.3) | async-done | bytes 32800 | tf_op jit(solution)/shard_map/all_to_all | solution.py:426
  94.2 1.8 %final.1 = (bf16[256,640]{1,0:T(8,128)(2,1)}, bf16[256,640]{1,0:T(8,128)(2,1)}, bf16[256,640]{1,0:T(8,128)(2,1)}) custom-call(s32[5]{0:T(128)S(1)} %copy-done.7, s32[5]{0:T(128)S(1)} %copy-done.8, f32[2,5,128]{2,1,0:T(8,128)S(1)} %copy-done.19, f32[8,128]{1,0:T(8,128)S(1)} %get-tuple-element.14.inv_ref, f32[8,8,128]{2,1,0:T(8,128)S(1)} %all-to-all-done.3.inner_ref, ...), custom_call_target="tpu_custom_call" | custom-call | flops 3000000000 | bytes 3000000 | tf_op jit(solution)/shard_map/final/pallas_call | solution.py:427
  (46 shorter events, 1.4 us)
Async XLA Ops:
  0.6 14.9 %copy-start.1 = (bf16[256,640]{1,0:T(8,128)(2,1)S(1)}, bf16[256,640]{1,0:T(8,128)(2,1)}, u32[]{:S(2)}) copy-start(bf16[256,640]{1,0:T(8,128)(2,1)} %k_ref.11) | copy-start | bytes 983044
  0.6 14.9 %copy-start.3 = (bf16[256,640]{1,0:T(8,128)(2,1)S(1)}, bf16[256,640]{1,0:T(8,128)(2,1)}, u32[]{:S(2)}) copy-start(bf16[256,640]{1,0:T(8,128)(2,1)} %v_ref.5) | copy-start | bytes 983044
  2.6 12.9 %copy-start.2 = (f32[8,8,128]{2,1,0:T(8,128)S(1)}, f32[8,8,128]{2,1,0:T(8,128)}, u32[]{:S(2)}) copy-start(f32[8,8,128]{2,1,0:T(8,128)} %squares.1.after_ref) | copy-start | bytes 98308
  2.6 12.9 %copy-start.7 = (s32[5]{0:T(128)S(1)}, s32[5]{0:T(128)}, u32[]{:S(2)}) copy-start(s32[5]{0:T(128)} %cls_ref.13) | copy-start | bytes 64
  2.6 12.9 %copy-start.8 = (s32[5]{0:T(128)S(1)}, s32[5]{0:T(128)}, u32[]{:S(2)}) copy-start(s32[5]{0:T(128)} %band_ref.13) | copy-start | bytes 64
  2.6 23.1 %all-to-all-start = ((f32[8,8,128]{2,1,0:T(8,128)}), f32[8,8,128]{2,1,0:T(8,128)S(1)}, u32[]{:S(2)}, u32[]{:S(2)}) async-start(f32[8,8,128]{2,1,0:T(8,128)} %squares.1.after_ref), calls=%async_computation | async-start | bytes 65536 | tf_op jit(solution)/shard_map/all_to_all | solution.py:377
  16.2 26.5 %collective-permute-start = (bf16[4,256,128]{2,1,0:T(8,128)(2,1)S(1)}, bf16[4,256,128]{2,1,0:T(8,128)(2,1)S(1)}, u32[]{:S(2)}, u32[]{:S(2)}) collective-permute-start(bf16[4,256,128]{2,1,0:T(8,128)(2,1)S(1)} %halo.1), channel_id=1, source_target_pairs={{8,16},{16,8},{24,32},{32,24},{40,48},{48,40},{56,64},{64,56},{72,... | collective-permute-start | bytes 786440 | tf_op jit(solution)/shard_map/ppermute | solution.py:373
  20.5 5.2 %copy-start = (bf16[256,640]{1,0:T(8,128)(2,1)S(1)}, bf16[256,640]{1,0:T(8,128)(2,1)}, u32[]{:S(2)}) copy-start(bf16[256,640]{1,0:T(8,128)(2,1)} %q_ref.11) | copy-start | bytes 983044
  20.5 22.2 %copy-start.17 = (f32[2,5,128]{2,1,0:T(8,128)}, f32[2,5,128]{2,1,0:T(8,128)S(1)}, u32[]{:S(2)}) copy-start(f32[2,5,128]{2,1,0:T(8,128)S(1)} %gains.1.gain_ref) | copy-start | bytes 15364
  27.2 24.9 %all-to-all-start.1 = ((bf16[64,4,8,128]{3,2,1,0:T(8,128)(2,1)}), bf16[64,4,8,128]{3,2,1,0:T(8,128)(2,1)S(1)}, u32[]{:S(2)}, u32[]{:S(2)}) async-start(bf16[64,4,8,128]{3,2,1,0:T(8,128)(2,1)} %get-tuple-element.15), calls=%async_computation.1 | async-start | bytes 1048576 | tf_op jit(solution)/shard_map/all_to_all | solution.py:385
  37.8 25.6 %collective-permute-start.1 = (f32[8,128]{1,0:T(8,128)S(1)}, f32[8,128]{1,0:T(8,128)S(1)}, u32[]{:S(2)}, u32[]{:S(2)}) collective-permute-start(f32[8,128]{1,0:T(8,128)S(1)} %get-tuple-element.14.inv_ref), channel_id=1, source_target_pairs={{8,16},{16,8},{24,32},{32,24},{40,48},{48,40},{56,64},{64,56},{72,... | collective-permute-start | bytes 12296 | tf_op jit(solution)/shard_map/ppermute | solution.py:386
  45.3 18.1 %collective-permute-start.2 = (bf16[4,256,128]{2,1,0:T(8,128)(2,1)S(1)}, bf16[4,256,128]{2,1,0:T(8,128)(2,1)S(1)}, u32[]{:S(2)}, u32[]{:S(2)}) collective-permute-start(bf16[4,256,128]{2,1,0:T(8,128)(2,1)S(1)} %get-tuple-element.18.halo_ref), channel_id=1, source_target_pairs={{0,8},{8,0},{16,24},{24,16},{32,40},{40,32},{48,56},{56,48},{64,72... | collective-permute-start | bytes 786440 | tf_op jit(solution)/shard_map/ppermute | solution.py:399
  54.3 9.1 %copy-start.18 = (f32[2,5,128]{2,1,0:T(8,128)S(1)}, f32[2,5,128]{2,1,0:T(8,128)}, u32[]{:S(2)}) copy-start(f32[2,5,128]{2,1,0:T(8,128)} %copy-done.17) | copy-start | bytes 15364
  54.3 24.8 %all-to-all-start.2 = ((bf16[64,3,8,128]{3,2,1,0:T(8,128)(2,1)}), bf16[64,3,8,128]{3,2,1,0:T(8,128)(2,1)S(1)}, u32[]{:S(2)}, u32[]{:S(2)}) async-start(bf16[64,3,8,128]{3,2,1,0:T(8,128)(2,1)} %temporal.1), calls=%async_computation.2 | async-start | bytes 786432 | tf_op jit(solution)/shard_map/all_to_all | solution.py:419
  63.5 14.2 %copy-start.10 = (bf16[2,256,128]{2,1,0:T(8,128)(2,1)S(1)}, bf16[2,256,128]{2,1,0:T(8,128)(2,1)}, u32[]{:S(2)}) copy-start(bf16[2,256,128]{2,1,0:T(8,128)(2,1)} %copy-done.9) | copy-start | bytes 393220
  63.5 14.2 %copy-start.15 = (bf16[256,128]{1,0:T(8,128)(2,1)S(1)}, bf16[256,128]{1,0:T(8,128)(2,1)}, u32[]{:S(2)}) copy-start(bf16[256,128]{1,0:T(8,128)(2,1)} %copy-done.14) | copy-start | bytes 196612
  66.1 11.6 %collective-permute-start.4 = (bf16[4,256,128]{2,1,0:T(8,128)(2,1)S(1)}, bf16[4,256,128]{2,1,0:T(8,128)(2,1)S(1)}, u32[]{:S(2)}, u32[]{:S(2)}) collective-permute-start(bf16[4,256,128]{2,1,0:T(8,128)(2,1)S(1)} %get-tuple-element.23), channel_id=1, source_target_pairs={{0,8},{8,0},{16,24},{24,16},{32,40},{40,32},{48,56},{56,48},{64,72... | collective-permute-start | bytes 786440 | tf_op jit(solution)/shard_map/ppermute | solution.py:417
  68.1 9.5 %collective-permute-start.3 = (f32[8,256]{1,0:T(8,128)S(1)}, f32[8,256]{1,0:T(8,128)S(1)}, u32[]{:S(2)}, u32[]{:S(2)}) collective-permute-start(f32[8,256]{1,0:T(8,128)S(1)} %get-tuple-element.22), channel_id=1, source_target_pairs={{8,16},{16,8},{24,32},{32,24},{40,48},{48,40},{56,64},{64,56},{72,... | collective-permute-start | bytes 24584 | tf_op jit(solution)/shard_map/ppermute | solution.py:415
  73.3 11.7 %collective-permute-start.5 = (bf16[4,256,128]{2,1,0:T(8,128)(2,1)S(1)}, bf16[4,256,128]{2,1,0:T(8,128)(2,1)S(1)}, u32[]{:S(2)}, u32[]{:S(2)}) collective-permute-start(bf16[4,256,128]{2,1,0:T(8,128)(2,1)S(1)} %get-tuple-element.24), channel_id=1, source_target_pairs={{8,16},{16,8},{24,32},{32,24},{40,48},{48,40},{56,64},{64,56},{72,... | collective-permute-start | bytes 786440 | tf_op jit(solution)/shard_map/ppermute | solution.py:416
  79.1 15.1 %copy-start.11 = (bf16[2,256,128]{2,1,0:T(8,128)(2,1)S(1)}, bf16[2,256,128]{2,1,0:T(8,128)(2,1)}, u32[]{:S(2)}) copy-start(bf16[2,256,128]{2,1,0:T(8,128)(2,1)} %copy-done.9) | copy-start | bytes 393220
  79.1 15.1 %copy-start.16 = (bf16[256,128]{1,0:T(8,128)(2,1)S(1)}, bf16[256,128]{1,0:T(8,128)(2,1)}, u32[]{:S(2)}) copy-start(bf16[256,128]{1,0:T(8,128)(2,1)} %copy-done.14) | copy-start | bytes 196612
  79.1 15.1 %copy-start.13 = (bf16[2,256,128]{2,1,0:T(8,128)(2,1)S(1)}, bf16[2,256,128]{2,1,0:T(8,128)(2,1)}, u32[]{:S(2)}) copy-start(bf16[2,256,128]{2,1,0:T(8,128)(2,1)} %copy-done.12) | copy-start | bytes 393220
  80.4 13.7 %copy-start.19 = (f32[2,5,128]{2,1,0:T(8,128)S(1)}, f32[2,5,128]{2,1,0:T(8,128)}, u32[]{:S(2)}) copy-start(f32[2,5,128]{2,1,0:T(8,128)} %copy-done.17) | copy-start | bytes 15364
  80.4 13.7 %all-to-all-start.3 = ((f32[8,8,128]{2,1,0:T(8,128)}), f32[8,8,128]{2,1,0:T(8,128)S(1)}, u32[]{:S(2)}, u32[]{:S(2)}) async-start(f32[8,8,128]{2,1,0:T(8,128)} %inner.1), calls=%async_computation.3 | async-start | bytes 65536 | tf_op jit(solution)/shard_map/all_to_all | solution.py:426
  (6 other events, 16.1 us)

commit v9 on v8

--- a/solution.py
+++ b/solution.py
@@ -129,7 +129,7 @@
         halo_ref[2 * s - 1] = v_ref[:, columns(slots[s])]
 
 
-def gains_body(q_ref, k_ref, after_ref, g_ref, out_ref):
+def gains_body(q_ref, k_ref, after_ref, next_ref, g_ref, out_ref):
     out_ref[0] = q_ref[...].astype(F32)
     out_ref[1] = k_ref[...].astype(F32)
 
@@ -371,8 +371,8 @@
         head_class, head_band, sums, key_pre, value
     )
     far = lax.ppermute(halo, "seq", chip)
-    gains = call(gains_body, shape((2, HEADS_DEV, HD), F32), [VM, VM, ANY, VM], "gains", 8)(
-        gain_q.reshape(HEADS_DEV, HD), gain_k.reshape(HEADS_DEV, HD), sums, d_out
+    gains = call(gains_body, shape((2, HEADS_DEV, HD), F32), [VM, VM, ANY, VM, VM], "gains", 8)(
+        gain_q.reshape(HEADS_DEV, HD), gain_k.reshape(HEADS_DEV, HD), sums, query_pre, d_out
     )
     sums = lax.all_to_all(sums, "head", 0, 0, tiled=True)
     send, inv = call(

time: 96.7 us -> 96.5 us (level)
  no operation moved by 1% of the time
where the time goes in v9:
time: 96.5 us; the launch traced here: 95.8 us
  starting transfers between devices  58.6 us (61%)
  waiting for transfers between devices  20.2 us (21%)
  Pallas kernels  14 us (15%)
  local copies, waits for them, and re-layouts  2.02 us (2%)
  between operations  1.01 us (1%)
    all_to_all x1, starting transfers between devices, per_device(): sums = lax.all_to_all(sums, 'head', 0, 0, tiled=True)  12.9 us
    all_to_all x1, starting transfers between devices, per_device(): held = lax.all_to_all(send, 'seq', 0, 0, tiled=True)  10.6 us
    all_to_all x1, starting transfers between devices, per_device(): back = lax.all_to_all(grads, 'seq', 0, 0, tiled=True)  9.11 us
    all_to_all x1, waiting for transfers between devices, per_device(): inner = lax.all_to_all(inner, 'head', 0, 0, tiled=True)  9.03 us
    all_to_all x1, waiting for transfers between devices, per_device(): sums = lax.all_to_all(sums, 'head', 0, 0, tiled=True)  5.14 us
    ppermute x1, starting transfers between devices, per_device(): tick = lax.ppermute(tick, 'seq', chip)  5.12 us
    all_to_all x1, waiting for transfers between devices, per_device(): held = lax.all_to_all(send, 'seq', 0, 0, tiled=True)  4.91 us
    ppermute x1, starting transfers between devices, per_device(): inv_far = lax.ppermute(inv, 'seq', chip)  4.91 us
  transfers between devices with their start and end apart: 10, of which 4 were waited for; matrix products, arithmetic and copies ran while one was open for 0% of the time, Pallas kernels for 11%

profile of v9, /device:TPU:32, one launch (start us, length us, event | category | flops | bytes accessed | tf_op | source)
XLA Modules:
  0.0 95.8 jit_solution(4062764077670981626)
XLA Ops:
  0.7 1.9 %squares.1.after_ref = f32[8,8,128]{2,1,0:T(8,128)} custom-call(bf16[256,640]{1,0:T(8,128)(2,1)} %q_ref.11, bf16[256,640]{1,0:T(8,128)(2,1)} %k_ref.11), custom_call_target="tpu_custom_call" | custom-call | tf_op jit(solution)/shard_map/squares/pallas_call | solution.py:361
  2.6 12.9 %all-to-all-start = ((f32[8,8,128]{2,1,0:T(8,128)}), f32[8,8,128]{2,1,0:T(8,128)S(1)}, u32[]{:S(2)}, u32[]{:S(2)}) async-start(f32[8,8,128]{2,1,0:T(8,128)} %squares.1.after_ref), calls=%async_computation | async-start | bytes 65536 | tf_op jit(solution)/shard_map/all_to_all | solution.py:377
  16.2 4.2 %collective-permute-start = (bf16[4,256,128]{2,1,0:T(8,128)(2,1)S(1)}, bf16[4,256,128]{2,1,0:T(8,128)(2,1)S(1)}, u32[]{:S(2)}, u32[]{:S(2)}) collective-permute-start(bf16[4,256,128]{2,1,0:T(8,128)(2,1)S(1)} %halo.1), channel_id=1, source_target_pairs={{8,16},{16,8},{24,32},{32,24},{40,48},{48,40},{56,64},{64,56},{72,... | collective-permute-start | bytes 786440 | tf_op jit(solution)/shard_map/ppermute | solution.py:373
  20.6 5.1 %all-to-all-done.sums_ref = f32[8,8,128]{2,1,0:T(8,128)S(1)} async-done(((f32[8,8,128]{2,1,0:T(8,128)}), f32[8,8,128]{2,1,0:T(8,128)S(1)}, u32[]{:S(2)}, u32[]{:S(2)}) %all-to-all-start) | async-done | bytes 32800 | tf_op jit(solution)/shard_map/all_to_all | solution.py:377
  25.7 1.5 %norm.1 = (bf16[64,4,8,128]{3,2,1,0:T(8,128)(2,1)}, f32[8,128]{1,0:T(8,128)S(1)}) custom-call(s32[5]{0:T(128)S(1)} %copy-done.7, s32[5]{0:T(128)S(1)} %copy-done.8, f32[8,8,128]{2,1,0:T(8,128)S(1)} %all-to-all-done.sums_ref, f32[2,5,128]{2,1,0:T(8,128)S(1)} %gains.1.gain_ref, bf16[256,640]{1,0:T(8,128)(2,1)S(1)} %copy-done, bf16[256,640]{1,0:T(8,128)(2,1)S(1)} %copy-done.1, ...), custom_call_target="tpu_custom_call" | custom-call | flops 2000000000 | bytes 2000000 | tf_op jit(solution)/shard_map/norm/pallas_call | solution.py:378
  27.2 10.6 %all-to-all-start.1 = ((bf16[64,4,8,128]{3,2,1,0:T(8,128)(2,1)}), bf16[64,4,8,128]{3,2,1,0:T(8,128)(2,1)S(1)}, u32[]{:S(2)}, u32[]{:S(2)}) async-start(bf16[64,4,8,128]{3,2,1,0:T(8,128)(2,1)} %get-tuple-element.15), calls=%async_computation.1 | async-start | bytes 1048576 | tf_op jit(solution)/shard_map/all_to_all | solution.py:385
  37.8 4.9 %collective-permute-start.1 = (f32[8,128]{1,0:T(8,128)S(1)}, f32[8,128]{1,0:T(8,128)S(1)}, u32[]{:S(2)}, u32[]{:S(2)}) collective-permute-start(f32[8,128]{1,0:T(8,128)S(1)} %get-tuple-element.14.inv_ref), channel_id=1, source_target_pairs={{8,16},{16,8},{24,32},{32,24},{40,48},{48,40},{56,64},{64,56},{72,... | collective-permute-start | bytes 12296 | tf_op jit(solution)/shard_map/ppermute | solution.py:386
  42.8 1.3 %own.1 = (bf16[256,128]{1,0:T(8,128)(2,1)S(1)}, bf16[2,256,128]{2,1,0:T(8,128)(2,1)S(1)}, bf16[4,256,128]{2,1,0:T(8,128)(2,1)S(1)}, f32[8,128]{1,0:T(8,128)S(1)}) custom-call(s32[5]{0:T(128)S(1)} %copy-done.7, s32[5]{0:T(128)S(1)} %copy-done.8, f32[2,5,128]{2,1,0:T(8,128)S(1)} %gains.1.gain_ref, f32[8,128]{1,0:T(8,128)S(1)} %get-tuple-element.14.inv_ref, ...), custom_call_target="tpu_custom_call" | custom-call | flops 10000000000 | bytes 10000000 | tf_op jit(solution)/shard_map/own/pallas_call | solution.py:387
  44.0 0.6 copy-done.9
  45.3 1.9 %collective-permute-start.2 = (bf16[4,256,128]{2,1,0:T(8,128)(2,1)S(1)}, bf16[4,256,128]{2,1,0:T(8,128)(2,1)S(1)}, u32[]{:S(2)}, u32[]{:S(2)}) collective-permute-start(bf16[4,256,128]{2,1,0:T(8,128)(2,1)S(1)} %get-tuple-element.18.halo_ref), channel_id=1, source_target_pairs={{0,8},{8,0},{16,24},{24,16},{32,40},{40,32},{48,56},{56,48},{64,72... | collective-permute-start | bytes 786440 | tf_op jit(solution)/shard_map/ppermute | solution.py:399
  47.2 4.9 %all-to-all-done.1.in_ref = bf16[64,4,8,128]{3,2,1,0:T(8,128)(2,1)S(1)} async-done(((bf16[64,4,8,128]{3,2,1,0:T(8,128)(2,1)}), bf16[64,4,8,128]{3,2,1,0:T(8,128)(2,1)S(1)}, u32[]{:S(2)}, u32[]{:S(2)}) %all-to-all-start.1) | async-done | bytes 524320 | tf_op jit(solution)/shard_map/all_to_all | solution.py:385
  52.1 2.2 %temporal.1 = bf16[64,3,8,128]{3,2,1,0:T(8,128)(2,1)} custom-call(bf16[64,4,8,128]{3,2,1,0:T(8,128)(2,1)S(1)} %all-to-all-done.1.in_ref, f32[8,128]{1,0:T(8,128)S(1)} %get-tuple-element.16.after_ref), custom_call_target="tpu_custom_call" | custom-call | flops 3000000000 | bytes 3000000 | tf_op jit(solution)/shard_map/temporal/pallas_call | solution.py:418
  54.3 9.1 %all-to-all-start.2 = ((bf16[64,3,8,128]{3,2,1,0:T(8,128)(2,1)}), bf16[64,3,8,128]{3,2,1,0:T(8,128)(2,1)S(1)}, u32[]{:S(2)}, u32[]{:S(2)}) async-start(bf16[64,3,8,128]{3,2,1,0:T(8,128)(2,1)} %temporal.1), calls=%async_computation.2 | async-start | bytes 786432 | tf_op jit(solution)/shard_map/all_to_all | solution.py:419
  63.5 2.6 %spatial.1 = (bf16[2,256,128]{2,1,0:T(8,128)(2,1)S(1)}, f32[4,256,128]{2,1,0:T(8,128)S(1)}, bf16[4,256,128]{2,1,0:T(8,128)(2,1)S(1)}, bf16[4,256,128]{2,1,0:T(8,128)(2,1)S(1)}, f32[8,256]{1,0:T(8,128)S(1)}) custom-call(s32[5]{0:T(128)S(1)} %copy-done.7, s32[5]{0:T(128)S(1)} %copy-done.8, s32[1]{0:T(128)} %bitcast.2.frame_ref, f32[2,5,128]{2,1,0:T(8,128)S(1)} %copy-done.18, ...), custom_call_target="tpu_custom_call" | custom-call | flops 6000000000 | bytes 6000000 | tf_op jit(solution)/shard_map/spatial/pallas_call | solution.py:400
  66.1 2.1 %collective-permute-start.4 = (bf16[4,256,128]{2,1,0:T(8,128)(2,1)S(1)}, bf16[4,256,128]{2,1,0:T(8,128)(2,1)S(1)}, u32[]{:S(2)}, u32[]{:S(2)}) collective-permute-start(bf16[4,256,128]{2,1,0:T(8,128)(2,1)S(1)} %get-tuple-element.23), channel_id=1, source_target_pairs={{0,8},{8,0},{16,24},{24,16},{32,40},{40,32},{48,56},{56,48},{64,72... | collective-permute-start | bytes 786440 | tf_op jit(solution)/shard_map/ppermute | solution.py:417
  68.1 5.1 %collective-permute-start.3 = (f32[8,256]{1,0:T(8,128)S(1)}, f32[8,256]{1,0:T(8,128)S(1)}, u32[]{:S(2)}, u32[]{:S(2)}) collective-permute-start(f32[8,256]{1,0:T(8,128)S(1)} %get-tuple-element.22), channel_id=1, source_target_pairs={{8,16},{16,8},{24,32},{32,24},{40,48},{48,40},{56,64},{64,56},{72,... | collective-permute-start | bytes 24584 | tf_op jit(solution)/shard_map/ppermute | solution.py:415
  73.3 4.3 %collective-permute-start.5 = (bf16[4,256,128]{2,1,0:T(8,128)(2,1)S(1)}, bf16[4,256,128]{2,1,0:T(8,128)(2,1)S(1)}, u32[]{:S(2)}, u32[]{:S(2)}) collective-permute-start(bf16[4,256,128]{2,1,0:T(8,128)(2,1)S(1)} %get-tuple-element.24), channel_id=1, source_target_pairs={{8,16},{16,8},{24,32},{32,24},{40,48},{48,40},{56,64},{64,56},{72,... | collective-permute-start | bytes 786440 | tf_op jit(solution)/shard_map/ppermute | solution.py:416
  77.6 0.8 spatial_sums.1.part_ref
  78.4 0.6 copy-done.12
  79.1 1.3 %inner.1 = f32[8,8,128]{2,1,0:T(8,128)} custom-call(s32[5]{0:T(128)S(1)} %copy-done.7, s32[5]{0:T(128)S(1)} %copy-done.8, f32[2,5,128]{2,1,0:T(8,128)S(1)} %copy-done.18, bf16[256,640]{1,0:T(8,128)(2,1)S(1)} %copy-done, bf16[256,640]{1,0:T(8,128)(2,1)S(1)} %copy-done.1, bf16[64,3,8,128]{3,2,1,0:T(8,128)(2,1)S(1)} %all-to-all-done.2.back_ref, ...), custom_call_target="tpu_custom_call" | custom-call | flops 2000000000 | bytes 2000000 | tf_op jit(solution)/shard_map/inner/pallas_call | solution.py:423
  80.4 3.5 %all-to-all-start.3 = ((f32[8,8,128]{2,1,0:T(8,128)}), f32[8,8,128]{2,1,0:T(8,128)S(1)}, u32[]{:S(2)}, u32[]{:S(2)}) async-start(f32[8,8,128]{2,1,0:T(8,128)} %inner.1), calls=%async_computation.3 | async-start | bytes 65536 | tf_op jit(solution)/shard_map/all_to_all | solution.py:426
  83.9 1.1 %collective-permute-done.5.far_ref = bf16[4,256,128]{2,1,0:T(8,128)(2,1)S(1)} collective-permute-done((bf16[4,256,128]{2,1,0:T(8,128)(2,1)S(1)}, bf16[4,256,128]{2,1,0:T(8,128)(2,1)S(1)}, u32[]{:S(2)}, u32[]{:S(2)}) %collective-permute-start.5) | collective-permute-done | bytes 262176 | tf_op jit(solution)/shard_map/ppermute | solution.py:416
  84.9 9.0 %all-to-all-done.3.inner_ref = f32[8,8,128]{2,1,0:T(8,128)S(1)} async-done(((f32[8,8,128]{2,1,0:T(8,128)}), f32[8,8,128]{2,1,0:T(8,128)S(1)}, u32[]{:S(2)}, u32[]{:S(2)}) %all-to-all-start.3) | async-done | bytes 32800 | tf_op jit(solution)/shard_map/all_to_all | solution.py:426
  94.0 1.8 %final.1 = (bf16[256,640]{1,0:T(8,128)(2,1)}, bf16[256,640]{1,0:T(8,128)(2,1)}, bf16[256,640]{1,0:T(8,128)(2,1)}) custom-call(s32[5]{0:T(128)S(1)} %copy-done.7, s32[5]{0:T(128)S(1)} %copy-done.8, f32[2,5,128]{2,1,0:T(8,128)S(1)} %copy-done.19, f32[8,128]{1,0:T(8,128)S(1)} %get-tuple-element.14.inv_ref, f32[8,8,128]{2,1,0:T(8,128)S(1)} %all-to-all-done.3.inner_ref, ...), custom_call_target="tpu_custom_call" | custom-call | flops 3000000000 | bytes 3000000 | tf_op jit(solution)/shard_map/final/pallas_call | solution.py:427
  (46 shorter events, 1.4 us)
Async XLA Ops:
  0.6 14.9 %copy-start.1 = (bf16[256,640]{1,0:T(8,128)(2,1)S(1)}, bf16[256,640]{1,0:T(8,128)(2,1)}, u32[]{:S(2)}) copy-start(bf16[256,640]{1,0:T(8,128)(2,1)} %k_ref.11) | copy-start | bytes 983044
  0.6 14.9 %copy-start.3 = (bf16[256,640]{1,0:T(8,128)(2,1)S(1)}, bf16[256,640]{1,0:T(8,128)(2,1)}, u32[]{:S(2)}) copy-start(bf16[256,640]{1,0:T(8,128)(2,1)} %v_ref.5) | copy-start | bytes 983044
  2.6 12.9 %copy-start.2 = (f32[8,8,128]{2,1,0:T(8,128)S(1)}, f32[8,8,128]{2,1,0:T(8,128)}, u32[]{:S(2)}) copy-start(f32[8,8,128]{2,1,0:T(8,128)} %squares.1.after_ref) | copy-start | bytes 98308
  2.6 12.9 %copy-start.7 = (s32[5]{0:T(128)S(1)}, s32[5]{0:T(128)}, u32[]{:S(2)}) copy-start(s32[5]{0:T(128)} %cls_ref.13) | copy-start | bytes 64
  2.6 12.9 %copy-start.8 = (s32[5]{0:T(128)S(1)}, s32[5]{0:T(128)}, u32[]{:S(2)}) copy-start(s32[5]{0:T(128)} %band_ref.13) | copy-start | bytes 64
  2.6 23.1 %all-to-all-start = ((f32[8,8,128]{2,1,0:T(8,128)}), f32[8,8,128]{2,1,0:T(8,128)S(1)}, u32[]{:S(2)}, u32[]{:S(2)}) async-start(f32[8,8,128]{2,1,0:T(8,128)} %squares.1.after_ref), calls=%async_computation | async-start | bytes 65536 | tf_op jit(solution)/shard_map/all_to_all | solution.py:377
  15.6 4.9 %copy-start = (bf16[256,640]{1,0:T(8,128)(2,1)S(1)}, bf16[256,640]{1,0:T(8,128)(2,1)}, u32[]{:S(2)}) copy-start(bf16[256,640]{1,0:T(8,128)(2,1)} %q_ref.11) | copy-start | bytes 983044
  16.2 26.5 %collective-permute-start = (bf16[4,256,128]{2,1,0:T(8,128)(2,1)S(1)}, bf16[4,256,128]{2,1,0:T(8,128)(2,1)S(1)}, u32[]{:S(2)}, u32[]{:S(2)}) collective-permute-start(bf16[4,256,128]{2,1,0:T(8,128)(2,1)S(1)} %halo.1), channel_id=1, source_target_pairs={{8,16},{16,8},{24,32},{32,24},{40,48},{48,40},{56,64},{64,56},{72,... | collective-permute-start | bytes 786440 | tf_op jit(solution)/shard_map/ppermute | solution.py:373
  20.5 22.2 %copy-start.17 = (f32[2,5,128]{2,1,0:T(8,128)}, f32[2,5,128]{2,1,0:T(8,128)S(1)}, u32[]{:S(2)}) copy-start(f32[2,5,128]{2,1,0:T(8,128)S(1)} %gains.1.gain_ref) | copy-start | bytes 15364
  27.2 24.9 %all-to-all-start.1 = ((bf16[64,4,8,128]{3,2,1,0:T(8,128)(2,1)}), bf16[64,4,8,128]{3,2,1,0:T(8,128)(2,1)S(1)}, u32[]{:S(2)}, u32[]{:S(2)}) async-start(bf16[64,4,8,128]{3,2,1,0:T(8,128)(2,1)} %get-tuple-element.15), calls=%async_computation.1 | async-start | bytes 1048576 | tf_op jit(solution)/shard_map/all_to_all | solution.py:385
  37.8 25.6 %collective-permute-start.1 = (f32[8,128]{1,0:T(8,128)S(1)}, f32[8,128]{1,0:T(8,128)S(1)}, u32[]{:S(2)}, u32[]{:S(2)}) collective-permute-start(f32[8,128]{1,0:T(8,128)S(1)} %get-tuple-element.14.inv_ref), channel_id=1, source_target_pairs={{8,16},{16,8},{24,32},{32,24},{40,48},{48,40},{56,64},{64,56},{72,... | collective-permute-start | bytes 12296 | tf_op jit(solution)/shard_map/ppermute | solution.py:386
  45.3 18.1 %collective-permute-start.2 = (bf16[4,256,128]{2,1,0:T(8,128)(2,1)S(1)}, bf16[4,256,128]{2,1,0:T(8,128)(2,1)S(1)}, u32[]{:S(2)}, u32[]{:S(2)}) collective-permute-start(bf16[4,256,128]{2,1,0:T(8,128)(2,1)S(1)} %get-tuple-element.18.halo_ref), channel_id=1, source_target_pairs={{0,8},{8,0},{16,24},{24,16},{32,40},{40,32},{48,56},{56,48},{64,72... | collective-permute-start | bytes 786440 | tf_op jit(solution)/shard_map/ppermute | solution.py:399
  54.3 9.1 %copy-start.18 = (f32[2,5,128]{2,1,0:T(8,128)S(1)}, f32[2,5,128]{2,1,0:T(8,128)}, u32[]{:S(2)}) copy-start(f32[2,5,128]{2,1,0:T(8,128)} %copy-done.17) | copy-start | bytes 15364
  54.3 24.8 %all-to-all-start.2 = ((bf16[64,3,8,128]{3,2,1,0:T(8,128)(2,1)}), bf16[64,3,8,128]{3,2,1,0:T(8,128)(2,1)S(1)}, u32[]{:S(2)}, u32[]{:S(2)}) async-start(bf16[64,3,8,128]{3,2,1,0:T(8,128)(2,1)} %temporal.1), calls=%async_computation.2 | async-start | bytes 786432 | tf_op jit(solution)/shard_map/all_to_all | solution.py:419
  63.5 14.2 %copy-start.10 = (bf16[2,256,128]{2,1,0:T(8,128)(2,1)S(1)}, bf16[2,256,128]{2,1,0:T(8,128)(2,1)}, u32[]{:S(2)}) copy-start(bf16[2,256,128]{2,1,0:T(8,128)(2,1)} %copy-done.9) | copy-start | bytes 393220
  63.5 14.2 %copy-start.15 = (bf16[256,128]{1,0:T(8,128)(2,1)S(1)}, bf16[256,128]{1,0:T(8,128)(2,1)}, u32[]{:S(2)}) copy-start(bf16[256,128]{1,0:T(8,128)(2,1)} %copy-done.14) | copy-start | bytes 196612
  66.1 11.6 %collective-permute-start.4 = (bf16[4,256,128]{2,1,0:T(8,128)(2,1)S(1)}, bf16[4,256,128]{2,1,0:T(8,128)(2,1)S(1)}, u32[]{:S(2)}, u32[]{:S(2)}) collective-permute-start(bf16[4,256,128]{2,1,0:T(8,128)(2,1)S(1)} %get-tuple-element.23), channel_id=1, source_target_pairs={{0,8},{8,0},{16,24},{24,16},{32,40},{40,32},{48,56},{56,48},{64,72... | collective-permute-start | bytes 786440 | tf_op jit(solution)/shard_map/ppermute | solution.py:417
  68.1 9.5 %collective-permute-start.3 = (f32[8,256]{1,0:T(8,128)S(1)}, f32[8,256]{1,0:T(8,128)S(1)}, u32[]{:S(2)}, u32[]{:S(2)}) collective-permute-start(f32[8,256]{1,0:T(8,128)S(1)} %get-tuple-element.22), channel_id=1, source_target_pairs={{8,16},{16,8},{24,32},{32,24},{40,48},{48,40},{56,64},{64,56},{72,... | collective-permute-start | bytes 24584 | tf_op jit(solution)/shard_map/ppermute | solution.py:415
  73.3 11.7 %collective-permute-start.5 = (bf16[4,256,128]{2,1,0:T(8,128)(2,1)S(1)}, bf16[4,256,128]{2,1,0:T(8,128)(2,1)S(1)}, u32[]{:S(2)}, u32[]{:S(2)}) collective-permute-start(bf16[4,256,128]{2,1,0:T(8,128)(2,1)S(1)} %get-tuple-element.24), channel_id=1, source_target_pairs={{8,16},{16,8},{24,32},{32,24},{40,48},{48,40},{56,64},{64,56},{72,... | collective-permute-start | bytes 786440 | tf_op jit(solution)/shard_map/ppermute | solution.py:416
  79.1 14.9 %copy-start.11 = (bf16[2,256,128]{2,1,0:T(8,128)(2,1)S(1)}, bf16[2,256,128]{2,1,0:T(8,128)(2,1)}, u32[]{:S(2)}) copy-start(bf16[2,256,128]{2,1,0:T(8,128)(2,1)} %copy-done.9) | copy-start | bytes 393220
  79.1 14.9 %copy-start.16 = (bf16[256,128]{1,0:T(8,128)(2,1)S(1)}, bf16[256,128]{1,0:T(8,128)(2,1)}, u32[]{:S(2)}) copy-start(bf16[256,128]{1,0:T(8,128)(2,1)} %copy-done.14) | copy-start | bytes 196612
  79.1 14.9 %copy-start.13 = (bf16[2,256,128]{2,1,0:T(8,128)(2,1)S(1)}, bf16[2,256,128]{2,1,0:T(8,128)(2,1)}, u32[]{:S(2)}) copy-start(bf16[2,256,128]{2,1,0:T(8,128)(2,1)} %copy-done.12) | copy-start | bytes 393220
  80.4 13.6 %copy-start.19 = (f32[2,5,128]{2,1,0:T(8,128)S(1)}, f32[2,5,128]{2,1,0:T(8,128)}, u32[]{:S(2)}) copy-start(f32[2,5,128]{2,1,0:T(8,128)} %copy-done.17) | copy-start | bytes 15364
  80.4 13.6 %all-to-all-start.3 = ((f32[8,8,128]{2,1,0:T(8,128)}), f32[8,8,128]{2,1,0:T(8,128)S(1)}, u32[]{:S(2)}, u32[]{:S(2)}) async-start(f32[8,8,128]{2,1,0:T(8,128)} %inner.1), calls=%async_computation.3 | async-start | bytes 65536 | tf_op jit(solution)/shard_map/all_to_all | solution.py:426
  (6 other events, 16.1 us)

commit v10 on v9

--- a/solution.py
+++ b/solution.py
@@ -139,23 +139,42 @@
 
 
 def norm_body(
-    cls_ref, band_ref, sums_ref, gain_ref, q_ref, k_ref, v_ref, g_ref, send_ref, inv_ref
+    cls_ref,
+    band_ref,
+    sums_ref,
+    gain_ref,
+    q_ref,
+    k_ref,
+    v_ref,
+    g_ref,
+    send_hbm,
+    inv_ref,
+    part_ref,
+    sems,
 ):
     slots, _ = head_slots(cls_ref, band_ref)
+    copies = []
+
+    def ship(a, s, part):
+        part_ref[2 * a + s] = part.reshape(32, 8, HD)
+        target = send_hbm.at[s * 32 : (s + 1) * 32, a]
+        copy = pltpu.make_async_copy(part_ref.at[2 * a + s], target, sems.at[2 * a + s])
+        copy.start()
+        copies.append(copy)
+
+    for s in range(2):
+        at = columns(slots[3 + s])
+        ship(2, s, v_ref[:, at])
+        ship(3, s, g_ref[:, at])
     inv = inverses(sums_ref)
     inv_ref[...] = inv
-    q_inv, k_inv = spread(inv, 0), spread(inv, 2)
-    for s in range(2):
-        slot = slots[3 + s]
-        at = columns(slot)
-        parts = (
-            normed(q_ref[:, at], q_inv, gain_ref[0, pl.ds(slot, 1), :]),
-            normed(k_ref[:, at], k_inv, gain_ref[1, pl.ds(slot, 1), :]),
-            v_ref[:, at],
-            g_ref[:, at],
-        )
-        for a, part in enumerate(parts):
-            send_ref[s * 32 : (s + 1) * 32, a] = part.reshape(32, 8, HD)
+    for a, ref in enumerate((q_ref, k_ref)):
+        inverse = spread(inv, 2 * a)
+        for s in range(2):
+            slot = slots[3 + s]
+            ship(a, s, normed(ref[:, columns(slot)], inverse, gain_ref[a, pl.ds(slot, 1), :]))
+    for copy in copies:
+        copy.wait()
 
 
 def attend(q, g, keys, values, allowed):
@@ -244,23 +263,20 @@
     tick_ref[...] = lane_sums(far_total)
 
 
-def temporal_body(in_ref, after_ref, out_ref):
+def temporal_body(in_ref, after_ref, out_hbm, part_ref, sems):
     rows = FRAMES * 8
     q, k, v, g = (in_ref[:, a].reshape(rows, HD) for a in range(4))
-    d_k = jnp.zeros((rows, HD), F32)
-    d_v = jnp.zeros((rows, HD), F32)
-    step = 512
-    for part in range(rows // step):
-        q_part, g_part = q[part * step : (part + 1) * step], g[part * step : (part + 1) * step]
-        key_tile = lax.broadcasted_iota(jnp.int32, (rows, step), 0) & 4
-        query_tile = lax.broadcasted_iota(jnp.int32, (rows, step), 1) & 4
-        d_q, d_keys, d_values = attend(q_part, g_part, [k], [v], [key_tile == query_tile])
-        frames = step // 8
-        out_ref[part * frames : (part + 1) * frames, 0] = d_q.astype(BF).reshape(frames, 8, HD)
-        d_k += d_keys[0]
-        d_v += d_values[0]
-    out_ref[:, 1] = d_k.astype(BF).reshape(FRAMES, 8, HD)
-    out_ref[:, 2] = d_v.astype(BF).reshape(FRAMES, 8, HD)
+    key_tile = lax.broadcasted_iota(jnp.int32, (rows, rows), 0) & 4
+    query_tile = lax.broadcasted_iota(jnp.int32, (rows, rows), 1) & 4
+    d_q, d_k, d_v = attend(q, g, [k], [v], [key_tile == query_tile])
+    copies = []
+    for a, part in ((2, d_v[0]), (1, d_k[0]), (0, d_q)):
+        part_ref[a] = part.astype(BF).reshape(FRAMES, 8, HD)
+        copy = pltpu.make_async_copy(part_ref.at[a], out_hbm.at[:, a], sems.at[a])
+        copy.start()
+        copies.append(copy)
+    for copy in copies:
+        copy.wait()
 
 
 def product(gain_ref, which, slot, grad, ref):
@@ -375,12 +391,17 @@
         gain_q.reshape(HEADS_DEV, HD), gain_k.reshape(HEADS_DEV, HD), sums, query_pre, d_out
     )
     sums = lax.all_to_all(sums, "head", 0, 0, tiled=True)
-    send, inv = call(
+    send, inv = pl.pallas_call(
         norm_body,
-        (shape((FRAMES, 4, 8, HD), BF), shape((8, HD), F32)),
-        [SM, SM] + [VM] * 6,
-        "norm",
-        2,
+        out_shape=(shape((FRAMES, 4, 8, HD), BF), shape((8, HD), F32)),
+        in_specs=[SM, SM] + [VM] * 6,
+        out_specs=(ANY, VM),
+        scratch_shapes=[pltpu.VMEM((8, 32, 8, HD), BF), pltpu.SemaphoreType.DMA((8,))],
+        name="norm",
+        compiler_params=pltpu.CompilerParams(vmem_limit_bytes=24 << 20),
+        cost_estimate=pl.CostEstimate(
+            flops=int(2e9), bytes_accessed=int(2e6), transcendentals=0
+        ),
     )(head_class, head_band, sums, gains, query_pre, key_pre, value, d_out)
     held = lax.all_to_all(send, "seq", 0, 0, tiled=True)
     inv_far = lax.ppermute(inv, "seq", chip)
@@ -415,7 +436,18 @@
     tick = lax.ppermute(tick, "seq", chip)
     from_far = lax.ppermute(to_far, "seq", chip)
     from_near = lax.ppermute(to_near, "seq", core)
-    grads = call(temporal_body, shape((FRAMES, 3, 8, HD), BF), [VM, ANY], "temporal", 3)(held, done)
+    grads = pl.pallas_call(
+        temporal_body,
+        out_shape=shape((FRAMES, 3, 8, HD), BF),
+        in_specs=[VM, ANY],
+        out_specs=ANY,
+        scratch_shapes=[pltpu.VMEM((3, FRAMES, 8, HD), BF), pltpu.SemaphoreType.DMA((3,))],
+        name="temporal",
+        compiler_params=pltpu.CompilerParams(vmem_limit_bytes=24 << 20),
+        cost_estimate=pl.CostEstimate(
+            flops=int(3e9), bytes_accessed=int(3e6), transcendentals=0
+        ),
+    )(held, done)
     back = lax.all_to_all(grads, "seq", 0, 0, tiled=True)
     part = call(
         spatial_sums_body, shape((2, 8, TOK), F32), [SM, SM] + [VM] * 9, "spatial_sums", 3

time: 96.5 us -> 96.4 us (level)
  no operation moved by 1% of the time
where the time goes in v10:
time: 96.4 us; the launch traced here: 95.7 us
  starting transfers between devices  58.5 us (61%)
  waiting for transfers between devices  20.2 us (21%)
  Pallas kernels  14 us (15%)
  local copies, waits for them, and re-layouts  2.02 us (2%)
  between operations  1.04 us (1%)
    all_to_all x1, starting transfers between devices, per_device(): sums = lax.all_to_all(sums, 'head', 0, 0, tiled=True)  12.9 us
    all_to_all x1, starting transfers between devices, per_device(): held = lax.all_to_all(send, 'seq', 0, 0, tiled=True)  10.6 us
    all_to_all x1, waiting for transfers between devices, per_device(): inner = lax.all_to_all(inner, 'head', 0, 0, tiled=True)  9.03 us
    all_to_all x1, starting transfers between devices, per_device(): back = lax.all_to_all(grads, 'seq', 0, 0, tiled=True)  8.99 us
    all_to_all x1, waiting for transfers between devices, per_device(): sums = lax.all_to_all(sums, 'head', 0, 0, tiled=True)  5.14 us
    ppermute x1, starting transfers between devices, per_device(): tick = lax.ppermute(tick, 'seq', chip)  5.12 us
    all_to_all x1, waiting for transfers between devices, per_device(): held = lax.all_to_all(send, 'seq', 0, 0, tiled=True)  4.91 us
    ppermute x1, starting transfers between devices, per_device(): inv_far = lax.ppermute(inv, 'seq', chip)  4.91 us
  transfers between devices with their start and end apart: 10, of which 4 were waited for; matrix products, arithmetic and copies ran while one was open for 0% of the time, Pallas kernels for 11%

profile of v10, /device:TPU:32, one launch (start us, length us, event | category | flops | bytes accessed | tf_op | source)
XLA Modules:
  0.0 95.7 jit_solution(4453004266601555089)
XLA Ops:
  0.7 1.9 %squares.1.after_ref = f32[8,8,128]{2,1,0:T(8,128)} custom-call(bf16[256,640]{1,0:T(8,128)(2,1)} %q_ref.11, bf16[256,640]{1,0:T(8,128)(2,1)} %k_ref.11), custom_call_target="tpu_custom_call" | custom-call | tf_op jit(solution)/shard_map/squares/pallas_call | solution.py:377
  2.6 12.9 %all-to-all-start = ((f32[8,8,128]{2,1,0:T(8,128)}), f32[8,8,128]{2,1,0:T(8,128)S(1)}, u32[]{:S(2)}, u32[]{:S(2)}) async-start(f32[8,8,128]{2,1,0:T(8,128)} %squares.1.after_ref), calls=%async_computation | async-start | bytes 65536 | tf_op jit(solution)/shard_map/all_to_all | solution.py:393
  16.2 4.2 %collective-permute-start = (bf16[4,256,128]{2,1,0:T(8,128)(2,1)S(1)}, bf16[4,256,128]{2,1,0:T(8,128)(2,1)S(1)}, u32[]{:S(2)}, u32[]{:S(2)}) collective-permute-start(bf16[4,256,128]{2,1,0:T(8,128)(2,1)S(1)} %halo.1), channel_id=1, source_target_pairs={{8,16},{16,8},{24,32},{32,24},{40,48},{48,40},{56,64},{64,56},{72,... | collective-permute-start | bytes 786440 | tf_op jit(solution)/shard_map/ppermute | solution.py:389
  20.6 5.1 %all-to-all-done.sums_ref = f32[8,8,128]{2,1,0:T(8,128)S(1)} async-done(((f32[8,8,128]{2,1,0:T(8,128)}), f32[8,8,128]{2,1,0:T(8,128)S(1)}, u32[]{:S(2)}, u32[]{:S(2)}) %all-to-all-start) | async-done | bytes 32800 | tf_op jit(solution)/shard_map/all_to_all | solution.py:393
  25.7 1.5 %norm.1 = (bf16[64,4,8,128]{3,2,1,0:T(8,128)(2,1)}, f32[8,128]{1,0:T(8,128)S(1)}) custom-call(s32[5]{0:T(128)S(1)} %copy-done.7, s32[5]{0:T(128)S(1)} %copy-done.8, f32[8,8,128]{2,1,0:T(8,128)S(1)} %all-to-all-done.sums_ref, f32[2,5,128]{2,1,0:T(8,128)S(1)} %gains.1.gain_ref, bf16[256,640]{1,0:T(8,128)(2,1)S(1)} %copy-done, bf16[256,640]{1,0:T(8,128)(2,1)S(1)} %copy-done.1, ...), custom_call_target="tpu_custom_call" | custom-call | flops 2000000000 | bytes 2000000 | tf_op jit(solution)/shard_map/norm/pallas_call | solution.py:394
  27.2 10.6 %all-to-all-start.1 = ((bf16[64,4,8,128]{3,2,1,0:T(8,128)(2,1)}), bf16[64,4,8,128]{3,2,1,0:T(8,128)(2,1)S(1)}, u32[]{:S(2)}, u32[]{:S(2)}) async-start(bf16[64,4,8,128]{3,2,1,0:T(8,128)(2,1)} %get-tuple-element.15), calls=%async_computation.1 | async-start | bytes 1048576 | tf_op jit(solution)/shard_map/all_to_all | solution.py:406
  37.8 4.9 %collective-permute-start.1 = (f32[8,128]{1,0:T(8,128)S(1)}, f32[8,128]{1,0:T(8,128)S(1)}, u32[]{:S(2)}, u32[]{:S(2)}) collective-permute-start(f32[8,128]{1,0:T(8,128)S(1)} %get-tuple-element.14.inv_ref), channel_id=1, source_target_pairs={{8,16},{16,8},{24,32},{32,24},{40,48},{48,40},{56,64},{64,56},{72,... | collective-permute-start | bytes 12296 | tf_op jit(solution)/shard_map/ppermute | solution.py:407
  42.7 1.3 %own.1 = (bf16[256,128]{1,0:T(8,128)(2,1)S(1)}, bf16[2,256,128]{2,1,0:T(8,128)(2,1)S(1)}, bf16[4,256,128]{2,1,0:T(8,128)(2,1)S(1)}, f32[8,128]{1,0:T(8,128)S(1)}) custom-call(s32[5]{0:T(128)S(1)} %copy-done.7, s32[5]{0:T(128)S(1)} %copy-done.8, f32[2,5,128]{2,1,0:T(8,128)S(1)} %gains.1.gain_ref, f32[8,128]{1,0:T(8,128)S(1)} %get-tuple-element.14.inv_ref, ...), custom_call_target="tpu_custom_call" | custom-call | flops 10000000000 | bytes 10000000 | tf_op jit(solution)/shard_map/own/pallas_call | solution.py:408
  44.0 0.6 copy-done.9
  45.3 1.9 %collective-permute-start.2 = (bf16[4,256,128]{2,1,0:T(8,128)(2,1)S(1)}, bf16[4,256,128]{2,1,0:T(8,128)(2,1)S(1)}, u32[]{:S(2)}, u32[]{:S(2)}) collective-permute-start(bf16[4,256,128]{2,1,0:T(8,128)(2,1)S(1)} %get-tuple-element.18.halo_ref), channel_id=1, source_target_pairs={{0,8},{8,0},{16,24},{24,16},{32,40},{40,32},{48,56},{56,48},{64,72... | collective-permute-start | bytes 786440 | tf_op jit(solution)/shard_map/ppermute | solution.py:420
  47.2 4.9 %all-to-all-done.1.in_ref = bf16[64,4,8,128]{3,2,1,0:T(8,128)(2,1)S(1)} async-done(((bf16[64,4,8,128]{3,2,1,0:T(8,128)(2,1)}), bf16[64,4,8,128]{3,2,1,0:T(8,128)(2,1)S(1)}, u32[]{:S(2)}, u32[]{:S(2)}) %all-to-all-start.1) | async-done | bytes 524320 | tf_op jit(solution)/shard_map/all_to_all | solution.py:406
  52.1 2.2 %temporal.1 = bf16[64,3,8,128]{3,2,1,0:T(8,128)(2,1)} custom-call(bf16[64,4,8,128]{3,2,1,0:T(8,128)(2,1)S(1)} %all-to-all-done.1.in_ref, f32[8,128]{1,0:T(8,128)S(1)} %get-tuple-element.16.after_ref), custom_call_target="tpu_custom_call" | custom-call | flops 3000000000 | bytes 3000000 | tf_op jit(solution)/shard_map/temporal/pallas_call | solution.py:439
  54.4 9.0 %all-to-all-start.2 = ((bf16[64,3,8,128]{3,2,1,0:T(8,128)(2,1)}), bf16[64,3,8,128]{3,2,1,0:T(8,128)(2,1)S(1)}, u32[]{:S(2)}, u32[]{:S(2)}) async-start(bf16[64,3,8,128]{3,2,1,0:T(8,128)(2,1)} %temporal.1), calls=%async_computation.2 | async-start | bytes 786432 | tf_op jit(solution)/shard_map/all_to_all | solution.py:451
  63.4 2.6 %spatial.1 = (bf16[2,256,128]{2,1,0:T(8,128)(2,1)S(1)}, f32[4,256,128]{2,1,0:T(8,128)S(1)}, bf16[4,256,128]{2,1,0:T(8,128)(2,1)S(1)}, bf16[4,256,128]{2,1,0:T(8,128)(2,1)S(1)}, f32[8,256]{1,0:T(8,128)S(1)}) custom-call(s32[5]{0:T(128)S(1)} %copy-done.7, s32[5]{0:T(128)S(1)} %copy-done.8, s32[1]{0:T(128)} %bitcast.2.frame_ref, f32[2,5,128]{2,1,0:T(8,128)S(1)} %copy-done.18, ...), custom_call_target="tpu_custom_call" | custom-call | flops 6000000000 | bytes 6000000 | tf_op jit(solution)/shard_map/spatial/pallas_call | solution.py:421
  66.0 2.1 %collective-permute-start.4 = (bf16[4,256,128]{2,1,0:T(8,128)(2,1)S(1)}, bf16[4,256,128]{2,1,0:T(8,128)(2,1)S(1)}, u32[]{:S(2)}, u32[]{:S(2)}) collective-permute-start(bf16[4,256,128]{2,1,0:T(8,128)(2,1)S(1)} %get-tuple-element.23), channel_id=1, source_target_pairs={{0,8},{8,0},{16,24},{24,16},{32,40},{40,32},{48,56},{56,48},{64,72... | collective-permute-start | bytes 786440 | tf_op jit(solution)/shard_map/ppermute | solution.py:438
  68.0 5.1 %collective-permute-start.3 = (f32[8,256]{1,0:T(8,128)S(1)}, f32[8,256]{1,0:T(8,128)S(1)}, u32[]{:S(2)}, u32[]{:S(2)}) collective-permute-start(f32[8,256]{1,0:T(8,128)S(1)} %get-tuple-element.22), channel_id=1, source_target_pairs={{8,16},{16,8},{24,32},{32,24},{40,48},{48,40},{56,64},{64,56},{72,... | collective-permute-start | bytes 24584 | tf_op jit(solution)/shard_map/ppermute | solution.py:436
  73.2 4.4 %collective-permute-start.5 = (bf16[4,256,128]{2,1,0:T(8,128)(2,1)S(1)}, bf16[4,256,128]{2,1,0:T(8,128)(2,1)S(1)}, u32[]{:S(2)}, u32[]{:S(2)}) collective-permute-start(bf16[4,256,128]{2,1,0:T(8,128)(2,1)S(1)} %get-tuple-element.24), channel_id=1, source_target_pairs={{8,16},{16,8},{24,32},{32,24},{40,48},{48,40},{56,64},{64,56},{72,... | collective-permute-start | bytes 786440 | tf_op jit(solution)/shard_map/ppermute | solution.py:437
  77.6 0.8 spatial_sums.1.part_ref
  78.4 0.6 copy-done.12
  79.0 1.3 %inner.1 = f32[8,8,128]{2,1,0:T(8,128)} custom-call(s32[5]{0:T(128)S(1)} %copy-done.7, s32[5]{0:T(128)S(1)} %copy-done.8, f32[2,5,128]{2,1,0:T(8,128)S(1)} %copy-done.18, bf16[256,640]{1,0:T(8,128)(2,1)S(1)} %copy-done, bf16[256,640]{1,0:T(8,128)(2,1)S(1)} %copy-done.1, bf16[64,3,8,128]{3,2,1,0:T(8,128)(2,1)S(1)} %all-to-all-done.2.back_ref, ...), custom_call_target="tpu_custom_call" | custom-call | flops 2000000000 | bytes 2000000 | tf_op jit(solution)/shard_map/inner/pallas_call | solution.py:455
  80.3 3.5 %all-to-all-start.3 = ((f32[8,8,128]{2,1,0:T(8,128)}), f32[8,8,128]{2,1,0:T(8,128)S(1)}, u32[]{:S(2)}, u32[]{:S(2)}) async-start(f32[8,8,128]{2,1,0:T(8,128)} %inner.1), calls=%async_computation.3 | async-start | bytes 65536 | tf_op jit(solution)/shard_map/all_to_all | solution.py:458
  83.8 1.1 %collective-permute-done.5.far_ref = bf16[4,256,128]{2,1,0:T(8,128)(2,1)S(1)} collective-permute-done((bf16[4,256,128]{2,1,0:T(8,128)(2,1)S(1)}, bf16[4,256,128]{2,1,0:T(8,128)(2,1)S(1)}, u32[]{:S(2)}, u32[]{:S(2)}) %collective-permute-start.5) | collective-permute-done | bytes 262176 | tf_op jit(solution)/shard_map/ppermute | solution.py:437
  84.9 9.0 %all-to-all-done.3.inner_ref = f32[8,8,128]{2,1,0:T(8,128)S(1)} async-done(((f32[8,8,128]{2,1,0:T(8,128)}), f32[8,8,128]{2,1,0:T(8,128)S(1)}, u32[]{:S(2)}, u32[]{:S(2)}) %all-to-all-start.3) | async-done | bytes 32800 | tf_op jit(solution)/shard_map/all_to_all | solution.py:458
  93.9 1.8 %final.1 = (bf16[256,640]{1,0:T(8,128)(2,1)}, bf16[256,640]{1,0:T(8,128)(2,1)}, bf16[256,640]{1,0:T(8,128)(2,1)}) custom-call(s32[5]{0:T(128)S(1)} %copy-done.7, s32[5]{0:T(128)S(1)} %copy-done.8, f32[2,5,128]{2,1,0:T(8,128)S(1)} %copy-done.19, f32[8,128]{1,0:T(8,128)S(1)} %get-tuple-element.14.inv_ref, f32[8,8,128]{2,1,0:T(8,128)S(1)} %all-to-all-done.3.inner_ref, ...), custom_call_target="tpu_custom_call" | custom-call | flops 3000000000 | bytes 3000000 | tf_op jit(solution)/shard_map/final/pallas_call | solution.py:459
  (46 shorter events, 1.4 us)
Async XLA Ops:
  0.6 14.9 %copy-start.1 = (bf16[256,640]{1,0:T(8,128)(2,1)S(1)}, bf16[256,640]{1,0:T(8,128)(2,1)}, u32[]{:S(2)}) copy-start(bf16[256,640]{1,0:T(8,128)(2,1)} %k_ref.11) | copy-start | bytes 983044
  0.6 14.9 %copy-start.3 = (bf16[256,640]{1,0:T(8,128)(2,1)S(1)}, bf16[256,640]{1,0:T(8,128)(2,1)}, u32[]{:S(2)}) copy-start(bf16[256,640]{1,0:T(8,128)(2,1)} %v_ref.5) | copy-start | bytes 983044
  2.6 12.9 %copy-start.2 = (f32[8,8,128]{2,1,0:T(8,128)S(1)}, f32[8,8,128]{2,1,0:T(8,128)}, u32[]{:S(2)}) copy-start(f32[8,8,128]{2,1,0:T(8,128)} %squares.1.after_ref) | copy-start | bytes 98308
  2.6 12.9 %copy-start.7 = (s32[5]{0:T(128)S(1)}, s32[5]{0:T(128)}, u32[]{:S(2)}) copy-start(s32[5]{0:T(128)} %cls_ref.13) | copy-start | bytes 64
  2.6 12.9 %copy-start.8 = (s32[5]{0:T(128)S(1)}, s32[5]{0:T(128)}, u32[]{:S(2)}) copy-start(s32[5]{0:T(128)} %band_ref.13) | copy-start | bytes 64
  2.6 23.1 %all-to-all-start = ((f32[8,8,128]{2,1,0:T(8,128)}), f32[8,8,128]{2,1,0:T(8,128)S(1)}, u32[]{:S(2)}, u32[]{:S(2)}) async-start(f32[8,8,128]{2,1,0:T(8,128)} %squares.1.after_ref), calls=%async_computation | async-start | bytes 65536 | tf_op jit(solution)/shard_map/all_to_all | solution.py:393
  15.6 4.9 %copy-start = (bf16[256,640]{1,0:T(8,128)(2,1)S(1)}, bf16[256,640]{1,0:T(8,128)(2,1)}, u32[]{:S(2)}) copy-start(bf16[256,640]{1,0:T(8,128)(2,1)} %q_ref.11) | copy-start | bytes 983044
  16.2 26.5 %collective-permute-start = (bf16[4,256,128]{2,1,0:T(8,128)(2,1)S(1)}, bf16[4,256,128]{2,1,0:T(8,128)(2,1)S(1)}, u32[]{:S(2)}, u32[]{:S(2)}) collective-permute-start(bf16[4,256,128]{2,1,0:T(8,128)(2,1)S(1)} %halo.1), channel_id=1, source_target_pairs={{8,16},{16,8},{24,32},{32,24},{40,48},{48,40},{56,64},{64,56},{72,... | collective-permute-start | bytes 786440 | tf_op jit(solution)/shard_map/ppermute | solution.py:389
  20.5 22.2 %copy-start.17 = (f32[2,5,128]{2,1,0:T(8,128)}, f32[2,5,128]{2,1,0:T(8,128)S(1)}, u32[]{:S(2)}) copy-start(f32[2,5,128]{2,1,0:T(8,128)S(1)} %gains.1.gain_ref) | copy-start | bytes 15364
  27.2 24.9 %all-to-all-start.1 = ((bf16[64,4,8,128]{3,2,1,0:T(8,128)(2,1)}), bf16[64,4,8,128]{3,2,1,0:T(8,128)(2,1)S(1)}, u32[]{:S(2)}, u32[]{:S(2)}) async-start(bf16[64,4,8,128]{3,2,1,0:T(8,128)(2,1)} %get-tuple-element.15), calls=%async_computation.1 | async-start | bytes 1048576 | tf_op jit(solution)/shard_map/all_to_all | solution.py:406
  37.8 25.6 %collective-permute-start.1 = (f32[8,128]{1,0:T(8,128)S(1)}, f32[8,128]{1,0:T(8,128)S(1)}, u32[]{:S(2)}, u32[]{:S(2)}) collective-permute-start(f32[8,128]{1,0:T(8,128)S(1)} %get-tuple-element.14.inv_ref), channel_id=1, source_target_pairs={{8,16},{16,8},{24,32},{32,24},{40,48},{48,40},{56,64},{64,56},{72,... | collective-permute-start | bytes 12296 | tf_op jit(solution)/shard_map/ppermute | solution.py:407
  45.3 18.1 %collective-permute-start.2 = (bf16[4,256,128]{2,1,0:T(8,128)(2,1)S(1)}, bf16[4,256,128]{2,1,0:T(8,128)(2,1)S(1)}, u32[]{:S(2)}, u32[]{:S(2)}) collective-permute-start(bf16[4,256,128]{2,1,0:T(8,128)(2,1)S(1)} %get-tuple-element.18.halo_ref), channel_id=1, source_target_pairs={{0,8},{8,0},{16,24},{24,16},{32,40},{40,32},{48,56},{56,48},{64,72... | collective-permute-start | bytes 786440 | tf_op jit(solution)/shard_map/ppermute | solution.py:420
  54.3 9.0 %copy-start.18 = (f32[2,5,128]{2,1,0:T(8,128)S(1)}, f32[2,5,128]{2,1,0:T(8,128)}, u32[]{:S(2)}) copy-start(f32[2,5,128]{2,1,0:T(8,128)} %copy-done.17) | copy-start | bytes 15364
  54.4 24.7 %all-to-all-start.2 = ((bf16[64,3,8,128]{3,2,1,0:T(8,128)(2,1)}), bf16[64,3,8,128]{3,2,1,0:T(8,128)(2,1)S(1)}, u32[]{:S(2)}, u32[]{:S(2)}) async-start(bf16[64,3,8,128]{3,2,1,0:T(8,128)(2,1)} %temporal.1), calls=%async_computation.2 | async-start | bytes 786432 | tf_op jit(solution)/shard_map/all_to_all | solution.py:451
  63.4 14.2 %copy-start.10 = (bf16[2,256,128]{2,1,0:T(8,128)(2,1)S(1)}, bf16[2,256,128]{2,1,0:T(8,128)(2,1)}, u32[]{:S(2)}) copy-start(bf16[2,256,128]{2,1,0:T(8,128)(2,1)} %copy-done.9) | copy-start | bytes 393220
  63.4 14.2 %copy-start.15 = (bf16[256,128]{1,0:T(8,128)(2,1)S(1)}, bf16[256,128]{1,0:T(8,128)(2,1)}, u32[]{:S(2)}) copy-start(bf16[256,128]{1,0:T(8,128)(2,1)} %copy-done.14) | copy-start | bytes 196612
  66.0 11.6 %collective-permute-start.4 = (bf16[4,256,128]{2,1,0:T(8,128)(2,1)S(1)}, bf16[4,256,128]{2,1,0:T(8,128)(2,1)S(1)}, u32[]{:S(2)}, u32[]{:S(2)}) collective-permute-start(bf16[4,256,128]{2,1,0:T(8,128)(2,1)S(1)} %get-tuple-element.23), channel_id=1, source_target_pairs={{0,8},{8,0},{16,24},{24,16},{32,40},{40,32},{48,56},{56,48},{64,72... | collective-permute-start | bytes 786440 | tf_op jit(solution)/shard_map/ppermute | solution.py:438
  68.0 9.5 %collective-permute-start.3 = (f32[8,256]{1,0:T(8,128)S(1)}, f32[8,256]{1,0:T(8,128)S(1)}, u32[]{:S(2)}, u32[]{:S(2)}) collective-permute-start(f32[8,256]{1,0:T(8,128)S(1)} %get-tuple-element.22), channel_id=1, source_target_pairs={{8,16},{16,8},{24,32},{32,24},{40,48},{48,40},{56,64},{64,56},{72,... | collective-permute-start | bytes 24584 | tf_op jit(solution)/shard_map/ppermute | solution.py:436
  73.2 11.7 %collective-permute-start.5 = (bf16[4,256,128]{2,1,0:T(8,128)(2,1)S(1)}, bf16[4,256,128]{2,1,0:T(8,128)(2,1)S(1)}, u32[]{:S(2)}, u32[]{:S(2)}) collective-permute-start(bf16[4,256,128]{2,1,0:T(8,128)(2,1)S(1)} %get-tuple-element.24), channel_id=1, source_target_pairs={{8,16},{16,8},{24,32},{32,24},{40,48},{48,40},{56,64},{64,56},{72,... | collective-permute-start | bytes 786440 | tf_op jit(solution)/shard_map/ppermute | solution.py:437
  79.0 14.9 %copy-start.11 = (bf16[2,256,128]{2,1,0:T(8,128)(2,1)S(1)}, bf16[2,256,128]{2,1,0:T(8,128)(2,1)}, u32[]{:S(2)}) copy-start(bf16[2,256,128]{2,1,0:T(8,128)(2,1)} %copy-done.9) | copy-start | bytes 393220
  79.0 14.9 %copy-start.16 = (bf16[256,128]{1,0:T(8,128)(2,1)S(1)}, bf16[256,128]{1,0:T(8,128)(2,1)}, u32[]{:S(2)}) copy-start(bf16[256,128]{1,0:T(8,128)(2,1)} %copy-done.14) | copy-start | bytes 196612
  79.0 14.9 %copy-start.13 = (bf16[2,256,128]{2,1,0:T(8,128)(2,1)S(1)}, bf16[2,256,128]{2,1,0:T(8,128)(2,1)}, u32[]{:S(2)}) copy-start(bf16[2,256,128]{2,1,0:T(8,128)(2,1)} %copy-done.12) | copy-start | bytes 393220
  80.3 13.6 %copy-start.19 = (f32[2,5,128]{2,1,0:T(8,128)S(1)}, f32[2,5,128]{2,1,0:T(8,128)}, u32[]{:S(2)}) copy-start(f32[2,5,128]{2,1,0:T(8,128)} %copy-done.17) | copy-start | bytes 15364
  80.3 13.6 %all-to-all-start.3 = ((f32[8,8,128]{2,1,0:T(8,128)}), f32[8,8,128]{2,1,0:T(8,128)S(1)}, u32[]{:S(2)}, u32[]{:S(2)}) async-start(f32[8,8,128]{2,1,0:T(8,128)} %inner.1), calls=%async_computation.3 | async-start | bytes 65536 | tf_op jit(solution)/shard_map/all_to_all | solution.py:458
  (6 other events, 16.1 us)

commit v11 on v9

--- a/solution.py
+++ b/solution.py
@@ -216,12 +216,14 @@
     to_near_ref,
     to_far_ref,
     tick_ref,
+    sum_ref,
 ):
     slots, bands = head_slots(cls_ref, band_ref)
     frame = frame_ref[0]
     q_inv = spread(inv_ref[...], 0)
     far_inv = spread(inv_far_ref[...], 2)
     far_total = jnp.zeros((TOK, HD), F32)
+    q_total = jnp.zeros((TOK, HD), F32)
     for s in (1, 2):
         cols = columns(slots[s])
         q = normed(q_ref[:, cols], q_inv, gain_ref[0, pl.ds(slots[s], 1), :])
@@ -233,7 +235,9 @@
         values = [near_ref[at + 1], halo_ref[at + 1], far_ref[at + 1]]
         allowed = [wide, None, wide & (frame > 0) & (frame < FRAMES - 1)]
         d_q, d_k, d_v = attend(q, g_ref[:, cols], keys, values, allowed)
-        dq_ref[s - 1] = d_q.astype(BF)
+        d_q = d_q.astype(BF)
+        dq_ref[s - 1] = d_q
+        q_total += product(gain_ref, 0, slots[s], d_q, q_ref)
         to_near_ref[at] = d_k[0].astype(BF)
         to_near_ref[at + 1] = d_v[0].astype(BF)
         own_ref[at] = d_k[1]
@@ -242,6 +246,7 @@
         to_far_ref[at + 1] = d_v[2].astype(BF)
         far_total += k_gain * d_k[2] * far_ref[at].astype(F32)
     tick_ref[...] = lane_sums(far_total)
+    sum_ref[...] = lane_sums(q_total)
 
 
 def temporal_body(in_ref, after_ref, out_ref):
@@ -275,7 +280,7 @@
     q_ref,
     k_ref,
     dq0_ref,
-    dq_ref,
+    q_part_ref,
     fin_ref,
     own_ref,
     tick_ref,
@@ -287,9 +292,8 @@
     k_total = product(gain_ref, 1, slots[0], fin_ref[0], k_ref)
     for s in (1, 2):
         at = 2 * s - 2
-        q_total += product(gain_ref, 0, slots[s], dq_ref[s - 1], q_ref)
         k_total += product(gain_ref, 1, slots[s], own_ref[at] + near_ref[at].astype(F32), k_ref)
-    part_ref[0] = lane_sums(q_total)
+    part_ref[0] = lane_sums(q_total) + q_part_ref[...]
     part_ref[1] = lane_sums(k_total) + tick_ref[...]
 
 
@@ -397,7 +401,7 @@
         10,
     )(head_class, head_band, gains, inv, query_pre, key_pre, value, d_out, far)
     near = lax.ppermute(halo, "seq", core)
-    dq, own, to_near, to_far, tick = call(
+    dq, own, to_near, to_far, tick, q_part = call(
         spatial_body,
         (
             shape((2, TOK, HD), BF),
@@ -405,6 +409,7 @@
             shape(block, BF),
             shape(block, BF),
             shape((8, TOK), F32),
+            shape((8, TOK), F32),
         ),
         [SM] * 3 + [VM] * 8,
         "spatial",
@@ -419,7 +424,7 @@
     back = lax.all_to_all(grads, "seq", 0, 0, tiled=True)
     part = call(
         spatial_sums_body, shape((2, 8, TOK), F32), [SM, SM] + [VM] * 9, "spatial_sums", 3
-    )(head_class, head_band, gains, query_pre, key_pre, dq0, dq, fin, own, tick, from_near)
+    )(head_class, head_band, gains, query_pre, key_pre, dq0, q_part, fin, own, tick, from_near)
     inner = call(inner_body, shape((8, 8, HD), F32), [SM, SM] + [VM] * 5, "inner", 2)(
         head_class, head_band, gains, query_pre, key_pre, back, part
     )

time: 96.5 us -> 96.5 us (level)
  no operation moved by 1% of the time
where the time goes in v11:
time: 96.5 us; the launch traced here: 95.8 us
  starting transfers between devices  58.6 us (61%)
  waiting for transfers between devices  20.2 us (21%)
  Pallas kernels  14 us (15%)
  local copies, waits for them, and re-layouts  2.02 us (2%)
  between operations  1.04 us (1%)
    all_to_all x1, starting transfers between devices, per_device(): sums = lax.all_to_all(sums, 'head', 0, 0, tiled=True)  12.9 us
    all_to_all x1, starting transfers between devices, per_device(): held = lax.all_to_all(send, 'seq', 0, 0, tiled=True)  10.6 us
    all_to_all x1, starting transfers between devices, per_device(): back = lax.all_to_all(grads, 'seq', 0, 0, tiled=True)  9.11 us
    all_to_all x1, waiting for transfers between devices, per_device(): inner = lax.all_to_all(inner, 'head', 0, 0, tiled=True)  8.3 us
    all_to_all x1, waiting for transfers between devices, per_device(): sums = lax.all_to_all(sums, 'head', 0, 0, tiled=True)  5.14 us
    ppermute x1, starting transfers between devices, per_device(): tick = lax.ppermute(tick, 'seq', chip)  5.12 us
    all_to_all x1, waiting for transfers between devices, per_device(): held = lax.all_to_all(send, 'seq', 0, 0, tiled=True)  4.91 us
    ppermute x1, starting transfers between devices, per_device(): inv_far = lax.ppermute(inv, 'seq', chip)  4.91 us
  transfers between devices with their start and end apart: 10, of which 4 were waited for; matrix products, arithmetic and copies ran while one was open for 0% of the time, Pallas kernels for 11%

profile of v11, /device:TPU:32, one launch (start us, length us, event | category | flops | bytes accessed | tf_op | source)
XLA Modules:
  0.0 95.8 jit_solution(132413157328610653)
XLA Ops:
  0.7 1.9 %squares.1.after_ref = f32[8,8,128]{2,1,0:T(8,128)} custom-call(bf16[256,640]{1,0:T(8,128)(2,1)} %q_ref.11, bf16[256,640]{1,0:T(8,128)(2,1)} %k_ref.11), custom_call_target="tpu_custom_call" | custom-call | tf_op jit(solution)/shard_map/squares/pallas_call | solution.py:365
  2.6 12.9 %all-to-all-start = ((f32[8,8,128]{2,1,0:T(8,128)}), f32[8,8,128]{2,1,0:T(8,128)S(1)}, u32[]{:S(2)}, u32[]{:S(2)}) async-start(f32[8,8,128]{2,1,0:T(8,128)} %squares.1.after_ref), calls=%async_computation | async-start | bytes 65536 | tf_op jit(solution)/shard_map/all_to_all | solution.py:381
  16.2 4.2 %collective-permute-start = (bf16[4,256,128]{2,1,0:T(8,128)(2,1)S(1)}, bf16[4,256,128]{2,1,0:T(8,128)(2,1)S(1)}, u32[]{:S(2)}, u32[]{:S(2)}) collective-permute-start(bf16[4,256,128]{2,1,0:T(8,128)(2,1)S(1)} %halo.1), channel_id=1, source_target_pairs={{8,16},{16,8},{24,32},{32,24},{40,48},{48,40},{56,64},{64,56},{72,... | collective-permute-start | bytes 786440 | tf_op jit(solution)/shard_map/ppermute | solution.py:377
  20.6 5.1 %all-to-all-done.sums_ref = f32[8,8,128]{2,1,0:T(8,128)S(1)} async-done(((f32[8,8,128]{2,1,0:T(8,128)}), f32[8,8,128]{2,1,0:T(8,128)S(1)}, u32[]{:S(2)}, u32[]{:S(2)}) %all-to-all-start) | async-done | bytes 32800 | tf_op jit(solution)/shard_map/all_to_all | solution.py:381
  25.7 1.5 %norm.1 = (bf16[64,4,8,128]{3,2,1,0:T(8,128)(2,1)}, f32[8,128]{1,0:T(8,128)S(1)}) custom-call(s32[5]{0:T(128)S(1)} %copy-done.7, s32[5]{0:T(128)S(1)} %copy-done.8, f32[8,8,128]{2,1,0:T(8,128)S(1)} %all-to-all-done.sums_ref, f32[2,5,128]{2,1,0:T(8,128)S(1)} %gains.1.gain_ref, bf16[256,640]{1,0:T(8,128)(2,1)S(1)} %copy-done, bf16[256,640]{1,0:T(8,128)(2,1)S(1)} %copy-done.1, ...), custom_call_target="tpu_custom_call" | custom-call | flops 2000000000 | bytes 2000000 | tf_op jit(solution)/shard_map/norm/pallas_call | solution.py:382
  27.2 10.6 %all-to-all-start.1 = ((bf16[64,4,8,128]{3,2,1,0:T(8,128)(2,1)}), bf16[64,4,8,128]{3,2,1,0:T(8,128)(2,1)S(1)}, u32[]{:S(2)}, u32[]{:S(2)}) async-start(bf16[64,4,8,128]{3,2,1,0:T(8,128)(2,1)} %get-tuple-element.16), calls=%async_computation.1 | async-start | bytes 1048576 | tf_op jit(solution)/shard_map/all_to_all | solution.py:389
  37.8 4.9 %collective-permute-start.1 = (f32[8,128]{1,0:T(8,128)S(1)}, f32[8,128]{1,0:T(8,128)S(1)}, u32[]{:S(2)}, u32[]{:S(2)}) collective-permute-start(f32[8,128]{1,0:T(8,128)S(1)} %get-tuple-element.15.inv_ref), channel_id=1, source_target_pairs={{8,16},{16,8},{24,32},{32,24},{40,48},{48,40},{56,64},{64,56},{72,... | collective-permute-start | bytes 12296 | tf_op jit(solution)/shard_map/ppermute | solution.py:390
  42.8 1.3 %own.1 = (bf16[256,128]{1,0:T(8,128)(2,1)S(1)}, bf16[2,256,128]{2,1,0:T(8,128)(2,1)S(1)}, bf16[4,256,128]{2,1,0:T(8,128)(2,1)S(1)}, f32[8,128]{1,0:T(8,128)S(1)}) custom-call(s32[5]{0:T(128)S(1)} %copy-done.7, s32[5]{0:T(128)S(1)} %copy-done.8, f32[2,5,128]{2,1,0:T(8,128)S(1)} %gains.1.gain_ref, f32[8,128]{1,0:T(8,128)S(1)} %get-tuple-element.15.inv_ref, ...), custom_call_target="tpu_custom_call" | custom-call | flops 10000000000 | bytes 10000000 | tf_op jit(solution)/shard_map/own/pallas_call | solution.py:391
  44.0 0.6 copy-done.9
  45.3 1.9 %collective-permute-start.2 = (bf16[4,256,128]{2,1,0:T(8,128)(2,1)S(1)}, bf16[4,256,128]{2,1,0:T(8,128)(2,1)S(1)}, u32[]{:S(2)}, u32[]{:S(2)}) collective-permute-start(bf16[4,256,128]{2,1,0:T(8,128)(2,1)S(1)} %get-tuple-element.19.halo_ref), channel_id=1, source_target_pairs={{0,8},{8,0},{16,24},{24,16},{32,40},{40,32},{48,56},{56,48},{64,72... | collective-permute-start | bytes 786440 | tf_op jit(solution)/shard_map/ppermute | solution.py:403
  47.2 4.9 %all-to-all-done.1.in_ref = bf16[64,4,8,128]{3,2,1,0:T(8,128)(2,1)S(1)} async-done(((bf16[64,4,8,128]{3,2,1,0:T(8,128)(2,1)}), bf16[64,4,8,128]{3,2,1,0:T(8,128)(2,1)S(1)}, u32[]{:S(2)}, u32[]{:S(2)}) %all-to-all-start.1) | async-done | bytes 524320 | tf_op jit(solution)/shard_map/all_to_all | solution.py:389
  52.1 2.2 %temporal.1 = bf16[64,3,8,128]{3,2,1,0:T(8,128)(2,1)} custom-call(bf16[64,4,8,128]{3,2,1,0:T(8,128)(2,1)S(1)} %all-to-all-done.1.in_ref, f32[8,128]{1,0:T(8,128)S(1)} %get-tuple-element.17.after_ref), custom_call_target="tpu_custom_call" | custom-call | flops 3000000000 | bytes 3000000 | tf_op jit(solution)/shard_map/temporal/pallas_call | solution.py:423
  54.3 9.1 %all-to-all-start.2 = ((bf16[64,3,8,128]{3,2,1,0:T(8,128)(2,1)}), bf16[64,3,8,128]{3,2,1,0:T(8,128)(2,1)S(1)}, u32[]{:S(2)}, u32[]{:S(2)}) async-start(bf16[64,3,8,128]{3,2,1,0:T(8,128)(2,1)} %temporal.1), calls=%async_computation.2 | async-start | bytes 786432 | tf_op jit(solution)/shard_map/all_to_all | solution.py:424
  63.5 2.6 %spatial.1 = (bf16[2,256,128]{2,1,0:T(8,128)(2,1)S(1)}, f32[4,256,128]{2,1,0:T(8,128)S(1)}, bf16[4,256,128]{2,1,0:T(8,128)(2,1)S(1)}, bf16[4,256,128]{2,1,0:T(8,...) custom-call(s32[5]{0:T(128)S(1)} %copy-done.7, s32[5]{0:T(128)S(1)} %copy-done.8, s32[1]{0:T(128)} %bitcast.2.frame_ref, ...), custom_call_target="tpu_custom_call" | custom-call | flops 6000000000 | bytes 6000000 | tf_op jit(solution)/shard_map/spatial/pallas_call | solution.py:404
  66.1 0.6 copy-done.12
  66.7 2.0 %collective-permute-start.4 = (bf16[4,256,128]{2,1,0:T(8,128)(2,1)S(1)}, bf16[4,256,128]{2,1,0:T(8,128)(2,1)S(1)}, u32[]{:S(2)}, u32[]{:S(2)}) collective-permute-start(bf16[4,256,128]{2,1,0:T(8,128)(2,1)S(1)} %get-tuple-element.24), channel_id=1, source_target_pairs={{0,8},{8,0},{16,24},{24,16},{32,40},{40,32},{48,56},{56,48},{64,72... | collective-permute-start | bytes 786440 | tf_op jit(solution)/shard_map/ppermute | solution.py:422
  68.8 5.1 %collective-permute-start.3 = (f32[8,256]{1,0:T(8,128)S(1)}, f32[8,256]{1,0:T(8,128)S(1)}, u32[]{:S(2)}, u32[]{:S(2)}) collective-permute-start(f32[8,256]{1,0:T(8,128)S(1)} %get-tuple-element.23), channel_id=1, source_target_pairs={{8,16},{16,8},{24,32},{32,24},{40,48},{48,40},{56,64},{64,56},{72,... | collective-permute-start | bytes 24584 | tf_op jit(solution)/shard_map/ppermute | solution.py:420
  73.9 4.3 %collective-permute-start.5 = (bf16[4,256,128]{2,1,0:T(8,128)(2,1)S(1)}, bf16[4,256,128]{2,1,0:T(8,128)(2,1)S(1)}, u32[]{:S(2)}, u32[]{:S(2)}) collective-permute-start(bf16[4,256,128]{2,1,0:T(8,128)(2,1)S(1)} %get-tuple-element.26), channel_id=1, source_target_pairs={{8,16},{16,8},{24,32},{32,24},{40,48},{48,40},{56,64},{64,56},{72,... | collective-permute-start | bytes 786440 | tf_op jit(solution)/shard_map/ppermute | solution.py:421
  78.3 0.7 spatial_sums.1.part_ref
  79.1 1.3 %inner.1 = f32[8,8,128]{2,1,0:T(8,128)} custom-call(s32[5]{0:T(128)S(1)} %copy-done.7, s32[5]{0:T(128)S(1)} %copy-done.8, f32[2,5,128]{2,1,0:T(8,128)S(1)} %copy-done.18, bf16[256,640]{1,0:T(8,128)(2,1)S(1)} %copy-done, bf16[256,640]{1,0:T(8,128)(2,1)S(1)} %copy-done.1, bf16[64,3,8,128]{3,2,1,0:T(8,128)(2,1)S(1)} %all-to-all-done.2.back_ref, ...), custom_call_target="tpu_custom_call" | custom-call | flops 2000000000 | bytes 2000000 | tf_op jit(solution)/shard_map/inner/pallas_call | solution.py:428
  80.4 3.5 %all-to-all-start.3 = ((f32[8,8,128]{2,1,0:T(8,128)}), f32[8,8,128]{2,1,0:T(8,128)S(1)}, u32[]{:S(2)}, u32[]{:S(2)}) async-start(f32[8,8,128]{2,1,0:T(8,128)} %inner.1), calls=%async_computation.3 | async-start | bytes 65536 | tf_op jit(solution)/shard_map/all_to_all | solution.py:431
  83.9 1.8 %collective-permute-done.5.far_ref = bf16[4,256,128]{2,1,0:T(8,128)(2,1)S(1)} collective-permute-done((bf16[4,256,128]{2,1,0:T(8,128)(2,1)S(1)}, bf16[4,256,128]{2,1,0:T(8,128)(2,1)S(1)}, u32[]{:S(2)}, u32[]{:S(2)}) %collective-permute-start.5) | collective-permute-done | bytes 262176 | tf_op jit(solution)/shard_map/ppermute | solution.py:421
  85.7 8.3 %all-to-all-done.3.inner_ref = f32[8,8,128]{2,1,0:T(8,128)S(1)} async-done(((f32[8,8,128]{2,1,0:T(8,128)}), f32[8,8,128]{2,1,0:T(8,128)S(1)}, u32[]{:S(2)}, u32[]{:S(2)}) %all-to-all-start.3) | async-done | bytes 32800 | tf_op jit(solution)/shard_map/all_to_all | solution.py:431
  94.0 1.8 %final.1 = (bf16[256,640]{1,0:T(8,128)(2,1)}, bf16[256,640]{1,0:T(8,128)(2,1)}, bf16[256,640]{1,0:T(8,128)(2,1)}) custom-call(s32[5]{0:T(128)S(1)} %copy-done.7, s32[5]{0:T(128)S(1)} %copy-done.8, f32[2,5,128]{2,1,0:T(8,128)S(1)} %copy-done.19, f32[8,128]{1,0:T(8,128)S(1)} %get-tuple-element.15.inv_ref, f32[8,8,128]{2,1,0:T(8,128)S(1)} %all-to-all-done.3.inner_ref, ...), custom_call_target="tpu_custom_call" | custom-call | flops 3000000000 | bytes 3000000 | tf_op jit(solution)/shard_map/final/pallas_call | solution.py:432
  (46 shorter events, 1.4 us)
Async XLA Ops:
  0.6 14.9 %copy-start.1 = (bf16[256,640]{1,0:T(8,128)(2,1)S(1)}, bf16[256,640]{1,0:T(8,128)(2,1)}, u32[]{:S(2)}) copy-start(bf16[256,640]{1,0:T(8,128)(2,1)} %k_ref.11) | copy-start | bytes 983044
  0.6 14.9 %copy-start.3 = (bf16[256,640]{1,0:T(8,128)(2,1)S(1)}, bf16[256,640]{1,0:T(8,128)(2,1)}, u32[]{:S(2)}) copy-start(bf16[256,640]{1,0:T(8,128)(2,1)} %v_ref.5) | copy-start | bytes 983044
  2.6 12.9 %copy-start.2 = (f32[8,8,128]{2,1,0:T(8,128)S(1)}, f32[8,8,128]{2,1,0:T(8,128)}, u32[]{:S(2)}) copy-start(f32[8,8,128]{2,1,0:T(8,128)} %squares.1.after_ref) | copy-start | bytes 98308
  2.6 12.9 %copy-start.7 = (s32[5]{0:T(128)S(1)}, s32[5]{0:T(128)}, u32[]{:S(2)}) copy-start(s32[5]{0:T(128)} %cls_ref.13) | copy-start | bytes 64
  2.6 12.9 %copy-start.8 = (s32[5]{0:T(128)S(1)}, s32[5]{0:T(128)}, u32[]{:S(2)}) copy-start(s32[5]{0:T(128)} %band_ref.13) | copy-start | bytes 64
  2.6 23.1 %all-to-all-start = ((f32[8,8,128]{2,1,0:T(8,128)}), f32[8,8,128]{2,1,0:T(8,128)S(1)}, u32[]{:S(2)}, u32[]{:S(2)}) async-start(f32[8,8,128]{2,1,0:T(8,128)} %squares.1.after_ref), calls=%async_computation | async-start | bytes 65536 | tf_op jit(solution)/shard_map/all_to_all | solution.py:381
  15.6 4.9 %copy-start = (bf16[256,640]{1,0:T(8,128)(2,1)S(1)}, bf16[256,640]{1,0:T(8,128)(2,1)}, u32[]{:S(2)}) copy-start(bf16[256,640]{1,0:T(8,128)(2,1)} %q_ref.11) | copy-start | bytes 983044
  16.2 26.5 %collective-permute-start = (bf16[4,256,128]{2,1,0:T(8,128)(2,1)S(1)}, bf16[4,256,128]{2,1,0:T(8,128)(2,1)S(1)}, u32[]{:S(2)}, u32[]{:S(2)}) collective-permute-start(bf16[4,256,128]{2,1,0:T(8,128)(2,1)S(1)} %halo.1), channel_id=1, source_target_pairs={{8,16},{16,8},{24,32},{32,24},{40,48},{48,40},{56,64},{64,56},{72,... | collective-permute-start | bytes 786440 | tf_op jit(solution)/shard_map/ppermute | solution.py:377
  20.5 22.2 %copy-start.17 = (f32[2,5,128]{2,1,0:T(8,128)}, f32[2,5,128]{2,1,0:T(8,128)S(1)}, u32[]{:S(2)}) copy-start(f32[2,5,128]{2,1,0:T(8,128)S(1)} %gains.1.gain_ref) | copy-start | bytes 15364
  27.2 24.9 %all-to-all-start.1 = ((bf16[64,4,8,128]{3,2,1,0:T(8,128)(2,1)}), bf16[64,4,8,128]{3,2,1,0:T(8,128)(2,1)S(1)}, u32[]{:S(2)}, u32[]{:S(2)}) async-start(bf16[64,4,8,128]{3,2,1,0:T(8,128)(2,1)} %get-tuple-element.16), calls=%async_computation.1 | async-start | bytes 1048576 | tf_op jit(solution)/shard_map/all_to_all | solution.py:389
  37.8 25.6 %collective-permute-start.1 = (f32[8,128]{1,0:T(8,128)S(1)}, f32[8,128]{1,0:T(8,128)S(1)}, u32[]{:S(2)}, u32[]{:S(2)}) collective-permute-start(f32[8,128]{1,0:T(8,128)S(1)} %get-tuple-element.15.inv_ref), channel_id=1, source_target_pairs={{8,16},{16,8},{24,32},{32,24},{40,48},{48,40},{56,64},{64,56},{72,... | collective-permute-start | bytes 12296 | tf_op jit(solution)/shard_map/ppermute | solution.py:390
  45.3 18.1 %collective-permute-start.2 = (bf16[4,256,128]{2,1,0:T(8,128)(2,1)S(1)}, bf16[4,256,128]{2,1,0:T(8,128)(2,1)S(1)}, u32[]{:S(2)}, u32[]{:S(2)}) collective-permute-start(bf16[4,256,128]{2,1,0:T(8,128)(2,1)S(1)} %get-tuple-element.19.halo_ref), channel_id=1, source_target_pairs={{0,8},{8,0},{16,24},{24,16},{32,40},{40,32},{48,56},{56,48},{64,72... | collective-permute-start | bytes 786440 | tf_op jit(solution)/shard_map/ppermute | solution.py:403
  54.3 9.1 %copy-start.18 = (f32[2,5,128]{2,1,0:T(8,128)S(1)}, f32[2,5,128]{2,1,0:T(8,128)}, u32[]{:S(2)}) copy-start(f32[2,5,128]{2,1,0:T(8,128)} %copy-done.17) | copy-start | bytes 15364
  54.3 24.8 %all-to-all-start.2 = ((bf16[64,3,8,128]{3,2,1,0:T(8,128)(2,1)}), bf16[64,3,8,128]{3,2,1,0:T(8,128)(2,1)S(1)}, u32[]{:S(2)}, u32[]{:S(2)}) async-start(bf16[64,3,8,128]{3,2,1,0:T(8,128)(2,1)} %temporal.1), calls=%async_computation.2 | async-start | bytes 786432 | tf_op jit(solution)/shard_map/all_to_all | solution.py:424
  63.5 14.9 %copy-start.10 = (bf16[2,256,128]{2,1,0:T(8,128)(2,1)S(1)}, bf16[2,256,128]{2,1,0:T(8,128)(2,1)}, u32[]{:S(2)}) copy-start(bf16[2,256,128]{2,1,0:T(8,128)(2,1)} %copy-done.9) | copy-start | bytes 393220
  63.5 14.9 %copy-start.15 = (bf16[256,128]{1,0:T(8,128)(2,1)S(1)}, bf16[256,128]{1,0:T(8,128)(2,1)}, u32[]{:S(2)}) copy-start(bf16[256,128]{1,0:T(8,128)(2,1)} %copy-done.14) | copy-start | bytes 196612
  66.7 11.6 %collective-permute-start.4 = (bf16[4,256,128]{2,1,0:T(8,128)(2,1)S(1)}, bf16[4,256,128]{2,1,0:T(8,128)(2,1)S(1)}, u32[]{:S(2)}, u32[]{:S(2)}) collective-permute-start(bf16[4,256,128]{2,1,0:T(8,128)(2,1)S(1)} %get-tuple-element.24), channel_id=1, source_target_pairs={{0,8},{8,0},{16,24},{24,16},{32,40},{40,32},{48,56},{56,48},{64,72... | collective-permute-start | bytes 786440 | tf_op jit(solution)/shard_map/ppermute | solution.py:422
  68.8 9.5 %collective-permute-start.3 = (f32[8,256]{1,0:T(8,128)S(1)}, f32[8,256]{1,0:T(8,128)S(1)}, u32[]{:S(2)}, u32[]{:S(2)}) collective-permute-start(f32[8,256]{1,0:T(8,128)S(1)} %get-tuple-element.23), channel_id=1, source_target_pairs={{8,16},{16,8},{24,32},{32,24},{40,48},{48,40},{56,64},{64,56},{72,... | collective-permute-start | bytes 24584 | tf_op jit(solution)/shard_map/ppermute | solution.py:420
  73.9 11.8 %collective-permute-start.5 = (bf16[4,256,128]{2,1,0:T(8,128)(2,1)S(1)}, bf16[4,256,128]{2,1,0:T(8,128)(2,1)S(1)}, u32[]{:S(2)}, u32[]{:S(2)}) collective-permute-start(bf16[4,256,128]{2,1,0:T(8,128)(2,1)S(1)} %get-tuple-element.26), channel_id=1, source_target_pairs={{8,16},{16,8},{24,32},{32,24},{40,48},{48,40},{56,64},{64,56},{72,... | collective-permute-start | bytes 786440 | tf_op jit(solution)/shard_map/ppermute | solution.py:421
  79.1 14.9 %copy-start.11 = (bf16[2,256,128]{2,1,0:T(8,128)(2,1)S(1)}, bf16[2,256,128]{2,1,0:T(8,128)(2,1)}, u32[]{:S(2)}) copy-start(bf16[2,256,128]{2,1,0:T(8,128)(2,1)} %copy-done.9) | copy-start | bytes 393220
  79.1 14.9 %copy-start.13 = (bf16[2,256,128]{2,1,0:T(8,128)(2,1)S(1)}, bf16[2,256,128]{2,1,0:T(8,128)(2,1)}, u32[]{:S(2)}) copy-start(bf16[2,256,128]{2,1,0:T(8,128)(2,1)} %copy-done.12) | copy-start | bytes 393220
  79.1 14.9 %copy-start.19 = (f32[2,5,128]{2,1,0:T(8,128)S(1)}, f32[2,5,128]{2,1,0:T(8,128)}, u32[]{:S(2)}) copy-start(f32[2,5,128]{2,1,0:T(8,128)} %copy-done.17) | copy-start | bytes 15364
  80.4 13.6 %copy-start.16 = (bf16[256,128]{1,0:T(8,128)(2,1)S(1)}, bf16[256,128]{1,0:T(8,128)(2,1)}, u32[]{:S(2)}) copy-start(bf16[256,128]{1,0:T(8,128)(2,1)} %copy-done.14) | copy-start | bytes 196612
  80.4 13.6 %all-to-all-start.3 = ((f32[8,8,128]{2,1,0:T(8,128)}), f32[8,8,128]{2,1,0:T(8,128)S(1)}, u32[]{:S(2)}, u32[]{:S(2)}) async-start(f32[8,8,128]{2,1,0:T(8,128)} %inner.1), calls=%async_computation.3 | async-start | bytes 65536 | tf_op jit(solution)/shard_map/all_to_all | solution.py:431
  (6 other events, 16.1 us)
